TPU v7x, 512 devices: a whole 4x8x8 slice. The times are simulated.
512 devices in a mesh: row: 16 (over x, z_lo), col: 32 (over y, z_hi, core).
Axes of the slice: x: 4, y: 8, z: 8 (z_hi: 2, z_lo: 4; z = z_hi * 4 + z_lo), core: 2. Of those that a mesh axis runs over, the one named last changes fastest.
Arguments:
- pair: bfloat16 [384, 384, 128], P('row', 'col'), may hold values from -6 to 6
- cotangent: bfloat16 [384, 384, 128], P('row', 'col'), may hold values from -6 to 6
- chain_counts: int32 [4], replicated, may hold values from 48 to 96
- in_gain: float32 [128], replicated, may hold values from 0.1 to 1.9
- in_bias: float32 [128], replicated, may hold values from -0.5 to 0.5
- w_values: bfloat16 [128, 256], replicated, may hold values from -0.5 to 0.5
- w_gates: bfloat16 [128, 256], replicated, may hold values from -0.5 to 0.5
- w_out_gate: bfloat16 [128, 128], replicated, may hold values from -0.5 to 0.5
- out_gain: float32 [128], replicated, may hold values from 0.1 to 1.9
- out_bias: float32 [128], replicated, may hold values from -0.5 to 0.5
- w_out: bfloat16 [128, 128], replicated, may hold values from -0.5 to 0.5
Outputs:
- update: bfloat16 [384, 384, 128], P('row', 'col')
- grad_pair: bfloat16 [384, 384, 128], P('row', 'col')
Inputs may be any that keep to these rules, and one draw needn't show every extreme that they name: Tokens at positions from the sum of chain_counts onward are padding.
All inputs are finite; a program needn't handle non-finite values.
Results may differ from a plain program's by a relative error of at most 0.0078.
Values may be sent and summed in bfloat16 or wider, within the bound.
No kernel may reach another device: no remote copies, remote signals or barrier semaphores. Data moves between devices by JAX's collectives and lax.ppermute only.
A program may use at most 64 MiB of HBM per device.

v0:
```python
import jax
import jax.numpy as jnp
from jax import lax
from jax.sharding import PartitionSpec as P

EPS = 1e-05


def from_root(block, axis, source):
    block = jnp.where(lax.axis_index(axis) == source, block, jnp.zeros_like(block))
    return lax.psum(block, axis)


def layer_norm(values_in, scale_vec, shift_vec):
    centre = values_in - jnp.mean(values_in, axis=-1, keepdims=True)
    inv_std = lax.rsqrt(jnp.mean(centre * centre, axis=-1, keepdims=True) + EPS)
    normed_hat = centre * inv_std
    return (normed_hat * scale_vec + shift_vec, normed_hat, inv_std)


def norm_back(upstream, scale_vec, normed_hat, inv_std):
    scaled = upstream * scale_vec
    first_mean = jnp.mean(scaled, axis=-1, keepdims=True)
    second_mean = jnp.mean(scaled * normed_hat, axis=-1, keepdims=True)
    return inv_std * (scaled - first_mean - normed_hat * second_mean)


def shards(
    pair,
    cotangent,
    chain_counts,
    in_gain,
    in_bias,
    w_values,
    w_gates,
    w_out_gate,
    out_gain,
    out_bias,
    w_out,
):
    rows_here, cols_here, width = pair.shape
    hidden = w_out.shape[0]
    n_rows = lax.axis_size("row")
    n_cols = lax.axis_size("col")
    col_ratio = n_cols // n_rows
    row_index = lax.axis_index("row")
    col_index = lax.axis_index("col")
    valid_count = jnp.sum(chain_counts)
    row_ids = row_index * rows_here + jnp.arange(rows_here, dtype=jnp.int32)
    col_ids = col_index * cols_here + jnp.arange(cols_here, dtype=jnp.int32)
    row_live = (row_ids < valid_count).astype(jnp.float32)
    col_live = (col_ids < valid_count).astype(jnp.float32)
    pair_mask = (row_live[:, None] * col_live[None, :])[..., None]
    pair_full = pair.astype(jnp.float32)
    normed, pair_hat, pair_inv = layer_norm(pair_full, in_gain, in_bias)
    normed_b = normed.astype(jnp.bfloat16)
    w_front = jnp.concatenate([w_values, w_gates, w_out_gate], axis=1)
    front = jnp.dot(normed_b, w_front, preferred_element_type=jnp.float32)
    values = front[..., : 2 * hidden]
    gate_sig = jax.nn.sigmoid(front[..., 2 * hidden : 4 * hidden])
    out_sig = jax.nn.sigmoid(front[..., 4 * hidden :])
    both = (gate_sig * values * pair_mask).astype(jnp.bfloat16)
    left_tile = both[..., :hidden]
    right_tile = both[..., hidden:]
    left_cols, right_cols = (
        lax.all_gather(left_tile, "row", axis=0, tiled=True),
        lax.all_gather(right_tile, "row", axis=0, tiled=True),
    )
    left_rows, right_panel = (
        lax.all_gather(left_tile, "col", axis=1, tiled=True),
        lax.all_gather(right_tile, "col", axis=1, tiled=True),
    )
    offset = col_index % col_ratio * cols_here
    right_part = lax.dynamic_slice_in_dim(right_panel, offset, cols_here, 0)
    right_rows = from_root(right_part, "row", col_index // col_ratio)
    inner = jnp.einsum("ikh,jkh->ijh", left_rows, right_rows, preferred_element_type=jnp.float32)
    inner_n, inner_hat, inner_inv = layer_norm(inner, out_gain, out_bias)
    inner_b = inner_n.astype(jnp.bfloat16)
    proj_out = jnp.dot(inner_b, w_out, preferred_element_type=jnp.float32)
    update = (out_sig * proj_out).astype(jnp.bfloat16)
    upstream = cotangent.astype(jnp.float32)
    d_proj = (upstream * out_sig).astype(jnp.bfloat16)
    d_gate_out = (upstream * proj_out * out_sig * (1.0 - out_sig)).astype(jnp.bfloat16)
    d_inner_n = jnp.dot(d_proj, w_out.T, preferred_element_type=jnp.float32)
    d_inner = norm_back(d_inner_n, out_gain, inner_hat, inner_inv).astype(jnp.bfloat16)
    d_inner_cols = lax.all_gather(d_inner, "row", axis=0, tiled=True)
    received = [
        from_root(d_inner_cols, "col", col_ratio * row_index + offset_step)
        for offset_step in range(col_ratio)
    ]
    d_inner_mine = jnp.concatenate(received, axis=1)
    d_right = jnp.einsum(
        "ijh,ikh->jkh", d_inner_mine, left_cols, preferred_element_type=jnp.float32
    )
    d_left = jnp.einsum(
        "ijh,jkh->ikh",
        lax.all_gather(d_inner, "col", axis=1, tiled=True),
        right_cols,
        preferred_element_type=jnp.float32,
    )
    d_both = jnp.concatenate([d_left, d_right], axis=-1) * pair_mask
    d_values = (d_both * gate_sig).astype(jnp.bfloat16)
    d_gates = (d_both * values * gate_sig * (1.0 - gate_sig)).astype(jnp.bfloat16)
    d_front = jnp.concatenate([d_values, d_gates, d_gate_out], axis=-1)
    d_normed = jnp.dot(d_front, w_front.T, preferred_element_type=jnp.float32)
    grad_pair = norm_back(d_normed, in_gain, pair_hat, pair_inv).astype(jnp.bfloat16)
    return (update, grad_pair)


def solution(mesh):
    return jax.shard_map(
        shards,
        mesh=mesh,
        in_specs=(
            P("row", "col", None),
            P("row", "col", None),
            P(),
            P(),
            P(),
            P(),
            P(),
            P(),
            P(),
            P(),
            P(),
        ),
        out_specs=(P("row", "col", None), P("row", "col", None)),
        check_vma=False,
    )
```

profile of v0, /device:TPU:1, one launch (start us, length us, event | category | flops | bytes accessed | tf_op | source)
XLA Modules:
  0.0 1117.0 jit_solution(3286931288571797449)
XLA Ops:
  7.2 0.0 copy-start
  7.2 0.0 all-gather.7.cloned.1.call-start
  7.2 1.3 reduce_sum.83
  8.5 0.6 compare_convert_fusion
  9.2 0.7 compare_convert_fusion.1
  9.8 1.0 convert_reduce_fusion
  10.9 1.1 fusion.23
  11.9 0.1 broadcast_multiply_fusion
  12.0 1.3 fusion.32
  13.3 0.9 copy-done.1
  14.2 0.1 multiply_convert_fusion.2
  14.3 0.7 fusion.52
  15.0 0.0 all-gather.7.cloned.1.call-update
  15.0 0.0 all-gather.9.cloned.1.call-start
  15.1 0.7 all-gather.9.cloned.1.call-update
  15.8 0.0 all-reduce.4.cloned.1.call-start
  15.9 101.1 %all-gather.7.cloned.1.call-done = bf16[24,384,128]{2,0,1:T(8,128)(2,1)} async-done(((bf16[24,12,128]{2,0,1:T(8,128)(2,1)}), bf16[24,384,128]{2,0,1:T(8,128)(2,1)}) %all-gather.7.cloned.1.call-update) | async-done | bytes 2359312 | tf_op jit(solution)/shard_map/all_gather | solution.py:71
  117.0 2.2 constant_dynamic-slice_fusion
  119.2 1.6 copy.44
  120.8 1.3 broadcast_select_fusion.2
  122.2 0.0 all-reduce.4.cloned.1.call-update
  122.2 0.0 all-gather.17.cloned.1.call-start
  122.2 88.0 %all-gather.9.cloned.1.call-done = bf16[24,384,128]{2,0,1:T(8,128)(2,1)} async-done(((bf16[24,12,128]{2,0,1:T(8,128)(2,1)}), bf16[24,384,128]{2,0,1:T(8,128)(2,1)}) %all-gather.9.cloned.1.call-update) | async-done | bytes 2359312 | tf_op jit(solution)/shard_map/all_gather | solution.py:70
  210.3 10.9 copy.35
  221.2 152.7 %all-reduce.4.cloned.1.call-done = bf16[12,384,128]{1,0,2:T(8,128)(2,1)} async-done(((bf16[12,384,128]{1,0,2:T(8,128)(2,1)}), bf16[12,384,128]{1,0,2:T(8,128)(2,1)}) %all-reduce.4.cloned.1.call-update) | async-done | bytes 1179664 | tf_op jit(solution)/shard_map/psum | solution.py:11
  373.8 7.3 fusion.53
  381.2 0.3 copy.36
  381.5 0.1 bitcast_reduce_fusion
  381.6 0.2 multiply_reduce_fusion.1
  381.9 0.3 fusion.51
  382.2 0.9 multiply_convert_fusion.3
  383.1 0.0 all-gather.17.cloned.1.call-update
  383.1 0.0 all-gather.11.cloned.1.call-start
  383.2 0.5 all-gather.11.cloned.1.call-update
  383.7 0.0 all-gather.15.cloned.1.call-start
  383.7 0.5 all-gather.15.cloned.1.call-update
  384.3 0.0 all-gather.13.cloned.1.call-start
  384.3 0.7 all-gather.13.cloned.1.call-update
  385.0 0.2 all-reduce.6.cloned.1.call-start
  385.3 80.6 %all-gather.17.cloned.1.call-done = bf16[384,12,128]{2,0,1:T(8,128)(2,1)} async-done(((bf16[24,12,128]{2,0,1:T(8,128)(2,1)}), bf16[384,12,128]{2,0,1:T(8,128)(2,1)}) %all-gather.17.cloned.1.call-update) | async-done | bytes 1179664 | tf_op jit(solution)/shard_map/all_gather | solution.py:86
  465.9 2.2 copy.40
  468.0 1.9 broadcast_select_fusion.1
  469.9 0.0 all-reduce.6.cloned.1.call-update
  470.0 83.3 %all-gather.11.cloned.1.call-done = bf16[384,12,128]{2,0,1:T(8,128)(2,1)} async-done(((bf16[24,12,128]{2,0,1:T(8,128)(2,1)}), bf16[384,12,128]{2,0,1:T(8,128)(2,1)}) %all-gather.11.cloned.1.call-update) | async-done | bytes 1179664 | tf_op jit(solution)/shard_map/all_gather | solution.py:67
  553.2 2.2 copy.37
  555.4 0.0 copy-start.9
  555.4 85.2 %all-gather.15.cloned.1.call-done = bf16[384,12,128]{2,0,1:T(8,128)(2,1)} async-done(((bf16[24,12,128]{2,0,1:T(8,128)(2,1)}), bf16[384,12,128]{2,0,1:T(8,128)(2,1)}) %all-gather.15.cloned.1.call-update) | async-done | bytes 1179664 | tf_op jit(solution)/shard_map/all_gather | solution.py:66
  640.6 3.0 copy.42
  643.6 0.9 fusion.27
  644.5 104.7 %all-gather.13.cloned.1.call-done = bf16[24,384,128]{2,0,1:T(8,128)(2,1)} async-done(((bf16[24,12,128]{2,0,1:T(8,128)(2,1)}), bf16[24,384,128]{2,0,1:T(8,128)(2,1)}) %all-gather.13.cloned.1.call-update) | async-done | bytes 2359312 | tf_op jit(solution)/shard_map/all_gather | solution.py:97
  749.2 10.9 copy.38
  760.1 5.8 fusion.54
  765.9 0.3 copy.39
  766.3 338.4 %all-reduce.6.cloned.1.call-done = (bf16[384,12,128]{0,1,2:T(8,128)(2,1)}, bf16[384,12,128]{0,1,2:T(8,128)(2,1)}) async-done(((bf16[384,12,128]{0,1,2:T(8,128)(2,1)}, bf16[384,12,128]{0,1,2:T(8,128)(2,1)}), (bf16[384,12,128]{0,1,2:T(8,128)(2,1)}, bf16[384,12,128]{0,1,2:T(8,128)(2,1)})) %all-reduce.6.cloned.1.call-update) | async-done | bytes 2359312 | tf_op jit(solution)/shard_map/psum | solution.py:11
  1104.7 3.3 fusion
  1108.0 0.0 copy-start.3
  1108.0 0.0 copy-start.4
  1108.0 0.0 copy-start.5
  1108.1 0.3 copy.43
  1108.4 0.2 multiply_convert_fusion.1
  1108.5 0.4 copy-done.3
  1108.9 0.0 copy-done.5
  1108.9 0.4 fusion.50
  1109.3 0.9 fusion.22
  (21 shorter events, 0.1 us)
Async XLA Ops:
  7.2 374.7 %copy-start = (bf16[128,128]{1,0:T(8,128)(2,1)S(1)}, bf16[128,128]{1,0:T(8,128)(2,1)}, u32[]{:S(2)}) copy-start(bf16[128,128]{1,0:T(8,128)(2,1)} %param.21) | copy-start | bytes 98308
  7.2 109.8 %all-gather.7.cloned.1.call-start = ((), (), s32[]{:S(2)}) async-start(), calls=%async_computation | async-start | bytes 2433024 | tf_op jit(solution)/shard_map/all_gather | solution.py:71
  13.3 0.9 copy-start.1
  15.0 195.2 %all-gather.9.cloned.1.call-start = ((), (), s32[]{:S(2)}) async-start(), calls=%async_computation.2 | async-start | bytes 2433024 | tf_op jit(solution)/shard_map/all_gather | solution.py:70
  15.8 358.0 %all-reduce.4.cloned.1.call-start = ((), (), s32[]{:S(2)}) async-start(), calls=%async_computation.1 | async-start | bytes 3145728 | tf_op jit(solution)/shard_map/psum | solution.py:11
  122.2 343.7 %all-gather.17.cloned.1.call-start = ((), (), s32[]{:S(2)}) async-start(), calls=%async_computation.6 | async-start | bytes 1253376 | tf_op jit(solution)/shard_map/all_gather | solution.py:86
  221.1 160.7 %copy-start.2 = (f32[24,12,640]{2,0,1:T(8,128)S(1)}, f32[24,12,640]{2,0,1:T(8,128)}, u32[]{:S(2)}) copy-start(f32[24,12,640]{2,0,1:T(8,128)} %copy-done.1) | copy-start | bytes 2211844
  221.2 160.7 %copy-start.8 = (bf16[24,12,128]{2,0,1:T(8,128)(2,1)S(1)}, bf16[24,12,128]{2,0,1:T(8,128)(2,1)}, u32[]{:S(2)}) copy-start(bf16[24,12,128]{2,0,1:T(8,128)(2,1)} %param.12) | copy-start | bytes 221188
  221.2 160.7 %copy-start.10 = (f32[128]{0:T(128)S(1)}, f32[128]{0:T(128)}, u32[]{:S(2)}) copy-start(f32[128]{0:T(128)} %param.19) | copy-start | bytes 1540
  383.1 170.1 %all-gather.11.cloned.1.call-start = ((), (), s32[]{:S(2)}) async-start(), calls=%async_computation.3 | async-start | bytes 1253376 | tf_op jit(solution)/shard_map/all_gather | solution.py:67
  383.7 256.9 %all-gather.15.cloned.1.call-start = ((), (), s32[]{:S(2)}) async-start(), calls=%async_computation.5 | async-start | bytes 1253376 | tf_op jit(solution)/shard_map/all_gather | solution.py:66
  384.3 365.0 %all-gather.13.cloned.1.call-start = ((), (), s32[]{:S(2)}) async-start(), calls=%async_computation.4 | async-start | bytes 2433024 | tf_op jit(solution)/shard_map/all_gather | solution.py:97
  385.0 719.6 %all-reduce.6.cloned.1.call-start = ((), (), s32[]{:S(2)}) async-start(), calls=%async_computation.7 | async-start | bytes 6291456 | tf_op jit(solution)/shard_map/psum | solution.py:11
  555.4 88.2 %copy-start.9 = (f32[128]{0:T(128)S(1)}, f32[128]{0:T(128)}, u32[]{:S(2)}) copy-start(f32[128]{0:T(128)} %param.20) | copy-start | bytes 1540
  1108.0 0.9 copy-start.3
  1108.0 0.9 copy-start.4
  1108.0 0.9 copy-start.5
  1108.0 0.9 copy-start.6
  1108.0 0.9 copy-start.7
Sparse Core Ops, SparseCore 0:
  15.2 101.8 all-gather.6
  120.9 89.3 all-gather.8
  213.2 160.5 all-reduce.3
  383.2 82.5 all-gather.16
  468.6 84.5 all-gather.10
  555.9 84.5 all-gather.14
  644.4 104.7 all-gather.12
  752.5 352.1 all-reduce.5
where the time goes:
time: 1120 us
  waiting for transfers between devices  1040 us (93%)
  local copies, waits for them, and re-layouts  35.9 us (3%)
  matrix products  19.4 us (2%)
  between operations  14.5 us (1%)
    psum x2, waiting for transfers between devices, from_root(): return lax.psum(block, axis)  491 us
    all_gather x1, waiting for transfers between devices, shards(): lax.all_gather(d_inner, 'col', axis=1, tiled=True)  105 us
    all_gather x1, waiting for transfers between devices, shards(): lax.all_gather(right_tile, 'col', axis=1, tiled=True)  101 us
    all_gather x1, waiting for transfers between devices, shards(): lax.all_gather(left_tile, 'col', axis=1, tiled=True)  88 us
    all_gather x1, waiting for transfers between devices, shards(): lax.all_gather(left_tile, 'row', axis=0, tiled=True)  85.2 us
    all_gather x1, waiting for transfers between devices, shards(): lax.all_gather(right_tile, 'row', axis=0, tiled=True)  83.3 us
    all_gather x1, waiting for transfers between devices, shards(): d_inner_cols = lax.all_gather(d_inner, 'row', axis=0, tiled=True)  80.6 us
  transfers between devices with their start and end apart: 8, of which 8 were waited for; matrix products, arithmetic and copies ran while one was open for 4% of the time, Pallas kernels for 0%

commit v1 on v0

v1 whole, which is shorter than its diff:
```python
import jax
import jax.numpy as jnp
from jax import lax
from jax.sharding import Mesh
from jax.sharding import PartitionSpec as P

EPS = 1e-05
ROW = ("x", "z_lo")
COL = ("y", "z_hi", "core")
GROUP = ("x", "z_lo", "y")
ALL = ROW + COL


def layer_norm(values_in, scale_vec, shift_vec, axis):
    centre = values_in - jnp.mean(values_in, axis=axis, keepdims=True)
    inv_std = lax.rsqrt(jnp.mean(centre * centre, axis=axis, keepdims=True) + EPS)
    normed_hat = centre * inv_std
    return (normed_hat * scale_vec + shift_vec, normed_hat, inv_std)


def norm_back(upstream, scale_vec, normed_hat, inv_std, axis):
    scaled = upstream * scale_vec
    first_mean = jnp.mean(scaled, axis=axis, keepdims=True)
    second_mean = jnp.mean(scaled * normed_hat, axis=axis, keepdims=True)
    return inv_std * (scaled - first_mean - normed_hat * second_mean)


def dot(a, b, contract):
    return lax.dot_general(a, b, ((contract[:1], contract[1:]), ((), ())), preferred_element_type=jnp.float32)


def shards(
    pair,
    cotangent,
    chain_counts,
    in_gain,
    in_bias,
    w_values,
    w_gates,
    w_out_gate,
    out_gain,
    out_bias,
    w_out,
):
    rows_here, cols_here, width = pair.shape
    hidden = w_out.shape[0]
    here = rows_here * cols_here
    n_rows = lax.axis_size(ROW)
    n_cols = lax.axis_size(COL)
    n_parts = n_cols // lax.axis_size("y")
    n_y = lax.axis_size("y")
    tokens = n_rows * rows_here
    valid_count = jnp.sum(chain_counts)
    row_ids = lax.axis_index(ROW) * rows_here + jnp.arange(rows_here, dtype=jnp.int32)
    col_ids = lax.axis_index(COL) * cols_here + jnp.arange(cols_here, dtype=jnp.int32)
    row_live = (row_ids < valid_count).astype(jnp.float32)
    col_live = (col_ids < valid_count).astype(jnp.float32)
    pair_mask = (row_live[:, None] * col_live[None, :]).reshape(1, here)

    pair_full = pair.reshape(here, width).astype(jnp.float32)
    normed, pair_hat, pair_inv = layer_norm(pair_full, in_gain, in_bias, 1)
    normed_b = normed.astype(jnp.bfloat16)
    w_front = jnp.concatenate([w_values, w_gates, w_out_gate], axis=1)
    front = dot(w_front, normed_b, (0, 1))
    values = front[: 2 * hidden]
    gate_sig = jax.nn.sigmoid(front[2 * hidden : 4 * hidden])
    out_sig = jax.nn.sigmoid(front[4 * hidden :])
    both = (gate_sig * values * pair_mask).astype(jnp.bfloat16)
    both = jnp.stack([both[:hidden], both[hidden:]], axis=1)
    both = lax.all_to_all(both, GROUP, 0, 0)

    def to_matrix(blocks):
        blocks = blocks.reshape(n_rows, -1, rows_here, cols_here)
        return blocks.transpose(0, 2, 1, 3).reshape(tokens, -1)

    def to_blocks(matrix):
        matrix = matrix.reshape(n_rows, rows_here, -1, cols_here)
        return matrix.transpose(0, 2, 1, 3).reshape(-1, here)

    left, right = to_matrix(both[:, 0]), to_matrix(both[:, 1])
    inner = to_blocks(dot(left, right, (1, 1)).astype(jnp.bfloat16))
    inner = lax.all_to_all(inner, ALL, 0, 0).reshape(hidden, n_parts, here)
    inner = jnp.sum(inner.astype(jnp.float32), axis=1)

    inner_n, inner_hat, inner_inv = layer_norm(inner, out_gain[:, None], out_bias[:, None], 0)
    inner_b = inner_n.astype(jnp.bfloat16)
    proj_out = dot(w_out, inner_b, (0, 0))
    update = (out_sig * proj_out).T.astype(jnp.bfloat16)
    upstream = cotangent.reshape(here, width).T.astype(jnp.float32)
    d_proj = (upstream * out_sig).astype(jnp.bfloat16)
    d_gate_out = (upstream * proj_out * out_sig * (1.0 - out_sig)).astype(jnp.bfloat16)
    d_inner_n = dot(w_out, d_proj, (1, 0))
    d_inner = norm_back(d_inner_n, out_gain[:, None], inner_hat, inner_inv, 0).astype(jnp.bfloat16)

    d_inner = jnp.broadcast_to(d_inner[:, None], (hidden, n_parts, here)).reshape(-1, here)
    d_inner = to_matrix(lax.all_to_all(d_inner, ALL, 0, 0))
    d_left = dot(d_inner, right, (1, 0)).astype(jnp.bfloat16)
    d_right = dot(d_inner, left, (0, 0)).astype(jnp.bfloat16)
    d_both = jnp.stack([to_blocks(d_left), to_blocks(d_right)], axis=1)
    d_both = lax.all_to_all(d_both, GROUP, 0, 0).astype(jnp.float32)

    d_both = jnp.concatenate([d_both[:, 0], d_both[:, 1]], axis=0) * pair_mask
    d_values = (d_both * gate_sig).astype(jnp.bfloat16)
    d_gates = (d_both * values * gate_sig * (1.0 - gate_sig)).astype(jnp.bfloat16)
    d_front = jnp.concatenate([d_values, d_gates, d_gate_out], axis=0)
    d_normed = dot(d_front, w_front, (0, 1))
    grad_pair = norm_back(d_normed, in_gain, pair_hat, pair_inv, 1).astype(jnp.bfloat16)
    return (update.reshape(pair.shape), grad_pair.reshape(pair.shape))


def solution(mesh):
    fine = Mesh(mesh.devices.reshape(4, 4, 8, 2, 2), ALL)
    placed = P(ROW, COL, None)
    return jax.shard_map(
        shards,
        mesh=fine,
        in_specs=(placed, placed) + (P(),) * 9,
        out_specs=(placed, placed),
        check_vma=False,
    )
```

time: 1120 us -> 166 us (0.15)
  waiting for transfers between devices: 1040 us -> 32.9 us
  blocking collectives: 0 us -> 62.4 us
  starting transfers between devices: 0.5 us -> 20.7 us
  matrix products: 19.4 us -> 2.74 us
  between operations: 14.5 us -> 1.32 us
    all_gather x6 -> x0, waiting for transfers between devices: 543 us -> none  [the longest x1 105 us: shards(): lax.all_gather(d_inner, 'col', axis=1, tiled=True)]
    psum x2 -> x0, waiting for transfers between devices: 491 us -> none  [from_root(): return lax.psum(block, axis)]
    all_to_all x0 -> x2, blocking collectives: none -> 62.4 us  [the longest x1 32.3 us: shards(): d_inner = to_matrix(lax.all_to_all(d_inner, ALL, 0, 0))]
    all_to_all x0 -> x2, waiting for transfers between devices: none -> 32.9 us  [the longest x1 21.5 us: shards(): inner = lax.all_to_all(inner, ALL, 0, 0).reshape(hidden, n_parts, here)]
    all_gather x5 -> x0, local copies, waits for them, and re-layouts: 29.1 us -> none  [the longest x1 10.9 us: shards(): lax.all_gather(left_tile, 'col', axis=1, tiled=True)]
    all_to_all x0 -> x2, starting transfers between devices: none -> 20.7 us  [the longest x1 13.4 us: shards(): inner = lax.all_to_all(inner, ALL, 0, 0).reshape(hidden, n_parts, here)]
    dot_general x7, matrix products: 19.4 us -> 2.74 us  [dot(): lax.dot_general(a, b, ((contract[:1], contract[1:]), ((), ())), preferred...]
  transfers between devices with their start and end apart: 8 -> 2, of which waited for: 8 -> 2; matrix products, arithmetic and copies ran while one was open for 4% -> 1% of each run, Pallas kernels for 0% -> 0%
where the time goes in v1:
time: 166 us; the launch traced here: 165 us
  blocking collectives  62.4 us (38%)
  waiting for transfers between devices  32.9 us (20%)
  local copies, waits for them, and re-layouts  31.8 us (19%)
  starting transfers between devices  20.7 us (12%)
  other arithmetic  13.6 us (8%)
  matrix products  2.74 us (2%)
    all_to_all x1, blocking collectives, shards(): d_inner = to_matrix(lax.all_to_all(d_inner, ALL, 0, 0))  32.3 us
    all_to_all x1, blocking collectives, shards(): both = lax.all_to_all(both, GROUP, 0, 0)  30.1 us
    all_to_all x1, waiting for transfers between devices, shards(): inner = lax.all_to_all(inner, ALL, 0, 0).reshape(hidden, n_parts, here)  21.5 us
    all_to_all x1, starting transfers between devices, shards(): inner = lax.all_to_all(inner, ALL, 0, 0).reshape(hidden, n_parts, here)  13.4 us
    all_to_all x1, waiting for transfers between devices, shards(): d_both = lax.all_to_all(d_both, GROUP, 0, 0).astype(jnp.float32)  11.4 us
    all_to_all x1, starting transfers between devices, shards(): d_both = lax.all_to_all(d_both, GROUP, 0, 0).astype(jnp.float32)  7.3 us
    unnamed x43, local copies, waits for them, and re-layouts  5.94 us
    reshape x5, local copies, waits for them, and re-layouts, to_blocks(): matrix = matrix.reshape(n_rows, rows_here, -1, cols_here)  4.85 us
  transfers between devices with their start and end apart: 2, of which 2 were waited for; matrix products, arithmetic and copies ran while one was open for 1% of the time, Pallas kernels for 0%

profile of v1, /device:TPU:1, one launch (start us, length us, event | category | flops | bytes accessed | tf_op | source)
XLA Modules:
  0.0 165.4 jit_solution(7197140021877260874)
XLA Ops:
  0.6 0.9 copy.39
  1.6 1.0 convert_reduce_fusion.2
  2.6 1.1 multiply_reduce_fusion.2
  3.7 0.8 constant_dynamic-update-slice_fusion.2
  4.9 1.3 reduce_sum.92
  6.2 0.6 compare_convert_fusion
  6.9 0.7 compare_convert_fusion.1
  7.7 0.8 constant_dynamic-update-slice_fusion.1
  8.5 0.8 constant_dynamic-update-slice_fusion
  9.3 1.0 fusion.19
  10.5 0.2 copy.42
  10.7 30.1 %all_to_all.29 = bf16[128,2,288]{2,1,0:T(2,128)(2,1)S(1)} all-to-all(bf16[128,2,288]{2,1,0:T(2,128)(2,1)S(1)} %copy.42), channel_id=1, replica_groups=mesh['x'=4,'z_lo'=4,'y'=8,'z_hi'=2,'core'=2] {'x','z_lo','y'}, dimensions={0} | all-to-all | bytes 294912 | tf_op jit(solution)/shard_map/all_to_all | solution.py:70
  40.8 1.0 slice_reduce_fusion
  41.9 0.6 reshape_squeeze.6
  42.5 0.9 copy.43
  43.4 0.4 reshape.143
  43.8 0.6 reshape_squeeze.7
  44.4 0.9 copy.44
  45.3 0.4 reshape.144
  45.7 0.3 convolution_convert_fusion
  46.0 0.3 copy-done.7
  46.3 0.2 copy.45
  46.5 2.0 %reshape.145 = bf16[16,24,32,12]{1,0,3,2:T(8,128)(2,1)S(1)} reshape(bf16[384,384]{0,1:T(8,128)(2,1)S(1)} %copy.45) | data formatting | bytes 589824 | tf_op jit(solution)/shard_map/reshape | solution.py:77
  48.6 2.7 %copy.46 = bf16[16,32,24,12]{1,0,3,2:T(8,128)(2,1)S(1)} copy(bf16[16,32,24,12]{2,0,3,1:T(8,128)(2,1)S(1)} %bitcast.83) | data formatting | bytes 589824 | tf_op jit(solution)/shard_map/transpose | solution.py:78
  51.3 1.1 all_to_all.19
  52.4 0.6 broadcast.138
  53.0 0.9 reduce.12
  53.9 0.2 copy.61
  54.1 1.0 reshape.158
  55.1 13.4 %all-to-all-start.1 = ((bf16[512,2,144]{2,1,0:T(2,128)(2,1)}), bf16[512,2,144]{2,1,0:T(2,128)(2,1)S(1)}, u32[]{:S(2)}, u32[]{:S(2)}) async-start(bf16[512,2,144]{2,1,0:T(2,128)(2,1)} %reshape.158), calls=%async_computation.1 | async-start | bytes 1048576 | tf_op jit(solution)/shard_map/all_to_all | solution.py:82
  68.6 21.5 %all-to-all-done.1 = bf16[512,2,144]{2,1,0:T(2,128)(2,1)S(1)} async-done(((bf16[512,2,144]{2,1,0:T(2,128)(2,1)}), bf16[512,2,144]{2,1,0:T(2,128)(2,1)S(1)}, u32[]{:S(2)}, u32[]{:S(2)}) %all-to-all-start.1) | async-done | bytes 294944 | tf_op jit(solution)/shard_map/all_to_all | solution.py:82
  90.1 0.6 reshape.159
  90.6 3.1 %convert_reduce_fusion = (f32[288]{0:T(512)S(1)}, f32[512,288]{1,0:T(8,128)S(1)}) fusion(bf16[512,1,288]{2,1,0:T(2,128)(2,1)S(1)} %reshape.159), kind=kLoop, calls=%fused_computation.6 | loop fusion | flops 294624 | bytes 885888 | tf_op jit(solution)/shard_map/reduce_sum | solution.py:15
  93.8 0.2 reshape.153
  94.0 0.5 reduce_sum.93
  94.6 0.2 multiply_reduce_fusion.1
  94.9 0.3 fusion.14
  95.3 0.2 fusion.13
  95.8 0.3 all_to_all.24
  96.1 3.2 %reduce.13 = bf16[512,288]{1,0:T(8,128)(2,1)S(1)} reduce(bf16[512,1,288]{2,1,0:T(2,128)(2,1)S(1)} %all_to_all.24, bf16[]{:T(256)} %broadcast.138), dimensions={1}, to_apply=%all_to_all.24.reduce_sub_computation | reduce | bytes 589826 | tf_op jit(solution)/shard_map/all_to_all | solution.py:96
  99.3 0.2 reshape.160
  99.5 32.3 %all_to_all.30 = bf16[512,2,144]{2,1,0:T(2,128)(2,1)S(1)} all-to-all(bf16[512,2,144]{2,1,0:T(2,128)(2,1)S(1)} %reshape.160), channel_id=1, replica_groups=mesh['x'=4,'z_lo'=4,'y'=8,'z_hi'=2,'core'=2] {'x','z_lo','y','z_hi','core'}, dimensions={0} | all-to-all | bytes 589824 | tf_op jit(solution)/shard_map/all_to_all | solution.py:96
  131.8 0.6 reshape.161
  132.3 1.1 copy.52
  133.4 0.7 reshape.147
  134.1 2.9 %copy.53 = bf16[16,24,32,12]{1,0,3,2:T(8,128)(2,1)S(1)} copy(bf16[16,24,32,12]{2,0,3,1:T(8,128)(2,1)S(1)} %bitcast.84) | data formatting | bytes 589824 | tf_op jit(solution)/shard_map/transpose | solution.py:74
  137.0 1.8 %reshape.148 = bf16[384,384]{0,1:T(8,128)(2,1)S(1)} reshape(bf16[16,24,32,12]{1,0,3,2:T(8,128)(2,1)S(1)} %copy.53) | data formatting | bytes 589824 | tf_op jit(solution)/shard_map/reshape | solution.py:74
  138.8 0.2 convolution_convert_fusion.2
  139.0 0.2 convolution_convert_fusion.1
  139.2 0.5 reshape.150
  139.7 0.9 copy.55
  140.6 0.4 stack_reshape.7
  141.1 0.5 reshape.149
  141.6 0.9 copy.54
  142.5 0.4 stack_reshape.6
  143.0 0.9 copy.56
  143.9 7.3 %all-to-all-start.3 = ((bf16[128,2,288]{2,1,0:T(2,128)(2,1)}), bf16[128,2,288]{2,1,0:T(2,128)(2,1)S(1)}, u32[]{:S(2)}, u32[]{:S(2)}) async-start(bf16[128,2,288]{2,1,0:T(2,128)(2,1)} %copy.56), calls=%async_computation.3 | async-start | bytes 393216 | tf_op jit(solution)/shard_map/all_to_all | solution.py:100
  151.2 0.3 fusion.18
  151.6 0.7 copy.58
  152.2 11.4 %all-to-all-done.3 = bf16[128,2,288]{2,1,0:T(2,128)(2,1)S(1)} async-done(((bf16[128,2,288]{2,1,0:T(2,128)(2,1)}), bf16[128,2,288]{2,1,0:T(2,128)(2,1)S(1)}, u32[]{:S(2)}, u32[]{:S(2)}) %all-to-all-start.3) | async-done | bytes 147488 | tf_op jit(solution)/shard_map/all_to_all | solution.py:100
  163.6 0.2 copy.57
  164.0 0.4 fusion.32
  164.5 0.2 multiply_convert_fusion.3
  164.8 0.7 copy.59
  (62 shorter events, 1.6 us)
Async XLA Ops:
  0.6 94.2 %copy-start = (bf16[128,128]{1,0:T(8,128)(2,1)S(1)}, bf16[128,128]{1,0:T(8,128)(2,1)}, u32[]{:S(2)}) copy-start(bf16[128,128]{1,0:T(8,128)(2,1)} %param.21) | copy-start | bytes 98308
  4.6 5.9 %copy-start.1 = (f32[288,128]{1,0:T(8,128)}, f32[288,128]{1,0:T(8,128)S(1)}, u32[]{:S(2)}) copy-start(f32[288,128]{1,0:T(8,128)S(1)} %reshape.152) | copy-start | bytes 442372
  9.3 1.2 copy-start.9
  43.8 2.2 %copy-start.5 = (bf16[384,96]{0,1:T(8,128)(2,1)}, bf16[384,96]{0,1:T(8,128)(2,1)S(1)}, u32[]{:S(2)}) copy-start(bf16[384,96]{0,1:T(8,128)(2,1)S(1)} %reshape.143) | copy-start | bytes 221188
  45.7 0.6 copy-start.7
  53.0 15.5 %copy-start.13 = (bf16[24,12,128]{2,0,1:T(8,128)(2,1)S(1)}, bf16[24,12,128]{2,0,1:T(8,128)(2,1)}, u32[]{:S(2)}) copy-start(bf16[24,12,128]{2,0,1:T(8,128)(2,1)} %param.12) | copy-start | bytes 221188
  55.1 35.0 %all-to-all-start.1 = ((bf16[512,2,144]{2,1,0:T(2,128)(2,1)}), bf16[512,2,144]{2,1,0:T(2,128)(2,1)S(1)}, u32[]{:S(2)}, u32[]{:S(2)}) async-start(bf16[512,2,144]{2,1,0:T(2,128)(2,1)} %reshape.158), calls=%async_computation.1 | async-start | bytes 1048576 | tf_op jit(solution)/shard_map/all_to_all | solution.py:82
  68.5 26.3 %copy-start.11 = (f32[288,128]{1,0:T(8,128)}, f32[288,128]{1,0:T(8,128)S(1)}, u32[]{:S(2)}) copy-start(f32[288,128]{1,0:T(8,128)S(1)} %reshape.154) | copy-start | bytes 442372
  93.8 1.1 copy-start.16
  94.6 1.1 copy-start.3
  136.9 1.8 %copy-start.6 = (bf16[384,96]{0,1:T(8,128)(2,1)S(1)}, bf16[384,96]{0,1:T(8,128)(2,1)}, u32[]{:S(2)}) copy-start(bf16[384,96]{0,1:T(8,128)(2,1)} %copy-done.5) | copy-start | bytes 221188
  137.0 2.0 %copy-start.8 = (bf16[384,96]{0,1:T(8,128)(2,1)S(1)}, bf16[384,96]{0,1:T(8,128)(2,1)}, u32[]{:S(2)}) copy-start(bf16[384,96]{0,1:T(8,128)(2,1)} %copy-done.7) | copy-start | bytes 221188
  141.6 9.6 %copy-start.4 = (f32[128,288]{0,1:T(8,128)S(1)}, f32[128,288]{0,1:T(8,128)}, u32[]{:S(2)}) copy-start(f32[128,288]{0,1:T(8,128)} %copy-done.3) | copy-start | bytes 442372
  141.6 9.6 %copy-start.12 = (f32[288,128]{1,0:T(8,128)S(1)}, f32[288,128]{1,0:T(8,128)}, u32[]{:S(2)}) copy-start(f32[288,128]{1,0:T(8,128)} %copy-done.11) | copy-start | bytes 442372
  141.6 9.6 %copy-start.15 = (f32[128]{0:T(128)S(1)}, f32[128]{0:T(128)}, u32[]{:S(2)}) copy-start(f32[128]{0:T(128)} %param.20) | copy-start | bytes 1540
  143.9 19.7 %all-to-all-start.3 = ((bf16[128,2,288]{2,1,0:T(2,128)(2,1)}), bf16[128,2,288]{2,1,0:T(2,128)(2,1)S(1)}, u32[]{:S(2)}, u32[]{:S(2)}) async-start(bf16[128,2,288]{2,1,0:T(2,128)(2,1)} %copy.56), calls=%async_computation.3 | async-start | bytes 393216 | tf_op jit(solution)/shard_map/all_to_all | solution.py:100
  151.5 12.5 %copy-start.2 = (f32[288,128]{1,0:T(8,128)S(1)}, f32[288,128]{1,0:T(8,128)}, u32[]{:S(2)}) copy-start(f32[288,128]{1,0:T(8,128)} %copy-done.1) | copy-start | bytes 442372
  151.5 12.5 %copy-start.10 = (bf16[128,640]{1,0:T(8,128)(2,1)S(1)}, bf16[128,640]{1,0:T(8,128)(2,1)}, u32[]{:S(2)}) copy-start(bf16[128,640]{1,0:T(8,128)(2,1)} %copy-done.9) | copy-start | bytes 491524
  151.5 12.5 %copy-start.14 = (f32[128]{0:T(128)S(1)}, f32[128]{0:T(128)}, u32[]{:S(2)}) copy-start(f32[128]{0:T(128)} %param.14) | copy-start | bytes 1540

commit v2 on v1

v2 whole, which is shorter than its diff:
```python
import jax
import jax.numpy as jnp
from jax import lax
from jax.experimental import pallas as pl
from jax.experimental.pallas import tpu as pltpu
from jax.sharding import Mesh
from jax.sharding import PartitionSpec as P

EPS = 1e-05
F32 = jnp.float32
BF16 = jnp.bfloat16
ROW = ("x", "z_lo")
COL = ("y", "z_hi", "core")
GROUP = ("z_lo",) + COL
SLOT = 16
SWAP = 8


def dot(a, b, contract):
    return lax.dot_general(a, b, ((contract[:1], contract[1:]), ((), ())), preferred_element_type=F32)


def swap_groups(x):
    sub = lax.broadcasted_iota(jnp.int32, x.shape, 1)
    group = lax.broadcasted_iota(jnp.int32, x.shape, 2) // SLOT
    for step in (4, 2, 1):
        up = pltpu.roll(pltpu.roll(x, SWAP - step, 1), SLOT * step, 2)
        down = up if step == 4 else pltpu.roll(pltpu.roll(x, step, 1), 128 - SLOT * step, 2)
        sub_bit, group_bit = (sub & step) != 0, (group & step) != 0
        x = jnp.where(sub_bit == group_bit, x, jnp.where(group_bit, up, down))
    return x


def to_matrix(blocks, out):
    for i_hi in range(3):
        part = blocks[:, 128 * i_hi : 128 * (i_hi + 1)].reshape(16, 8, 128)
        part = swap_groups(part)
        for z in range(4):
            for c_hi in range(4):
                row = 24 * z + 8 * i_hi
                out[row : row + 8, 128 * c_hi : 128 * (c_hi + 1)] = part[4 * z + c_hi]


def to_blocks(matrix, out):
    for i_hi in range(3):
        for z in range(4):
            row = 24 * z + 8 * i_hi
            part = jnp.stack([matrix[row : row + 8, 128 * c : 128 * (c + 1)] for c in range(4)])
            part = swap_groups(part).reshape(32, 128)
            out[32 * z : 32 * (z + 1), 128 * i_hi : 128 * (i_hi + 1)] = part


def spread():
    token = lax.broadcasted_iota(jnp.int32, (384, 512), 0)
    lane = lax.broadcasted_iota(jnp.int32, (384, 512), 1)
    slot = lane % SLOT
    hit = (token == lane // SLOT * 12 + slot) & (slot < 12)
    return hit.astype(F32).astype(BF16)


def live_mask(counts):
    valid = counts[0] + counts[1] + counts[2] + counts[3]
    lane = lax.broadcasted_iota(jnp.int32, (1, 384), 1)
    i, j = lane // SLOT, lane % SLOT
    row = lax.axis_index("x") * 4 + lax.axis_index("z_lo")
    col = lax.axis_index("y") * 4 + lax.axis_index("z_hi") * 2 + lax.axis_index("core")
    live = (row * 24 + i < valid) & (col * 12 + j < valid) & (j < 12)
    return live.astype(F32)


def column(vector, width):
    square = jnp.broadcast_to(vector.reshape(1, 128), (128, 128)).T
    return jnp.concatenate([square] * (width // 128), axis=1)


def load_tile(tile, scratch):
    scratch[...] = jnp.zeros_like(scratch)
    scratch[:, :12, :] = tile[...].astype(F32)
    return scratch[...].reshape(384, 128)


def front_kernel(counts, pair, gain, bias, w_values, w_gates, both, values, gate, hat, inv, normed, tile):
    x = load_tile(pair, tile)
    centre = x - jnp.mean(x, axis=1, keepdims=True)
    inv_std = lax.rsqrt(jnp.mean(centre * centre, axis=1, keepdims=True) + EPS)
    pair_hat = centre * inv_std
    normed_b = (pair_hat * gain[...].reshape(1, 128) + bias[...].reshape(1, 128)).astype(BF16)
    hat[...] = pair_hat
    inv[...] = jnp.broadcast_to(inv_std, (384, 128))
    normed[...] = normed_b
    vals = dot(w_values[...], normed_b, (0, 1))
    sig = jax.nn.sigmoid(dot(w_gates[...], normed_b, (0, 1)))
    values[...] = vals
    gate[...] = sig
    out = (sig * vals * live_mask(counts)).astype(BF16)
    both[:, :384] = out[:128]
    both[:, 384:] = out[128:]


def gate_kernel(normed, cotangent, w_out_gate, w_out, out_gain, out_sig, upstream, scaled, tile):
    sig = jax.nn.sigmoid(dot(w_out_gate[...], normed[...], (0, 1)))
    up = load_tile(cotangent, tile).T
    d_proj = (up * sig).astype(BF16)
    out_sig[...] = sig
    upstream[...] = up
    scaled[...] = dot(w_out[...], d_proj, (1, 0)) * column(out_gain[...], 384)


def split_kernel(both, left, right, matrix):
    to_matrix(both[:, :384].astype(F32), matrix)
    left[...] = matrix[...].astype(BF16)
    to_matrix(both[:, 384:].astype(F32), matrix)
    rounded = matrix[...].astype(BF16)
    for part in range(4):
        right[part] = rounded


def inner_kernel(left, right, inner, blocks):
    product = dot(left[...], right[...].reshape(384, 512), (1, 1)).astype(BF16)
    to_blocks(dot(product, spread(), (1, 0)), blocks)
    inner[...] = blocks[...].astype(BF16)


def norm_kernel(inner, scaled, out_gain, out_bias, d_inner, inner_b):
    x = inner[...].astype(F32)
    centre = x - jnp.mean(x, axis=0, keepdims=True)
    inv_std = lax.rsqrt(jnp.mean(centre * centre, axis=0, keepdims=True) + EPS)
    hat = centre * inv_std
    up = scaled[...]
    first_mean = jnp.mean(up, axis=0, keepdims=True)
    second_mean = jnp.mean(up * hat, axis=0, keepdims=True)
    d_inner[...] = (inv_std * (up - first_mean - hat * second_mean)).astype(BF16)
    inner_b[...] = (hat * column(out_gain[...], 384) + column(out_bias[...], 384)).astype(BF16)


def update_kernel(inner_b, out_sig, upstream, w_out, w_out_gate, update, d_normed):
    proj = dot(w_out[...], inner_b[...], (0, 0))
    sig = out_sig[...]
    gated = (sig * proj).T.reshape(24, SLOT, 128)
    update[...] = gated[:, :12, :].astype(BF16)
    d_gate_out = (upstream[...] * proj * sig * (1.0 - sig)).astype(BF16)
    d_normed[...] = dot(d_gate_out, w_out_gate[...], (0, 1))


def grad_kernel(d_inner, left, right, d_left, d_right, matrix):
    to_matrix(d_inner[...].astype(F32), matrix)
    packed = dot(matrix[...].astype(BF16), spread(), (1, 1)).astype(BF16)
    d_left[...] = dot(packed, right[...].reshape(384, 512), (1, 0))
    d_right[...] = dot(packed, left[...], (0, 0)).astype(BF16).reshape(4, 96, 512)


def merge_kernel(d_left, d_right, d_both, blocks):
    to_blocks(d_left[...], blocks)
    d_both[:, :384] = blocks[...].astype(BF16)
    parts = [d_right[part].astype(F32) for part in range(4)]
    to_blocks((parts[0] + parts[1]) + (parts[2] + parts[3]), blocks)
    d_both[:, 384:] = blocks[...].astype(BF16)


def back_kernel(counts, d_both, values, gate, d_out, hat, inv, gain, w_values, w_gates, grad):
    live = live_mask(counts)
    incoming = jnp.concatenate([d_both[:, :384], d_both[:, 384:]], axis=0).astype(F32) * live
    sig = gate[...]
    d_values = (incoming * sig).astype(BF16)
    d_gates = (incoming * values[...] * sig * (1.0 - sig)).astype(BF16)
    d_normed = d_out[...] + dot(d_values, w_values[...], (0, 1)) + dot(d_gates, w_gates[...], (0, 1))
    scaled = d_normed * gain[...].reshape(1, 128)
    pair_hat = hat[...]
    first_mean = jnp.mean(scaled, axis=1, keepdims=True)
    second_mean = jnp.mean(scaled * pair_hat, axis=1, keepdims=True)
    out = inv[...] * (scaled - first_mean - pair_hat * second_mean)
    grad[...] = out.reshape(24, SLOT, 128)[:, :12, :].astype(BF16)


def call(kernel, outs, args, scratch=(), scalars=0, flops=0):
    vmem, smem = pl.BlockSpec(memory_space=pltpu.VMEM), pl.BlockSpec(memory_space=pltpu.SMEM)
    outs = [jax.ShapeDtypeStruct(shape, dtype) for shape, dtype in outs]
    size = sum(a.size * a.dtype.itemsize for a in list(args) + outs)
    return pl.pallas_call(
        kernel,
        out_shape=outs,
        in_specs=[smem] * scalars + [vmem] * (len(args) - scalars),
        out_specs=[vmem] * len(outs),
        scratch_shapes=[pltpu.VMEM(shape, F32) for shape in scratch],
        compiler_params=pltpu.CompilerParams(vmem_limit_bytes=24 * 1024 * 1024),
        cost_estimate=pl.CostEstimate(flops=flops, bytes_accessed=size, transcendentals=0),
    )(*args)


def shards(
    pair,
    cotangent,
    chain_counts,
    in_gain,
    in_bias,
    w_values,
    w_gates,
    w_out_gate,
    out_gain,
    out_bias,
    w_out,
):
    wide, tall = (256, 384), (128, 384)
    tile = (24, SLOT, 128)
    both, values, gate, hat, inv, normed = call(
        front_kernel,
        [((128, 768), BF16), (wide, F32), (wide, F32), ((384, 128), F32), ((384, 128), F32), ((384, 128), BF16)],
        [chain_counts, pair, in_gain, in_bias, w_values, w_gates],
        [tile],
        scalars=1,
    )
    both = lax.all_to_all(both, GROUP, 0, 0)
    out_sig, upstream, scaled = call(
        gate_kernel,
        [(tall, F32)] * 3,
        [normed, cotangent, w_out_gate, w_out, out_gain],
        [tile],
    )
    left, right = call(split_kernel, [((96, 512), BF16), ((4, 96, 512), BF16)], [both], [(96, 512)])
    right = lax.all_to_all(right, "x", 0, 0)
    (inner,) = call(inner_kernel, [(tall, BF16)], [left, right], [tall])
    inner = lax.all_to_all(inner, GROUP, 0, 0)
    d_inner, inner_b = call(norm_kernel, [(tall, BF16)] * 2, [inner, scaled, out_gain, out_bias])
    d_inner = lax.all_to_all(d_inner, GROUP, 0, 0)
    update, d_out = call(
        update_kernel,
        [(pair.shape, BF16), ((384, 128), F32)],
        [inner_b, out_sig, upstream, w_out, w_out_gate],
    )
    d_left, d_right = call(
        grad_kernel, [((96, 512), F32), ((4, 96, 512), BF16)], [d_inner, left, right], [(96, 512)]
    )
    d_right = lax.all_to_all(d_right, "x", 0, 0)
    (d_both,) = call(merge_kernel, [((128, 768), BF16)], [d_left, d_right], [tall])
    d_both = lax.all_to_all(d_both, GROUP, 0, 0)
    (grad,) = call(
        back_kernel,
        [(pair.shape, BF16)],
        [chain_counts, d_both, values, gate, d_out, hat, inv, in_gain, w_values, w_gates],
        scalars=1,
    )
    return (update, grad)


def solution(mesh):
    fine = Mesh(mesh.devices.reshape(4, 4, 8, 2, 2), ROW + COL)
    placed = P(ROW, COL, None)
    return jax.shard_map(
        shards,
        mesh=fine,
        in_specs=(placed, placed) + (P(),) * 9,
        out_specs=(placed, placed),
        check_vma=False,
    )
```

time: 166 us -> 125 us (0.75)
  local copies, waits for them, and re-layouts: 31.8 us -> 6.62 us
  other arithmetic: 13.6 us -> 2.79 us
  waiting for transfers between devices: 32.9 us -> 23.9 us
  blocking collectives: 62.4 us -> 70.5 us
  starting transfers between devices: 20.7 us -> 13.5 us
  Pallas kernels: 0 us -> 6.59 us
  matrix products: 2.74 us -> 0 us
    all_to_all x2, waiting for transfers between devices: 32.9 us -> 23.9 us  [the longest x1 12.7 us: shards(): d_both = lax.all_to_all(d_both, GROUP, 0, 0)]
    reshape x11 -> x0, local copies, waits for them, and re-layouts: 8.1 us -> none  [the longest x5 4.85 us: to_blocks(): matrix = matrix.reshape(n_rows, rows_here, -1, cols_here)]
    transpose x4 -> x0, local copies, waits for them, and re-layouts: 7.36 us -> none  [the longest x3 4.68 us: to_matrix(): return blocks.transpose(0, 2, 1, 3).reshape(tokens, -1)]
    reduce_sum x7 -> x0, other arithmetic: 7.31 us -> none  [the longest x2 4.12 us: layer_norm(): centre = values_in - jnp.mean(values_in, axis=axis, keepdims=True)]
    all_to_all x2, starting transfers between devices: 20.7 us -> 13.5 us  [the longest x1 7.13 us: shards(): inner = lax.all_to_all(inner, GROUP, 0, 0)]
    pallas_call x0 -> x9, Pallas kernels: none -> 6.59 us  [call(): pl.pallas_call(kernel, out_shape=outs, in_specs=[smem] * scalars + [vmem]...]
    all_to_all x1 -> x3, blocking collectives: 32.3 us -> 38.7 us  [the longest x1 17.5 us: shards(): d_inner = lax.all_to_all(d_inner, GROUP, 0, 0)]
    another operation x7 -> x0, local copies, waits for them, and re-layouts: 3.16 us -> none  [the longest x3 1.74 us: shards(): d_both = jnp.stack([to_blocks(d_left), to_blocks(d_right)], axis=1)]
  transfers between devices with their start and end apart: 2 -> 2, of which waited for: 2 -> 2; matrix products, arithmetic and copies ran while one was open for 1% -> 1% of each run, Pallas kernels for 0% -> 1%
where the time goes in v2:
time: 125 us
  blocking collectives  70.5 us (56%)
  waiting for transfers between devices  23.9 us (19%)
  starting transfers between devices  13.5 us (11%)
  local copies, waits for them, and re-layouts  6.62 us (5%)
  Pallas kernels  6.59 us (5%)
  other arithmetic  2.79 us (2%)
    all_to_all x1, blocking collectives, shards(): both = lax.all_to_all(both, GROUP, 0, 0)  31.8 us
    all_to_all x1, blocking collectives, shards(): d_inner = lax.all_to_all(d_inner, GROUP, 0, 0)  17.5 us
    all_to_all x1, waiting for transfers between devices, shards(): d_both = lax.all_to_all(d_both, GROUP, 0, 0)  12.7 us
    all_to_all x1, waiting for transfers between devices, shards(): inner = lax.all_to_all(inner, GROUP, 0, 0)  11.3 us
    all_to_all x1, blocking collectives, shards(): right = lax.all_to_all(right, 'x', 0, 0)  11 us
    all_to_all x1, blocking collectives, shards(): d_right = lax.all_to_all(d_right, 'x', 0, 0)  10.2 us
    all_to_all x1, starting transfers between devices, shards(): inner = lax.all_to_all(inner, GROUP, 0, 0)  7.13 us
    pallas_call x9, Pallas kernels, call(): pl.pallas_call(kernel, out_shape=outs, in_specs=[smem] * scalars + [vmem]...  6.59 us
  transfers between devices with their start and end apart: 2, of which 2 were waited for; matrix products, arithmetic and copies ran while one was open for 1% of the time, Pallas kernels for 1%

profile of v2, /device:TPU:1, one launch (start us, length us, event | category | flops | bytes accessed | tf_op | source)
XLA Modules:
  0.0 124.9 jit_solution(10137662454757345547)
XLA Ops:
  0.6 0.0 copy-start.1
  0.6 0.0 copy-start
  0.7 0.0 copy-start.6
  0.7 0.0 copy-start.5
  0.7 0.0 copy-start.7
  0.7 1.0 copy.25.pair
  1.6 0.0 copy-done.1
  1.7 0.0 copy-done
  1.7 0.0 copy-done.6
  1.7 0.0 copy-done.5
  1.7 0.0 copy-done.7
  1.7 1.0 shard_map.122
  2.7 0.5 broadcast
  3.2 0.7 reduce
  4.0 0.1 reshape.12
  4.0 31.8 %all_to_all.54 = bf16[128,2,384]{2,1,0:T(2,128)(2,1)S(1)} all-to-all(bf16[128,2,384]{2,1,0:T(2,128)(2,1)S(1)} %reshape.12), channel_id=1, replica_groups=mesh['x'=4,'z_lo'=4,'y'=8,'z_hi'=2,'core'=2] {'z_lo','y','z_hi','core'}, dimensions={0} | all-to-all | bytes 393216 | tf_op jit(solution)/shard_map/all_to_all | solution.py:212
  35.9 0.1 reshape.13
  36.1 0.8 shard_map.123
  36.8 11.0 %all_to_all.55.right = bf16[4,96,512]{2,1,0:T(8,128)(2,1)S(1)} all-to-all(bf16[4,96,512]{2,1,0:T(8,128)(2,1)S(1)} %get-tuple-element.21), channel_id=1, replica_groups=mesh['x'=4,'z_lo'=4,'y'=8,'z_hi'=2,'core'=2] {'x'}, dimensions={0} | all-to-all | bytes 786432 | tf_op jit(solution)/shard_map/all_to_all | solution.py:220
  47.8 0.7 shard_map.124
  48.5 0.7 reduce.1
  49.2 0.8 reshape.14
  50.0 0.0 copy-start.9
  50.0 7.1 %all-to-all-start.2 = ((bf16[128,2,192]{2,1,0:T(2,128)(2,1)}), bf16[128,2,192]{2,1,0:T(2,128)(2,1)S(1)}, u32[]{:S(2)}, u32[]{:S(2)}) async-start(bf16[128,2,192]{2,1,0:T(2,128)(2,1)} %reshape.14), calls=%async_computation.2 | async-start | bytes 262144 | tf_op jit(solution)/shard_map/all_to_all | solution.py:222
  57.1 0.0 copy-done.9
  57.1 0.0 copy-start.2
  57.1 0.0 copy-start.3
  57.2 0.0 copy-start.4
  57.2 0.7 copy-done.2
  57.9 0.0 copy-done.3
  57.9 0.0 copy-done.4
  57.9 0.4 shard_map.125
  58.3 11.3 %all-to-all-done.2 = bf16[128,2,192]{2,1,0:T(2,128)(2,1)S(1)} async-done(((bf16[128,2,192]{2,1,0:T(2,128)(2,1)}), bf16[128,2,192]{2,1,0:T(2,128)(2,1)S(1)}, u32[]{:S(2)}, u32[]{:S(2)}) %all-to-all-start.2) | async-done | bytes 98336 | tf_op jit(solution)/shard_map/all_to_all | solution.py:222
  69.6 0.2 reshape.15
  69.8 0.0 copy-start.8
  69.8 0.6 copy-done.8
  70.4 0.2 shard_map.126
  70.6 0.7 reduce.2
  71.3 0.1 reshape.16
  71.4 17.5 %all_to_all.56 = bf16[128,2,192]{2,1,0:T(2,128)(2,1)S(1)} all-to-all(bf16[128,2,192]{2,1,0:T(2,128)(2,1)S(1)} %reshape.16), channel_id=1, replica_groups=mesh['x'=4,'z_lo'=4,'y'=8,'z_hi'=2,'core'=2] {'z_lo','y','z_hi','core'}, dimensions={0} | all-to-all | bytes 196608 | tf_op jit(solution)/shard_map/all_to_all | solution.py:224
  88.9 0.2 reshape.17
  89.1 0.8 shard_map.128
  89.9 10.2 %all_to_all.57.d_right = bf16[4,96,512]{2,1,0:T(8,128)(2,1)S(1)} all-to-all(bf16[4,96,512]{2,1,0:T(8,128)(2,1)S(1)} %get-tuple-element.30), channel_id=1, replica_groups=mesh['x'=4,'z_lo'=4,'y'=8,'z_hi'=2,'core'=2] {'x'}, dimensions={0} | all-to-all | bytes 786432 | tf_op jit(solution)/shard_map/all_to_all | solution.py:233
  100.1 1.4 %shard_map.129 = bf16[128,768]{1,0:T(8,128)(2,1)S(1)} custom-call(f32[96,512]{1,0:T(8,128)S(1)} %get-tuple-element.29.d_left, bf16[4,96,512]{2,1,0:T(8,128)(2,1)S(1)} %all_to_all.57.d_right), custom_call_target="tpu_custom_call" | custom-call | bytes 786432 | tf_op jit(solution)/shard_map/pallas_call | solution.py:179
  101.5 0.7 reduce.3
  102.2 0.7 reshape.18
  103.0 6.4 %all-to-all-start.5 = ((bf16[128,2,384]{2,1,0:T(2,128)(2,1)}), bf16[128,2,384]{2,1,0:T(2,128)(2,1)S(1)}, u32[]{:S(2)}, u32[]{:S(2)}) async-start(bf16[128,2,384]{2,1,0:T(2,128)(2,1)} %reshape.18), calls=%async_computation.5 | async-start | bytes 393216 | tf_op jit(solution)/shard_map/all_to_all | solution.py:235
  109.3 0.4 shard_map.127
  109.8 0.7 copy.31
  110.4 12.7 %all-to-all-done.5 = bf16[128,2,384]{2,1,0:T(2,128)(2,1)S(1)} async-done(((bf16[128,2,384]{2,1,0:T(2,128)(2,1)}), bf16[128,2,384]{2,1,0:T(2,128)(2,1)S(1)}, u32[]{:S(2)}, u32[]{:S(2)}) %all-to-all-start.5) | async-done | bytes 196640 | tf_op jit(solution)/shard_map/all_to_all | solution.py:235
  123.1 0.1 reshape.19
  123.3 1.0 shard_map.130
  124.2 0.7 copy.32
  (5 shorter events, 0.1 us)
Async XLA Ops:
  0.6 1.0 copy-start.1
  0.6 1.0 copy-start
  0.7 1.0 copy-start.6
  0.7 1.0 copy-start.5
  0.7 1.0 copy-start.7
  50.0 7.1 %copy-start.9 = (bf16[24,12,128]{2,0,1:T(8,128)(2,1)S(1)}, bf16[24,12,128]{2,0,1:T(8,128)(2,1)}, u32[]{:S(2)}) copy-start(bf16[24,12,128]{2,0,1:T(8,128)(2,1)} %param.12) | copy-start | bytes 221188
  50.0 19.6 %all-to-all-start.2 = ((bf16[128,2,192]{2,1,0:T(2,128)(2,1)}), bf16[128,2,192]{2,1,0:T(2,128)(2,1)S(1)}, u32[]{:S(2)}, u32[]{:S(2)}) async-start(bf16[128,2,192]{2,1,0:T(2,128)(2,1)} %reshape.14), calls=%async_computation.2 | async-start | bytes 262144 | tf_op jit(solution)/shard_map/all_to_all | solution.py:222
  57.1 0.8 copy-start.2
  57.1 0.8 copy-start.3
  57.2 0.7 copy-start.4
  69.8 0.7 copy-start.8
  103.0 20.1 %all-to-all-start.5 = ((bf16[128,2,384]{2,1,0:T(2,128)(2,1)}), bf16[128,2,384]{2,1,0:T(2,128)(2,1)S(1)}, u32[]{:S(2)}, u32[]{:S(2)}) async-start(bf16[128,2,384]{2,1,0:T(2,128)(2,1)} %reshape.18), calls=%async_computation.5 | async-start | bytes 393216 | tf_op jit(solution)/shard_map/all_to_all | solution.py:235

commit v3 on v2

v3 whole, which is shorter than its diff:
```python
import jax
import jax.numpy as jnp
from jax import lax
from jax.experimental import pallas as pl
from jax.experimental.pallas import tpu as pltpu
from jax.sharding import Mesh
from jax.sharding import PartitionSpec as P

EPS = 1e-05
F32 = jnp.float32
BF16 = jnp.bfloat16
ROW = ("x", "z_lo")
COL = ("y", "z_hi", "core")
GROUP = ("z_lo",) + COL
SLOTS = 16
LOW = 8


def dot(a, b, contract):
    return lax.dot_general(a, b, ((contract[:1], contract[1:]), ((), ())), preferred_element_type=F32)


def swap_groups(x):
    sub = lax.broadcasted_iota(jnp.int32, x.shape, 1)
    lane = lax.broadcasted_iota(jnp.int32, x.shape, 2)
    for step in (4, 2, 1):
        up = pltpu.roll(pltpu.roll(x, LOW - step, 1), step, 2)
        down = pltpu.roll(pltpu.roll(x, step, 1), 128 - step, 2)
        sub_bit, lane_bit = (sub & step) != 0, (lane & step) != 0
        x = jnp.where(sub_bit == lane_bit, x, jnp.where(lane_bit, up, down))
    return x


def to_matrix(rows, first, per, out):
    for i_hi in range(3):
        part = rows[pl.ds(first + i_hi, 128, stride=per), :].reshape(16, LOW, 128)
        part = swap_groups(part)
        for z in range(4):
            for c_hi in range(4):
                row = 24 * z + LOW * i_hi
                out[row : row + LOW, 128 * c_hi : 128 * (c_hi + 1)] = part[4 * z + c_hi]


def to_rows(matrix, rows, first, per):
    for i_hi in range(3):
        parts = []
        for z in range(4):
            row = 24 * z + LOW * i_hi
            parts += [matrix[row : row + LOW, 128 * c : 128 * (c + 1)] for c in range(4)]
        rows[pl.ds(first + i_hi, 128, stride=per), :] = swap_groups(jnp.stack(parts)).reshape(128, 128)


def spread():
    lane = lax.broadcasted_iota(jnp.int32, (1, 512), 1)
    slot = lane % 128 // LOW
    token = (lane // 128 * LOW + lane % LOW) * 12 + slot
    token = jnp.where(slot < 12, token, -1)
    hit = lax.broadcasted_iota(jnp.int32, (384, 512), 0) == token
    return jnp.where(hit, 1.0, 0.0).astype(BF16)


def live_mask(counts):
    valid = counts[0] + counts[1] + counts[2] + counts[3]
    lane = lax.broadcasted_iota(jnp.int32, (1, 384), 1)
    i, j = lane // 128 * LOW + lane % LOW, lane % 128 // LOW
    row = lax.axis_index("x") * 4 + lax.axis_index("z_lo")
    col = lax.axis_index("y") * 4 + lax.axis_index("z_hi") * 2 + lax.axis_index("core")
    live = (row * 24 + i < valid) & (col * 12 + j < valid) & (j < 12)
    return live.astype(F32)


def column(vector, width):
    square = jnp.broadcast_to(vector.reshape(1, 128), (128, 128)).T
    return jnp.concatenate([square] * (width // 128), axis=1)


def load_tile(tile):
    x = tile[...].astype(F32)
    gap = jnp.zeros(((SLOTS - 12) * LOW, 128), F32)
    parts = []
    for i_hi in range(3):
        parts += [x[:, LOW * i_hi : LOW * (i_hi + 1)].reshape(12 * LOW, 128), gap]
    return jnp.concatenate(parts, axis=0)


def store_tile(value, scratch, tile):
    for i_hi in range(3):
        part = value[128 * i_hi : 128 * i_hi + 12 * LOW].reshape(12, LOW, 128)
        scratch[:, LOW * i_hi : LOW * (i_hi + 1), :] = part
    tile[...] = scratch[...].astype(BF16)


def third(value, i_hi):
    return value[:, 128 * i_hi : 128 * (i_hi + 1)]


def front_kernel(counts, pair, gain, bias, w_values, w_gates, both, values, gate, hat, inv, normed, rows):
    x = load_tile(pair)
    centre = x - jnp.mean(x, axis=1, keepdims=True)
    inv_std = lax.rsqrt(jnp.mean(centre * centre, axis=1, keepdims=True) + EPS)
    pair_hat = centre * inv_std
    normed_b = (pair_hat * gain[...].reshape(1, 128) + bias[...].reshape(1, 128)).astype(BF16)
    hat[...] = pair_hat
    inv[...] = jnp.broadcast_to(inv_std, (384, 128))
    normed[...] = normed_b
    vals = dot(w_values[...], normed_b, (0, 1))
    sig = jax.nn.sigmoid(dot(w_gates[...], normed_b, (0, 1)))
    values[...] = vals
    gate[...] = sig
    out = sig * vals * live_mask(counts)
    for i_hi in range(3):
        rows[pl.ds(i_hi, 128, stride=8), :] = third(out[:128], i_hi)
        rows[pl.ds(3 + i_hi, 128, stride=8), :] = third(out[128:], i_hi)
    for spare in (6, 7):
        rows[pl.ds(spare, 128, stride=8), :] = jnp.zeros((128, 128), F32)
    both[...] = rows[...].astype(BF16)


def gate_kernel(normed, cotangent, w_out_gate, w_out, out_gain, out_sig, upstream, scaled):
    sig = jax.nn.sigmoid(dot(w_out_gate[...], normed[...], (0, 1)))
    up = load_tile(cotangent).T
    d_proj = (up * sig).astype(BF16)
    out_sig[...] = sig
    upstream[...] = up
    scaled[...] = dot(w_out[...], d_proj, (1, 0)) * column(out_gain[...], 384)


def split_kernel(both, left, right, rows, matrix):
    rows[...] = both[...].astype(F32)
    one_hot = spread()
    to_matrix(rows, 0, 8, matrix)
    left[...] = dot(matrix[...].astype(BF16), one_hot, (1, 1)).astype(BF16)
    to_matrix(rows, 3, 8, matrix)
    packed = dot(matrix[...].astype(BF16), one_hot, (1, 1)).astype(BF16)
    for part in range(4):
        right[part] = packed


def inner_kernel(left, right, inner, rows):
    product = dot(left[...], right[...].reshape(384, 384), (1, 1)).astype(BF16)
    to_rows(dot(product, spread(), (1, 0)), rows, 0, 4)
    rows[pl.ds(3, 128, stride=4), :] = jnp.zeros((128, 128), F32)
    inner[...] = rows[...].astype(BF16)


def norm_kernel(inner, scaled, d_inner, inner_hat, rows):
    rows[...] = inner[...].astype(F32)
    for i_hi in range(3):
        x = rows[pl.ds(i_hi, 128, stride=4), :]
        centre = x - jnp.mean(x, axis=0, keepdims=True)
        inv_std = lax.rsqrt(jnp.mean(centre * centre, axis=0, keepdims=True) + EPS)
        hat = centre * inv_std
        up = scaled[:, 128 * i_hi : 128 * (i_hi + 1)]
        first_mean = jnp.mean(up, axis=0, keepdims=True)
        second_mean = jnp.mean(up * hat, axis=0, keepdims=True)
        rows[pl.ds(i_hi, 128, stride=4), :] = inv_std * (up - first_mean - hat * second_mean)
        inner_hat[:, 128 * i_hi : 128 * (i_hi + 1)] = hat
    d_inner[...] = rows[...].astype(BF16)


def update_kernel(inner_hat, out_sig, upstream, out_gain, out_bias, w_out, w_out_gate, update, d_normed, tile):
    inner_n = inner_hat[...] * column(out_gain[...], 384) + column(out_bias[...], 384)
    proj = dot(w_out[...], inner_n.astype(BF16), (0, 0))
    sig = out_sig[...]
    store_tile((sig * proj).T, tile, update)
    d_gate_out = (upstream[...] * proj * sig * (1.0 - sig)).astype(BF16)
    d_normed[...] = dot(d_gate_out, w_out_gate[...], (0, 1))


def grad_kernel(d_inner, left, right, d_left, d_right, rows, matrix):
    rows[...] = d_inner[...].astype(F32)
    to_matrix(rows, 0, 4, matrix)
    packed = dot(matrix[...].astype(BF16), spread(), (1, 1)).astype(BF16)
    d_left[...] = dot(packed, right[...].reshape(384, 384), (1, 0)).astype(BF16)
    d_right[...] = dot(packed, left[...], (0, 0)).astype(BF16).reshape(4, 96, 384)


def merge_kernel(d_left, d_right, d_both, rows):
    one_hot = spread()
    to_rows(dot(d_left[...], one_hot, (1, 0)), rows, 0, 8)
    parts = [d_right[part].astype(F32) for part in range(4)]
    total = ((parts[0] + parts[1]) + (parts[2] + parts[3])).astype(BF16)
    to_rows(dot(total, one_hot, (1, 0)), rows, 3, 8)
    for spare in (6, 7):
        rows[pl.ds(spare, 128, stride=8), :] = jnp.zeros((128, 128), F32)
    d_both[...] = rows[...].astype(BF16)


def back_kernel(counts, d_both, values, gate, d_out, hat, inv, gain, w_values, w_gates, grad, rows, tile):
    rows[...] = d_both[...].astype(F32)
    parts = [
        jnp.concatenate([rows[pl.ds(3 * side + i_hi, 128, stride=8), :] for i_hi in range(3)], axis=1)
        for side in range(2)
    ]
    incoming = jnp.concatenate(parts, axis=0) * live_mask(counts)
    sig = gate[...]
    d_values = (incoming * sig).astype(BF16)
    d_gates = (incoming * values[...] * sig * (1.0 - sig)).astype(BF16)
    d_normed = d_out[...] + dot(d_values, w_values[...], (0, 1)) + dot(d_gates, w_gates[...], (0, 1))
    scaled = d_normed * gain[...].reshape(1, 128)
    pair_hat = hat[...]
    first_mean = jnp.mean(scaled, axis=1, keepdims=True)
    second_mean = jnp.mean(scaled * pair_hat, axis=1, keepdims=True)
    store_tile(inv[...] * (scaled - first_mean - pair_hat * second_mean), tile, grad)


def call(kernel, outs, args, scratch=(), scalars=0, flops=0):
    vmem, smem = pl.BlockSpec(memory_space=pltpu.VMEM), pl.BlockSpec(memory_space=pltpu.SMEM)
    outs = [jax.ShapeDtypeStruct(shape, dtype) for shape, dtype in outs]
    size = sum(a.size * a.dtype.itemsize for a in list(args) + outs)
    return pl.pallas_call(
        kernel,
        out_shape=outs,
        in_specs=[smem] * scalars + [vmem] * (len(args) - scalars),
        out_specs=[vmem] * len(outs),
        scratch_shapes=[pltpu.VMEM(shape, F32) for shape in scratch],
        compiler_params=pltpu.CompilerParams(vmem_limit_bytes=24 * 1024 * 1024),
        cost_estimate=pl.CostEstimate(flops=flops, bytes_accessed=size, transcendentals=0),
    )(*args)


def exchange(rows):
    return lax.all_to_all(rows.reshape(128, -1, 128), GROUP, 0, 0).reshape(rows.shape)


def shards(
    pair,
    cotangent,
    chain_counts,
    in_gain,
    in_bias,
    w_values,
    w_gates,
    w_out_gate,
    out_gain,
    out_bias,
    w_out,
):
    pair, cotangent = pair.transpose(1, 0, 2), cotangent.transpose(1, 0, 2)
    wide, tall, tokens, tile = (256, 384), (128, 384), (384, 128), (12, 24, 128)
    one, two = (512, 128), (1024, 128)
    both, values, gate, hat, inv, normed = call(
        front_kernel,
        [(two, BF16), (wide, F32), (wide, F32), (tokens, F32), (tokens, F32), (tokens, BF16)],
        [chain_counts, pair, in_gain, in_bias, w_values, w_gates],
        [two],
        scalars=1,
    )
    both = exchange(both)
    out_sig, upstream, scaled = call(
        gate_kernel, [(tall, F32)] * 3, [normed, cotangent, w_out_gate, w_out, out_gain]
    )
    left, right = call(split_kernel, [((96, 384), BF16), ((4, 96, 384), BF16)], [both], [two, (96, 512)])
    right = lax.all_to_all(right, "x", 0, 0)
    (inner,) = call(inner_kernel, [(one, BF16)], [left, right], [one])
    inner = exchange(inner)
    d_inner, inner_hat = call(norm_kernel, [(one, BF16), (tall, F32)], [inner, scaled], [one])
    d_inner = exchange(d_inner)
    update, d_out = call(
        update_kernel,
        [(tile, BF16), (tokens, F32)],
        [inner_hat, out_sig, upstream, out_gain, out_bias, w_out, w_out_gate],
        [tile],
    )
    d_left, d_right = call(
        grad_kernel, [((96, 384), BF16), ((4, 96, 384), BF16)], [d_inner, left, right], [one, (96, 512)]
    )
    d_right = lax.all_to_all(d_right, "x", 0, 0)
    (d_both,) = call(merge_kernel, [(two, BF16)], [d_left, d_right], [two])
    d_both = exchange(d_both)
    (grad,) = call(
        back_kernel,
        [(tile, BF16)],
        [chain_counts, d_both, values, gate, d_out, hat, inv, in_gain, w_values, w_gates],
        [two, tile],
        scalars=1,
    )
    return (update.transpose(1, 0, 2), grad.transpose(1, 0, 2))


def solution(mesh):
    fine = Mesh(mesh.devices.reshape(4, 4, 8, 2, 2), ROW + COL)
    placed = P(ROW, COL, None)
    return jax.shard_map(
        shards,
        mesh=fine,
        in_specs=(placed, placed) + (P(),) * 9,
        out_specs=(placed, placed),
        check_vma=False,
    )
```

time: 125 us -> 123 us (0.984)
  other arithmetic: 2.79 us -> 0 us
  Pallas kernels: 6.59 us -> 9.28 us
  local copies, waits for them, and re-layouts: 6.62 us -> 4.51 us
    all_to_all x4 -> x0, other arithmetic: 2.79 us -> none  [the longest x1 0.73 us: shards(): d_both = lax.all_to_all(d_both, GROUP, 0, 0)]
    pallas_call x9, Pallas kernels: 6.59 us -> 9.28 us  [call(): pl.pallas_call(kernel, out_shape=outs, in_specs=[smem] * scalars + [vmem]...]
    unnamed x36 -> x26, local copies, waits for them, and re-layouts: 6.1 us -> 4.51 us
    all_to_all x2, blocking collectives: 49.3 us -> 50.6 us  [exchange(): lax.all_to_all(rows.reshape(128, -1, 128), GROUP, 0, 0).reshape(rows.shape)]
  transfers between devices with their start and end apart: 2 -> 2, of which waited for: 2 -> 2; matrix products, arithmetic and copies ran while one was open for 1% -> 0% of each run, Pallas kernels for 1% -> 1%
where the time goes in v3:
time: 123 us; the launch traced here: 122 us
  blocking collectives  69.9 us (57%)
  waiting for transfers between devices  24.7 us (20%)
  starting transfers between devices  13.2 us (11%)
  Pallas kernels  9.28 us (8%)
  local copies, waits for them, and re-layouts  4.51 us (4%)
    all_to_all x2, blocking collectives, exchange(): lax.all_to_all(rows.reshape(128, -1, 128), GROUP, 0, 0).reshape(rows.shape)  50.6 us
    all_to_all x2, waiting for transfers between devices, exchange(): lax.all_to_all(rows.reshape(128, -1, 128), GROUP, 0, 0).reshape(rows.shape)  24.7 us
    all_to_all x2, starting transfers between devices, exchange(): lax.all_to_all(rows.reshape(128, -1, 128), GROUP, 0, 0).reshape(rows.shape)  13.2 us
    all_to_all x1, blocking collectives, shards(): right = lax.all_to_all(right, 'x', 0, 0)  10.3 us
    pallas_call x9, Pallas kernels, call(): pl.pallas_call(kernel, out_shape=outs, in_specs=[smem] * scalars + [vmem]...  9.28 us
    all_to_all x1, blocking collectives, shards(): d_right = lax.all_to_all(d_right, 'x', 0, 0)  9.01 us
    unnamed x26, local copies, waits for them, and re-layouts  4.51 us
  transfers between devices with their start and end apart: 2, of which 2 were waited for; matrix products, arithmetic and copies ran while one was open for 0% of the time, Pallas kernels for 1%

profile of v3, /device:TPU:1, one launch (start us, length us, event | category | flops | bytes accessed | tf_op | source)
XLA Modules:
  0.0 122.4 jit_solution(4200563484966689988)
XLA Ops:
  0.6 0.0 copy-start.10
  0.6 0.0 copy-start.9
  0.7 0.0 copy-start.11
  0.7 0.6 copy-done.10
  1.3 0.0 copy-done.9
  1.3 0.0 copy-done.11
  1.3 0.0 copy-start
  1.3 0.8 copy-done
  2.2 0.0 copy-start.2
  2.2 0.8 copy-done.2
  3.0 0.0 copy-start.6
  3.0 0.9 copy-done.6
  3.9 1.1 shard_map.122
  5.0 33.1 %all_to_all.30 = bf16[128,8,128]{2,1,0:T(8,128)(2,1)S(1)} all-to-all(bf16[128,8,128]{2,1,0:T(8,128)(2,1)S(1)} %bitcast.16), channel_id=1, replica_groups=mesh['x'=4,'z_lo'=4,'y'=8,'z_hi'=2,'core'=2] {'z_lo','y','z_hi','core'}, dimensions={0} | all-to-all | bytes 524288 | tf_op jit(solution)/shard_map/all_to_all | solution.py:223
  38.1 0.9 shard_map.123
  39.0 10.3 %all_to_all.31.right = bf16[4,96,384]{2,1,0:T(8,128)(2,1)S(1)} all-to-all(bf16[4,96,384]{2,1,0:T(8,128)(2,1)S(1)} %get-tuple-element.21), channel_id=1, replica_groups=mesh['x'=4,'z_lo'=4,'y'=8,'z_hi'=2,'core'=2] {'x'}, dimensions={0} | all-to-all | bytes 589824 | tf_op jit(solution)/shard_map/all_to_all | solution.py:254
  49.3 1.4 %shard_map.124 = bf16[512,128]{1,0:T(8,128)(2,1)} custom-call(bf16[96,384]{1,0:T(8,128)(2,1)S(1)} %get-tuple-element.20.left, bf16[4,96,384]{2,1,0:T(8,128)(2,1)S(1)} %all_to_all.31.right), custom_call_target="tpu_custom_call" | custom-call | bytes 499712 | tf_op jit(solution)/shard_map/pallas_call | solution.py:211
  50.7 0.0 copy-start.4
  50.7 0.0 copy-start.5
  50.7 0.0 copy-start.7
  50.7 6.8 %all-to-all-start.2 = ((bf16[128,4,128]{2,1,0:T(4,128)(2,1)}), bf16[128,4,128]{2,1,0:T(4,128)(2,1)S(1)}, u32[]{:S(2)}, u32[]{:S(2)}) async-start(bf16[128,4,128]{2,1,0:T(4,128)(2,1)} %bitcast.3), calls=%async_computation.2 | async-start | bytes 262144 | tf_op jit(solution)/shard_map/all_to_all | solution.py:223
  57.5 0.0 copy-start.8
  57.5 0.0 copy-done.4
  57.5 0.0 copy-done.5
  57.5 0.0 copy-done.7
  57.5 0.6 copy-done.8
  58.1 0.4 shard_map.125
  58.5 11.4 %all-to-all-done.2 = bf16[128,4,128]{2,1,0:T(4,128)(2,1)S(1)} async-done(((bf16[128,4,128]{2,1,0:T(4,128)(2,1)}), bf16[128,4,128]{2,1,0:T(4,128)(2,1)S(1)}, u32[]{:S(2)}, u32[]{:S(2)}) %all-to-all-start.2) | async-done | bytes 131104 | tf_op jit(solution)/shard_map/all_to_all | solution.py:223
  69.9 0.2 shard_map.126
  70.1 17.5 %all_to_all.32 = bf16[128,4,128]{2,1,0:T(4,128)(2,1)S(1)} all-to-all(bf16[128,4,128]{2,1,0:T(4,128)(2,1)S(1)} %bitcast.17), channel_id=1, replica_groups=mesh['x'=4,'z_lo'=4,'y'=8,'z_hi'=2,'core'=2] {'z_lo','y','z_hi','core'}, dimensions={0} | all-to-all | bytes 262144 | tf_op jit(solution)/shard_map/all_to_all | solution.py:223
  87.6 0.8 shard_map.128
  88.4 9.0 %all_to_all.33.d_right = bf16[4,96,384]{2,1,0:T(8,128)(2,1)S(1)} all-to-all(bf16[4,96,384]{2,1,0:T(8,128)(2,1)S(1)} %get-tuple-element.30), channel_id=1, replica_groups=mesh['x'=4,'z_lo'=4,'y'=8,'z_hi'=2,'core'=2] {'x'}, dimensions={0} | all-to-all | bytes 589824 | tf_op jit(solution)/shard_map/all_to_all | solution.py:268
  97.4 1.9 %shard_map.129 = bf16[1024,128]{1,0:T(8,128)(2,1)} custom-call(bf16[96,384]{1,0:T(8,128)(2,1)S(1)} %get-tuple-element.29.d_left, bf16[4,96,384]{2,1,0:T(8,128)(2,1)S(1)} %all_to_all.33.d_right), custom_call_target="tpu_custom_call" | custom-call | bytes 630784 | tf_op jit(solution)/shard_map/pallas_call | solution.py:211
  99.3 6.5 %all-to-all-start.5 = ((bf16[128,8,128]{2,1,0:T(8,128)(2,1)}), bf16[128,8,128]{2,1,0:T(8,128)(2,1)S(1)}, u32[]{:S(2)}, u32[]{:S(2)}) async-start(bf16[128,8,128]{2,1,0:T(8,128)(2,1)} %bitcast.9), calls=%async_computation.5 | async-start | bytes 524288 | tf_op jit(solution)/shard_map/all_to_all | solution.py:223
  105.8 0.0 copy-start.12
  105.8 0.6 copy-done.12
  106.4 0.0 copy-start.1
  106.4 0.0 copy-start.3
  106.4 1.0 shard_map.127
  107.5 13.3 %all-to-all-done.5 = bf16[128,8,128]{2,1,0:T(8,128)(2,1)S(1)} async-done(((bf16[128,8,128]{2,1,0:T(8,128)(2,1)}), bf16[128,8,128]{2,1,0:T(8,128)(2,1)S(1)}, u32[]{:S(2)}, u32[]{:S(2)}) %all-to-all-start.5) | async-done | bytes 262176 | tf_op jit(solution)/shard_map/all_to_all | solution.py:223
  120.8 0.0 copy-done.1
  120.8 0.0 copy-done.3
  120.8 1.6 %shard_map.130 = bf16[12,24,128]{2,1,0:T(8,128)(2,1)} custom-call(s32[4]{0:T(128)S(1)} %copy-done.9, bf16[1024,128]{1,0:T(8,128)(2,1)S(1)} %bitcast.12, f32[256,384]{1,0:T(8,128)S(1)} %get-tuple-element.31.values, f32[256,384]{1,0:T(8,128)S(1)} %get-tuple-element.32.gate, f32[384,128]{1,0:T(8,128)S(1)} %get-tuple-element.33.d_out, ...), custom_call_target="tpu_custom_call" | custom-call | bytes 1843728 | tf_op jit(solution)/shard_map/pallas_call | solution.py:211
Async XLA Ops:
  0.6 0.7 copy-start.10
  0.6 0.7 copy-start.9
  0.7 0.7 copy-start.11
  1.3 0.8 copy-start
  2.2 0.8 copy-start.2
  3.0 0.9 copy-start.6
  50.7 6.8 %copy-start.4 = (bf16[128,128]{1,0:T(8,128)(2,1)S(1)}, bf16[128,128]{1,0:T(8,128)(2,1)}, u32[]{:S(2)}) copy-start(bf16[128,128]{1,0:T(8,128)(2,1)} %w_out_gate.3) | copy-start | bytes 98308
  50.7 6.8 %copy-start.5 = (bf16[128,128]{1,0:T(8,128)(2,1)S(1)}, bf16[128,128]{1,0:T(8,128)(2,1)}, u32[]{:S(2)}) copy-start(bf16[128,128]{1,0:T(8,128)(2,1)} %w_out.3) | copy-start | bytes 98308
  50.7 6.8 %copy-start.7 = (bf16[24,12,128]{2,0,1:T(8,128)(2,1)S(1)}, bf16[24,12,128]{2,0,1:T(8,128)(2,1)}, u32[]{:S(2)}) copy-start(bf16[24,12,128]{2,0,1:T(8,128)(2,1)} %param.12) | copy-start | bytes 221188
  50.7 19.2 %all-to-all-start.2 = ((bf16[128,4,128]{2,1,0:T(4,128)(2,1)}), bf16[128,4,128]{2,1,0:T(4,128)(2,1)S(1)}, u32[]{:S(2)}, u32[]{:S(2)}) async-start(bf16[128,4,128]{2,1,0:T(4,128)(2,1)} %bitcast.3), calls=%async_computation.2 | async-start | bytes 262144 | tf_op jit(solution)/shard_map/all_to_all | solution.py:223
  57.5 0.7 copy-start.8
  99.3 21.5 %all-to-all-start.5 = ((bf16[128,8,128]{2,1,0:T(8,128)(2,1)}), bf16[128,8,128]{2,1,0:T(8,128)(2,1)S(1)}, u32[]{:S(2)}, u32[]{:S(2)}) async-start(bf16[128,8,128]{2,1,0:T(8,128)(2,1)} %bitcast.9), calls=%async_computation.5 | async-start | bytes 524288 | tf_op jit(solution)/shard_map/all_to_all | solution.py:223
  105.8 0.7 copy-start.12
  106.4 14.4 %copy-start.1 = (bf16[128,256]{1,0:T(8,128)(2,1)S(1)}, bf16[128,256]{1,0:T(8,128)(2,1)}, u32[]{:S(2)}) copy-start(bf16[128,256]{1,0:T(8,128)(2,1)} %w_values.3) | copy-start | bytes 196612
  106.4 14.4 %copy-start.3 = (bf16[128,256]{1,0:T(8,128)(2,1)S(1)}, bf16[128,256]{1,0:T(8,128)(2,1)}, u32[]{:S(2)}) copy-start(bf16[128,256]{1,0:T(8,128)(2,1)} %w_gates.3) | copy-start | bytes 196612

commit v4 on v3

--- a/solution.py
+++ b/solution.py
@@ -94,20 +94,30 @@
     return value[:, 128 * i_hi : 128 * (i_hi + 1)]
 
 
-def front_kernel(counts, pair, gain, bias, w_values, w_gates, both, values, gate, hat, inv, normed, rows):
-    x = load_tile(pair)
+def front_kernel(
+    counts, pair, gain, bias, w_values, w_gates, both, values, gate, hat, inv, normed,
+    rows, counts_s, pair_s, gain_s, bias_s, w_values_s, w_gates_s, sems,
+):
+    ends = ((pair, pair_s), (gain, gain_s), (bias, bias_s), (w_values, w_values_s), (w_gates, w_gates_s), (counts, counts_s))
+    copies = [pltpu.make_async_copy(src, dst, sems.at[n]) for n, (src, dst) in enumerate(ends)]
+    for copy in copies:
+        copy.start()
+    copies[0].wait()
+    x = load_tile(pair_s)
     centre = x - jnp.mean(x, axis=1, keepdims=True)
     inv_std = lax.rsqrt(jnp.mean(centre * centre, axis=1, keepdims=True) + EPS)
     pair_hat = centre * inv_std
-    normed_b = (pair_hat * gain[...].reshape(1, 128) + bias[...].reshape(1, 128)).astype(BF16)
+    for copy in copies[1:]:
+        copy.wait()
+    normed_b = (pair_hat * gain_s[...] + bias_s[...]).astype(BF16)
     hat[...] = pair_hat
     inv[...] = jnp.broadcast_to(inv_std, (384, 128))
     normed[...] = normed_b
-    vals = dot(w_values[...], normed_b, (0, 1))
-    sig = jax.nn.sigmoid(dot(w_gates[...], normed_b, (0, 1)))
+    vals = dot(w_values_s[...], normed_b, (0, 1))
+    sig = jax.nn.sigmoid(dot(w_gates_s[...], normed_b, (0, 1)))
     values[...] = vals
     gate[...] = sig
-    out = sig * vals * live_mask(counts)
+    out = sig * vals * live_mask(counts_s)
     for i_hi in range(3):
         rows[pl.ds(i_hi, 128, stride=8), :] = third(out[:128], i_hi)
         rows[pl.ds(3 + i_hi, 128, stride=8), :] = third(out[128:], i_hi)
@@ -116,13 +126,23 @@
     both[...] = rows[...].astype(BF16)
 
 
-def gate_kernel(normed, cotangent, w_out_gate, w_out, out_gain, out_sig, upstream, scaled):
+def gate_kernel(
+    counts, normed, cotangent, values, gate, hat, inv, w_out_gate, w_out, in_gain, out_gain,
+    out_sig, upstream, scaled, to_values, to_gates, hat_t, inv_t, gain_t,
+):
     sig = jax.nn.sigmoid(dot(w_out_gate[...], normed[...], (0, 1)))
     up = load_tile(cotangent).T
     d_proj = (up * sig).astype(BF16)
     out_sig[...] = sig
     upstream[...] = up
     scaled[...] = dot(w_out[...], d_proj, (1, 0)) * column(out_gain[...], 384)
+    live = live_mask(counts)
+    sig = gate[...]
+    to_values[...] = sig * live
+    to_gates[...] = values[...] * sig * (1.0 - sig) * live
+    hat_t[...] = hat[...].T
+    inv_t[...] = inv[...].T[:8]
+    gain_t[...] = column(in_gain[...], 128)
 
 
 def split_kernel(both, left, right, rows, matrix):
@@ -164,7 +184,7 @@
     sig = out_sig[...]
     store_tile((sig * proj).T, tile, update)
     d_gate_out = (upstream[...] * proj * sig * (1.0 - sig)).astype(BF16)
-    d_normed[...] = dot(d_gate_out, w_out_gate[...], (0, 1))
+    d_normed[...] = dot(w_out_gate[...], d_gate_out, (1, 0))
 
 
 def grad_kernel(d_inner, left, right, d_left, d_right, rows, matrix):
@@ -186,36 +206,49 @@
     d_both[...] = rows[...].astype(BF16)
 
 
-def back_kernel(counts, d_both, values, gate, d_out, hat, inv, gain, w_values, w_gates, grad, rows, tile):
+def back_kernel(d_both, to_values, to_gates, d_out, hat_t, inv_t, gain_t, w_values, w_gates, grad, rows, tile):
     rows[...] = d_both[...].astype(F32)
     parts = [
         jnp.concatenate([rows[pl.ds(3 * side + i_hi, 128, stride=8), :] for i_hi in range(3)], axis=1)
         for side in range(2)
     ]
-    incoming = jnp.concatenate(parts, axis=0) * live_mask(counts)
-    sig = gate[...]
-    d_values = (incoming * sig).astype(BF16)
-    d_gates = (incoming * values[...] * sig * (1.0 - sig)).astype(BF16)
-    d_normed = d_out[...] + dot(d_values, w_values[...], (0, 1)) + dot(d_gates, w_gates[...], (0, 1))
-    scaled = d_normed * gain[...].reshape(1, 128)
-    pair_hat = hat[...]
-    first_mean = jnp.mean(scaled, axis=1, keepdims=True)
-    second_mean = jnp.mean(scaled * pair_hat, axis=1, keepdims=True)
-    store_tile(inv[...] * (scaled - first_mean - pair_hat * second_mean), tile, grad)
-
-
-def call(kernel, outs, args, scratch=(), scalars=0, flops=0):
+    incoming = jnp.concatenate(parts, axis=0)
+    d_values = (incoming * to_values[...]).astype(BF16)
+    d_gates = (incoming * to_gates[...]).astype(BF16)
+    d_normed = d_out[...] + dot(w_values[...], d_values, (1, 0)) + dot(w_gates[...], d_gates, (1, 0))
+    scaled = d_normed * jnp.concatenate([gain_t[...]] * 3, axis=1)
+    pair_hat = hat_t[...]
+    first_mean = jnp.mean(scaled, axis=0, keepdims=True)
+    second_mean = jnp.mean(scaled * pair_hat, axis=0, keepdims=True)
+    store_tile((inv_t[:1] * (scaled - first_mean - pair_hat * second_mean)).T, tile, grad)
+
+
+def call(kernel, outs, args, scratch=(), scalars=0, flops=0, last=0):
     vmem, smem = pl.BlockSpec(memory_space=pltpu.VMEM), pl.BlockSpec(memory_space=pltpu.SMEM)
-    outs = [jax.ShapeDtypeStruct(shape, dtype) for shape, dtype in outs]
-    size = sum(a.size * a.dtype.itemsize for a in list(args) + outs)
+    size = sum(a.size * a.dtype.itemsize for a in args)
+    shapes = [jax.ShapeDtypeStruct(*out) if n < last else pltpu.VMEM(*out) for n, out in enumerate(outs)]
     return pl.pallas_call(
         kernel,
-        out_shape=outs,
+        out_shape=shapes,
         in_specs=[smem] * scalars + [vmem] * (len(args) - scalars),
         out_specs=[vmem] * len(outs),
         scratch_shapes=[pltpu.VMEM(shape, F32) for shape in scratch],
         compiler_params=pltpu.CompilerParams(vmem_limit_bytes=24 * 1024 * 1024),
         cost_estimate=pl.CostEstimate(flops=flops, bytes_accessed=size, transcendentals=0),
+    )(*args)
+
+
+def call_front(outs, args, rows):
+    args = [pltpu.with_memory_space_constraint(arg, pltpu.HBM) for arg in args]
+    spaces = [pltpu.SMEM] + [pltpu.VMEM] * 5
+    held = [space(arg.shape, arg.dtype) for space, arg in zip(spaces, args)]
+    return pl.pallas_call(
+        front_kernel,
+        out_shape=[pltpu.VMEM(*out) for out in outs],
+        in_specs=[pl.BlockSpec(memory_space=pltpu.HBM)] * 6,
+        out_specs=[pl.BlockSpec(memory_space=pltpu.VMEM)] * len(outs),
+        scratch_shapes=[pltpu.VMEM(rows, F32)] + held + [pltpu.SemaphoreType.DMA((6,))],
+        compiler_params=pltpu.CompilerParams(vmem_limit_bytes=24 * 1024 * 1024),
     )(*args)
 
 
@@ -239,16 +272,17 @@
     pair, cotangent = pair.transpose(1, 0, 2), cotangent.transpose(1, 0, 2)
     wide, tall, tokens, tile = (256, 384), (128, 384), (384, 128), (12, 24, 128)
     one, two = (512, 128), (1024, 128)
-    both, values, gate, hat, inv, normed = call(
-        front_kernel,
+    both, values, gate, hat, inv, normed = call_front(
         [(two, BF16), (wide, F32), (wide, F32), (tokens, F32), (tokens, F32), (tokens, BF16)],
-        [chain_counts, pair, in_gain, in_bias, w_values, w_gates],
-        [two],
+        [chain_counts, pair, in_gain.reshape(1, 128), in_bias.reshape(1, 128), w_values, w_gates],
+        two,
+    )
+    both = exchange(both)
+    out_sig, upstream, scaled, to_values, to_gates, hat_t, inv_t, gain_t = call(
+        gate_kernel,
+        [(tall, F32)] * 3 + [(wide, F32)] * 2 + [(tall, F32), ((8, 384), F32), ((128, 128), F32)],
+        [chain_counts, normed, cotangent, values, gate, hat, inv, w_out_gate, w_out, in_gain, out_gain],
         scalars=1,
-    )
-    both = exchange(both)
-    out_sig, upstream, scaled = call(
-        gate_kernel, [(tall, F32)] * 3, [normed, cotangent, w_out_gate, w_out, out_gain]
     )
     left, right = call(split_kernel, [((96, 384), BF16), ((4, 96, 384), BF16)], [both], [two, (96, 512)])
     right = lax.all_to_all(right, "x", 0, 0)
@@ -258,9 +292,10 @@
     d_inner = exchange(d_inner)
     update, d_out = call(
         update_kernel,
-        [(tile, BF16), (tokens, F32)],
+        [(tile, BF16), (tall, F32)],
         [inner_hat, out_sig, upstream, out_gain, out_bias, w_out, w_out_gate],
         [tile],
+        last=1,
     )
     d_left, d_right = call(
         grad_kernel, [((96, 384), BF16), ((4, 96, 384), BF16)], [d_inner, left, right], [one, (96, 512)]
@@ -271,9 +306,9 @@
     (grad,) = call(
         back_kernel,
         [(tile, BF16)],
-        [chain_counts, d_both, values, gate, d_out, hat, inv, in_gain, w_values, w_gates],
+        [d_both, to_values, to_gates, d_out, hat_t, inv_t, gain_t, w_values, w_gates],
         [two, tile],
-        scalars=1,
+        last=1,
     )
     return (update.transpose(1, 0, 2), grad.transpose(1, 0, 2))
 

time: 123 us -> 120 us (0.976)
  local copies, waits for them, and re-layouts: 4.51 us -> 1.91 us
    unnamed x26 -> x24, local copies, waits for them, and re-layouts: 4.51 us -> 1.91 us
  transfers between devices with their start and end apart: 2 -> 2, of which waited for: 2 -> 2; matrix products, arithmetic and copies ran while one was open for 0% -> 0% of each run, Pallas kernels for 1% -> 2%
where the time goes in v4:
time: 120 us; the launch traced here: 119 us
  blocking collectives  69.9 us (58%)
  waiting for transfers between devices  23.5 us (20%)
  starting transfers between devices  13.2 us (11%)
  Pallas kernels  9.74 us (8%)
  local copies, waits for them, and re-layouts  1.91 us (2%)
    all_to_all x2, blocking collectives, exchange(): lax.all_to_all(rows.reshape(128, -1, 128), GROUP, 0, 0).reshape(rows.shape)  50.6 us
    all_to_all x2, waiting for transfers between devices, exchange(): lax.all_to_all(rows.reshape(128, -1, 128), GROUP, 0, 0).reshape(rows.shape)  23.5 us
    all_to_all x2, starting transfers between devices, exchange(): lax.all_to_all(rows.reshape(128, -1, 128), GROUP, 0, 0).reshape(rows.shape)  13.2 us
    all_to_all x1, blocking collectives, shards(): right = lax.all_to_all(right, 'x', 0, 0)  10.3 us
    all_to_all x1, blocking collectives, shards(): d_right = lax.all_to_all(d_right, 'x', 0, 0)  8.99 us
    pallas_call x8, Pallas kernels, call(): pl.pallas_call(kernel, out_shape=shapes, in_specs=[smem] * scalars + [vme...  8.19 us
  transfers between devices with their start and end apart: 2, of which 2 were waited for; matrix products, arithmetic and copies ran while one was open for 0% of the time, Pallas kernels for 2%

profile of v4, /device:TPU:1, one launch (start us, length us, event | category | flops | bytes accessed | tf_op | source)
XLA Modules:
  0.0 119.1 jit_solution(4289685024256301037)
XLA Ops:
  0.6 1.6 %shard_map.122 = (bf16[1024,128]{1,0:T(8,128)(2,1)S(1)}, f32[256,384]{1,0:T(8,128)S(1)}, f32[256,384]{1,0:T(8,128)S(1)}, f32[384,128]{1,0:T(8,128)S(1)}, f32[384...) custom-call(s32[4]{0:T(128)} %counts.3, bf16[12,24,128]{2,1,0:T(8,128)(2,1)} %bitcast.22, f32[1,128]{1,0:T(1,128)} %bitcast.21, ...), custom_call_target="tpu_custom_call" | custom-call | tf_op jit(solution)/shard_map/pallas_call | solution.py:245
  2.2 33.1 %all_to_all.30 = bf16[128,8,128]{2,1,0:T(8,128)(2,1)S(1)} all-to-all(bf16[128,8,128]{2,1,0:T(8,128)(2,1)S(1)} %bitcast.18), channel_id=1, replica_groups=mesh['x'=4,'z_lo'=4,'y'=8,'z_hi'=2,'core'=2] {'z_lo','y','z_hi','core'}, dimensions={0} | all-to-all | bytes 524288 | tf_op jit(solution)/shard_map/all_to_all | solution.py:256
  35.3 0.9 shard_map.123
  36.2 10.3 %all_to_all.31.right = bf16[4,96,384]{2,1,0:T(8,128)(2,1)S(1)} all-to-all(bf16[4,96,384]{2,1,0:T(8,128)(2,1)S(1)} %get-tuple-element.26), channel_id=1, replica_groups=mesh['x'=4,'z_lo'=4,'y'=8,'z_hi'=2,'core'=2] {'x'}, dimensions={0} | all-to-all | bytes 589824 | tf_op jit(solution)/shard_map/all_to_all | solution.py:288
  46.5 1.4 %shard_map.124 = bf16[512,128]{1,0:T(8,128)(2,1)} custom-call(bf16[96,384]{1,0:T(8,128)(2,1)S(1)} %get-tuple-element.25.left, bf16[4,96,384]{2,1,0:T(8,128)(2,1)S(1)} %all_to_all.31.right), custom_call_target="tpu_custom_call" | custom-call | bytes 368640 | tf_op jit(solution)/shard_map/pallas_call | solution.py:230
  47.9 0.0 copy-start.2
  47.9 0.0 copy-start.3
  47.9 0.0 copy-start.4
  47.9 6.8 %all-to-all-start.2 = ((bf16[128,4,128]{2,1,0:T(4,128)(2,1)}), bf16[128,4,128]{2,1,0:T(4,128)(2,1)S(1)}, u32[]{:S(2)}, u32[]{:S(2)}) async-start(bf16[128,4,128]{2,1,0:T(4,128)(2,1)} %bitcast.5), calls=%async_computation.2 | async-start | bytes 262144 | tf_op jit(solution)/shard_map/all_to_all | solution.py:256
  54.7 0.0 copy-start.7
  54.7 0.0 copy-start.8
  54.7 0.0 copy-start.9
  54.7 0.0 copy-done.2
  54.7 0.0 copy-done.3
  54.7 0.0 copy-done.4
  54.8 0.6 copy-done.7
  55.3 0.0 copy-done.8
  55.4 0.0 copy-done.9
  55.4 1.0 shard_map.125
  56.4 0.0 copy-start.5
  56.4 0.6 copy-done.5
  57.0 10.1 %all-to-all-done.2 = bf16[128,4,128]{2,1,0:T(4,128)(2,1)S(1)} async-done(((bf16[128,4,128]{2,1,0:T(4,128)(2,1)}), bf16[128,4,128]{2,1,0:T(4,128)(2,1)S(1)}, u32[]{:S(2)}, u32[]{:S(2)}) %all-to-all-start.2) | async-done | bytes 131104 | tf_op jit(solution)/shard_map/all_to_all | solution.py:256
  67.1 0.2 shard_map.126
  67.3 17.5 %all_to_all.32 = bf16[128,4,128]{2,1,0:T(4,128)(2,1)S(1)} all-to-all(bf16[128,4,128]{2,1,0:T(4,128)(2,1)S(1)} %bitcast.19), channel_id=1, replica_groups=mesh['x'=4,'z_lo'=4,'y'=8,'z_hi'=2,'core'=2] {'z_lo','y','z_hi','core'}, dimensions={0} | all-to-all | bytes 262144 | tf_op jit(solution)/shard_map/all_to_all | solution.py:256
  84.8 0.8 shard_map.128
  85.6 9.0 %all_to_all.33.d_right = bf16[4,96,384]{2,1,0:T(8,128)(2,1)S(1)} all-to-all(bf16[4,96,384]{2,1,0:T(8,128)(2,1)S(1)} %get-tuple-element.39), channel_id=1, replica_groups=mesh['x'=4,'z_lo'=4,'y'=8,'z_hi'=2,'core'=2] {'x'}, dimensions={0} | all-to-all | bytes 589824 | tf_op jit(solution)/shard_map/all_to_all | solution.py:303
  94.6 1.9 %shard_map.129 = bf16[1024,128]{1,0:T(8,128)(2,1)} custom-call(bf16[96,384]{1,0:T(8,128)(2,1)S(1)} %get-tuple-element.38.d_left, bf16[4,96,384]{2,1,0:T(8,128)(2,1)S(1)} %all_to_all.33.d_right), custom_call_target="tpu_custom_call" | custom-call | bytes 368640 | tf_op jit(solution)/shard_map/pallas_call | solution.py:230
  96.5 6.5 %all-to-all-start.5 = ((bf16[128,8,128]{2,1,0:T(8,128)(2,1)}), bf16[128,8,128]{2,1,0:T(8,128)(2,1)S(1)}, u32[]{:S(2)}, u32[]{:S(2)}) async-start(bf16[128,8,128]{2,1,0:T(8,128)(2,1)} %bitcast.11), calls=%async_computation.5 | async-start | bytes 524288 | tf_op jit(solution)/shard_map/all_to_all | solution.py:256
  103.0 0.0 copy-start.10
  103.0 0.0 copy-start.11
  103.0 0.6 copy-done.10
  103.6 0.0 copy-done.11
  103.7 0.0 copy-start
  103.7 0.0 copy-start.1
  103.7 1.0 shard_map.127
  104.6 0.0 copy-start.6
  104.6 13.4 %all-to-all-done.5 = bf16[128,8,128]{2,1,0:T(8,128)(2,1)S(1)} async-done(((bf16[128,8,128]{2,1,0:T(8,128)(2,1)}), bf16[128,8,128]{2,1,0:T(8,128)(2,1)S(1)}, u32[]{:S(2)}, u32[]{:S(2)}) %all-to-all-start.5) | async-done | bytes 262176 | tf_op jit(solution)/shard_map/all_to_all | solution.py:256
  118.0 0.0 copy-done
  118.0 0.0 copy-done.1
  118.0 0.0 copy-done.6
  118.0 1.1 shard_map.130
Async XLA Ops:
  47.9 6.8 %copy-start.2 = (bf16[128,128]{1,0:T(8,128)(2,1)S(1)}, bf16[128,128]{1,0:T(8,128)(2,1)}, u32[]{:S(2)}) copy-start(bf16[128,128]{1,0:T(8,128)(2,1)} %w_out_gate.3) | copy-start | bytes 98308
  47.9 6.8 %copy-start.3 = (bf16[128,128]{1,0:T(8,128)(2,1)S(1)}, bf16[128,128]{1,0:T(8,128)(2,1)}, u32[]{:S(2)}) copy-start(bf16[128,128]{1,0:T(8,128)(2,1)} %w_out.3) | copy-start | bytes 98308
  47.9 6.8 %copy-start.4 = (bf16[24,12,128]{2,0,1:T(8,128)(2,1)S(1)}, bf16[24,12,128]{2,0,1:T(8,128)(2,1)}, u32[]{:S(2)}) copy-start(bf16[24,12,128]{2,0,1:T(8,128)(2,1)} %param.12) | copy-start | bytes 221188
  47.9 19.2 %all-to-all-start.2 = ((bf16[128,4,128]{2,1,0:T(4,128)(2,1)}), bf16[128,4,128]{2,1,0:T(4,128)(2,1)S(1)}, u32[]{:S(2)}, u32[]{:S(2)}) async-start(bf16[128,4,128]{2,1,0:T(4,128)(2,1)} %bitcast.5), calls=%async_computation.2 | async-start | bytes 262144 | tf_op jit(solution)/shard_map/all_to_all | solution.py:256
  54.7 0.7 copy-start.7
  54.7 0.7 copy-start.8
  54.7 0.7 copy-start.9
  56.4 0.6 copy-start.5
  96.5 21.5 %all-to-all-start.5 = ((bf16[128,8,128]{2,1,0:T(8,128)(2,1)}), bf16[128,8,128]{2,1,0:T(8,128)(2,1)S(1)}, u32[]{:S(2)}, u32[]{:S(2)}) async-start(bf16[128,8,128]{2,1,0:T(8,128)(2,1)} %bitcast.11), calls=%async_computation.5 | async-start | bytes 524288 | tf_op jit(solution)/shard_map/all_to_all | solution.py:256
  103.0 0.7 copy-start.10
  103.0 0.7 copy-start.11
  103.7 14.3 %copy-start = (bf16[128,256]{1,0:T(8,128)(2,1)S(1)}, bf16[128,256]{1,0:T(8,128)(2,1)}, u32[]{:S(2)}) copy-start(bf16[128,256]{1,0:T(8,128)(2,1)} %w_values.3) | copy-start | bytes 196612
  103.7 14.3 %copy-start.1 = (bf16[128,256]{1,0:T(8,128)(2,1)S(1)}, bf16[128,256]{1,0:T(8,128)(2,1)}, u32[]{:S(2)}) copy-start(bf16[128,256]{1,0:T(8,128)(2,1)} %w_gates.3) | copy-start | bytes 196612
  104.6 13.4 %copy-start.6 = (f32[8,384]{1,0:T(8,128)S(1)}, f32[8,384]{1,0:T(8,128)}, u32[]{:S(2)}) copy-start(f32[8,384]{1,0:T(8,128)} %copy-done.5) | copy-start | bytes 36868

commit v5 on v4

--- a/solution.py
+++ b/solution.py
@@ -119,10 +119,8 @@
     gate[...] = sig
     out = sig * vals * live_mask(counts_s)
     for i_hi in range(3):
-        rows[pl.ds(i_hi, 128, stride=8), :] = third(out[:128], i_hi)
-        rows[pl.ds(3 + i_hi, 128, stride=8), :] = third(out[128:], i_hi)
-    for spare in (6, 7):
-        rows[pl.ds(spare, 128, stride=8), :] = jnp.zeros((128, 128), F32)
+        rows[pl.ds(i_hi, 128, stride=6), :] = third(out[:128], i_hi)
+        rows[pl.ds(3 + i_hi, 128, stride=6), :] = third(out[128:], i_hi)
     both[...] = rows[...].astype(BF16)
 
 
@@ -148,9 +146,9 @@
 def split_kernel(both, left, right, rows, matrix):
     rows[...] = both[...].astype(F32)
     one_hot = spread()
-    to_matrix(rows, 0, 8, matrix)
+    to_matrix(rows, 0, 6, matrix)
     left[...] = dot(matrix[...].astype(BF16), one_hot, (1, 1)).astype(BF16)
-    to_matrix(rows, 3, 8, matrix)
+    to_matrix(rows, 3, 6, matrix)
     packed = dot(matrix[...].astype(BF16), one_hot, (1, 1)).astype(BF16)
     for part in range(4):
         right[part] = packed
@@ -197,19 +195,17 @@
 
 def merge_kernel(d_left, d_right, d_both, rows):
     one_hot = spread()
-    to_rows(dot(d_left[...], one_hot, (1, 0)), rows, 0, 8)
+    to_rows(dot(d_left[...], one_hot, (1, 0)), rows, 0, 6)
     parts = [d_right[part].astype(F32) for part in range(4)]
     total = ((parts[0] + parts[1]) + (parts[2] + parts[3])).astype(BF16)
-    to_rows(dot(total, one_hot, (1, 0)), rows, 3, 8)
-    for spare in (6, 7):
-        rows[pl.ds(spare, 128, stride=8), :] = jnp.zeros((128, 128), F32)
+    to_rows(dot(total, one_hot, (1, 0)), rows, 3, 6)
     d_both[...] = rows[...].astype(BF16)
 
 
 def back_kernel(d_both, to_values, to_gates, d_out, hat_t, inv_t, gain_t, w_values, w_gates, grad, rows, tile):
     rows[...] = d_both[...].astype(F32)
     parts = [
-        jnp.concatenate([rows[pl.ds(3 * side + i_hi, 128, stride=8), :] for i_hi in range(3)], axis=1)
+        jnp.concatenate([rows[pl.ds(3 * side + i_hi, 128, stride=6), :] for i_hi in range(3)], axis=1)
         for side in range(2)
     ]
     incoming = jnp.concatenate(parts, axis=0)
@@ -253,7 +249,7 @@
 
 
 def exchange(rows):
-    return lax.all_to_all(rows.reshape(128, -1, 128), GROUP, 0, 0).reshape(rows.shape)
+    return lax.all_to_all(rows.reshape(128, -1, 2, 128), GROUP, 0, 0).reshape(rows.shape)
 
 
 def shards(
@@ -271,7 +267,7 @@
 ):
     pair, cotangent = pair.transpose(1, 0, 2), cotangent.transpose(1, 0, 2)
     wide, tall, tokens, tile = (256, 384), (128, 384), (384, 128), (12, 24, 128)
-    one, two = (512, 128), (1024, 128)
+    one, two = (512, 128), (768, 128)
     both, values, gate, hat, inv, normed = call_front(
         [(two, BF16), (wide, F32), (wide, F32), (tokens, F32), (tokens, F32), (tokens, BF16)],
         [chain_counts, pair, in_gain.reshape(1, 128), in_bias.reshape(1, 128), w_values, w_gates],

time: 120 us -> 117 us (0.975)
  blocking collectives: 69.9 us -> 68.6 us
  waiting for transfers between devices: 23.5 us -> 22.2 us
    all_to_all x2, waiting for transfers between devices: 23.5 us -> 22.2 us  [exchange(): lax.all_to_all(rows.reshape(128, -1, 2, 128), GROUP, 0, 0)]
    all_to_all x2, blocking collectives: 50.6 us -> 49.4 us  [exchange(): lax.all_to_all(rows.reshape(128, -1, 2, 128), GROUP, 0, 0)]
where the time goes in v5:
time: 117 us; the launch traced here: 116 us
  blocking collectives  68.6 us (59%)
  waiting for transfers between devices  22.2 us (19%)
  starting transfers between devices  13.3 us (11%)
  Pallas kernels  9.6 us (8%)
  local copies, waits for them, and re-layouts  1.91 us (2%)
    all_to_all x2, blocking collectives, exchange(): lax.all_to_all(rows.reshape(128, -1, 2, 128), GROUP, 0, 0)  49.4 us
    all_to_all x2, waiting for transfers between devices, exchange(): lax.all_to_all(rows.reshape(128, -1, 2, 128), GROUP, 0, 0)  22.2 us
    all_to_all x2, starting transfers between devices, exchange(): lax.all_to_all(rows.reshape(128, -1, 2, 128), GROUP, 0, 0)  13.3 us
    all_to_all x1, blocking collectives, shards(): right = lax.all_to_all(right, 'x', 0, 0)  10.2 us
    all_to_all x1, blocking collectives, shards(): d_right = lax.all_to_all(d_right, 'x', 0, 0)  9 us
    pallas_call x8, Pallas kernels, call(): pl.pallas_call(kernel, out_shape=shapes, in_specs=[smem] * scalars + [vme...  8.1 us
  transfers between devices with their start and end apart: 2, of which 2 were waited for; matrix products, arithmetic and copies ran while one was open for 0% of the time, Pallas kernels for 2%

profile of v5, /device:TPU:1, one launch (start us, length us, event | category | flops | bytes accessed | tf_op | source)
XLA Modules:
  0.0 116.4 jit_solution(10496697144652131099)
XLA Ops:
  0.6 1.5 %shard_map.122 = (bf16[768,128]{1,0:T(8,128)(2,1)S(1)}, f32[256,384]{1,0:T(8,128)S(1)}, f32[256,384]{1,0:T(8,128)S(1)}, f32[384,128]{1,0:T(8,128)S(1)}, f32[384,...) custom-call(s32[4]{0:T(128)} %counts.3, bf16[12,24,128]{2,1,0:T(8,128)(2,1)} %bitcast.23, f32[1,128]{1,0:T(1,128)} %bitcast.21, ...), custom_call_target="tpu_custom_call" | custom-call | tf_op jit(solution)/shard_map/pallas_call | solution.py:241
  2.1 31.8 %all_to_all.30 = bf16[128,3,2,128]{3,2,1,0:T(2,128)(2,1)S(1)} all-to-all(bf16[128,3,2,128]{3,2,1,0:T(2,128)(2,1)S(1)} %bitcast.18), channel_id=1, replica_groups=mesh['x'=4,'z_lo'=4,'y'=8,'z_hi'=2,'core'=2] {'z_lo','y','z_hi','core'}, dimensions={0} | all-to-all | bytes 393216 | tf_op jit(solution)/shard_map/all_to_all | solution.py:252
  34.0 0.9 shard_map.123
  34.9 10.2 %all_to_all.31.right = bf16[4,96,384]{2,1,0:T(8,128)(2,1)S(1)} all-to-all(bf16[4,96,384]{2,1,0:T(8,128)(2,1)S(1)} %get-tuple-element.26), channel_id=1, replica_groups=mesh['x'=4,'z_lo'=4,'y'=8,'z_hi'=2,'core'=2] {'x'}, dimensions={0} | all-to-all | bytes 589824 | tf_op jit(solution)/shard_map/all_to_all | solution.py:284
  45.1 1.4 %shard_map.124 = bf16[512,128]{1,0:T(8,128)(2,1)} custom-call(bf16[96,384]{1,0:T(8,128)(2,1)S(1)} %get-tuple-element.25.left, bf16[4,96,384]{2,1,0:T(8,128)(2,1)S(1)} %all_to_all.31.right), custom_call_target="tpu_custom_call" | custom-call | bytes 368640 | tf_op jit(solution)/shard_map/pallas_call | solution.py:226
  46.6 0.0 copy-start.2
  46.6 0.0 copy-start.3
  46.6 0.0 copy-start.4
  46.6 6.8 %all-to-all-start.2 = ((bf16[128,2,2,128]{3,2,1,0:T(2,128)(2,1)}), bf16[128,2,2,128]{3,2,1,0:T(2,128)(2,1)S(1)}, u32[]{:S(2)}, u32[]{:S(2)}) async-start(bf16[128,2,2,128]{3,2,1,0:T(2,128)(2,1)} %bitcast.5), calls=%async_computation.2 | async-start | bytes 262144 | tf_op jit(solution)/shard_map/all_to_all | solution.py:252
  53.4 0.0 copy-start.7
  53.4 0.0 copy-start.8
  53.4 0.0 copy-start.9
  53.4 0.0 copy-done.2
  53.4 0.0 copy-done.3
  53.4 0.0 copy-done.4
  53.4 0.6 copy-done.7
  54.0 0.0 copy-done.8
  54.0 0.0 copy-done.9
  54.1 1.0 shard_map.125
  55.1 0.0 copy-start.5
  55.1 0.6 copy-done.5
  55.7 10.1 %all-to-all-done.2 = bf16[128,2,2,128]{3,2,1,0:T(2,128)(2,1)S(1)} async-done(((bf16[128,2,2,128]{3,2,1,0:T(2,128)(2,1)}), bf16[128,2,2,128]{3,2,1,0:T(2,128)(2,1)S(1)}, u32[]{:S(2)}, u32[]{:S(2)}) %all-to-all-start.2) | async-done | bytes 131104 | tf_op jit(solution)/shard_map/all_to_all | solution.py:252
  65.8 0.2 shard_map.126
  65.9 17.5 %all_to_all.32 = bf16[128,2,2,128]{3,2,1,0:T(2,128)(2,1)S(1)} all-to-all(bf16[128,2,2,128]{3,2,1,0:T(2,128)(2,1)S(1)} %bitcast.19), channel_id=1, replica_groups=mesh['x'=4,'z_lo'=4,'y'=8,'z_hi'=2,'core'=2] {'z_lo','y','z_hi','core'}, dimensions={0} | all-to-all | bytes 262144 | tf_op jit(solution)/shard_map/all_to_all | solution.py:252
  83.5 0.8 shard_map.128
  84.3 9.0 %all_to_all.33.d_right = bf16[4,96,384]{2,1,0:T(8,128)(2,1)S(1)} all-to-all(bf16[4,96,384]{2,1,0:T(8,128)(2,1)S(1)} %get-tuple-element.39), channel_id=1, replica_groups=mesh['x'=4,'z_lo'=4,'y'=8,'z_hi'=2,'core'=2] {'x'}, dimensions={0} | all-to-all | bytes 589824 | tf_op jit(solution)/shard_map/all_to_all | solution.py:299
  93.3 1.9 %shard_map.129 = bf16[768,128]{1,0:T(8,128)(2,1)} custom-call(bf16[96,384]{1,0:T(8,128)(2,1)S(1)} %get-tuple-element.38.d_left, bf16[4,96,384]{2,1,0:T(8,128)(2,1)S(1)} %all_to_all.33.d_right), custom_call_target="tpu_custom_call" | custom-call | bytes 368640 | tf_op jit(solution)/shard_map/pallas_call | solution.py:226
  95.1 6.5 %all-to-all-start.5 = ((bf16[128,3,2,128]{3,2,1,0:T(2,128)(2,1)}), bf16[128,3,2,128]{3,2,1,0:T(2,128)(2,1)S(1)}, u32[]{:S(2)}, u32[]{:S(2)}) async-start(bf16[128,3,2,128]{3,2,1,0:T(2,128)(2,1)} %bitcast.11), calls=%async_computation.5 | async-start | bytes 393216 | tf_op jit(solution)/shard_map/all_to_all | solution.py:252
  101.6 0.0 copy-start.10
  101.6 0.0 copy-start.11
  101.6 0.6 copy-done.10
  102.3 0.0 copy-done.11
  102.3 0.0 copy-start
  102.3 0.0 copy-start.1
  102.3 1.0 shard_map.127
  103.2 0.0 copy-start.6
  103.2 12.1 %all-to-all-done.5 = bf16[128,3,2,128]{3,2,1,0:T(2,128)(2,1)S(1)} async-done(((bf16[128,3,2,128]{3,2,1,0:T(2,128)(2,1)}), bf16[128,3,2,128]{3,2,1,0:T(2,128)(2,1)S(1)}, u32[]{:S(2)}, u32[]{:S(2)}) %all-to-all-start.5) | async-done | bytes 196640 | tf_op jit(solution)/shard_map/all_to_all | solution.py:252
  115.3 0.0 copy-done
  115.3 0.0 copy-done.1
  115.3 0.0 copy-done.6
  115.3 1.0 shard_map.130
Async XLA Ops:
  46.6 6.8 %copy-start.2 = (bf16[128,128]{1,0:T(8,128)(2,1)S(1)}, bf16[128,128]{1,0:T(8,128)(2,1)}, u32[]{:S(2)}) copy-start(bf16[128,128]{1,0:T(8,128)(2,1)} %w_out_gate.3) | copy-start | bytes 98308
  46.6 6.9 %copy-start.3 = (bf16[128,128]{1,0:T(8,128)(2,1)S(1)}, bf16[128,128]{1,0:T(8,128)(2,1)}, u32[]{:S(2)}) copy-start(bf16[128,128]{1,0:T(8,128)(2,1)} %w_out.3) | copy-start | bytes 98308
  46.6 6.9 %copy-start.4 = (bf16[24,12,128]{2,0,1:T(8,128)(2,1)S(1)}, bf16[24,12,128]{2,0,1:T(8,128)(2,1)}, u32[]{:S(2)}) copy-start(bf16[24,12,128]{2,0,1:T(8,128)(2,1)} %param.12) | copy-start | bytes 221188
  46.6 19.2 %all-to-all-start.2 = ((bf16[128,2,2,128]{3,2,1,0:T(2,128)(2,1)}), bf16[128,2,2,128]{3,2,1,0:T(2,128)(2,1)S(1)}, u32[]{:S(2)}, u32[]{:S(2)}) async-start(bf16[128,2,2,128]{3,2,1,0:T(2,128)(2,1)} %bitcast.5), calls=%async_computation.2 | async-start | bytes 262144 | tf_op jit(solution)/shard_map/all_to_all | solution.py:252
  53.4 0.7 copy-start.7
  53.4 0.7 copy-start.8
  53.4 0.7 copy-start.9
  55.1 0.6 copy-start.5
  95.1 20.2 %all-to-all-start.5 = ((bf16[128,3,2,128]{3,2,1,0:T(2,128)(2,1)}), bf16[128,3,2,128]{3,2,1,0:T(2,128)(2,1)S(1)}, u32[]{:S(2)}, u32[]{:S(2)}) async-start(bf16[128,3,2,128]{3,2,1,0:T(2,128)(2,1)} %bitcast.11), calls=%async_computation.5 | async-start | bytes 393216 | tf_op jit(solution)/shard_map/all_to_all | solution.py:252
  101.6 0.7 copy-start.10
  101.6 0.7 copy-start.11
  102.3 13.1 %copy-start = (bf16[128,256]{1,0:T(8,128)(2,1)S(1)}, bf16[128,256]{1,0:T(8,128)(2,1)}, u32[]{:S(2)}) copy-start(bf16[128,256]{1,0:T(8,128)(2,1)} %w_values.3) | copy-start | bytes 196612
  102.3 13.1 %copy-start.1 = (bf16[128,256]{1,0:T(8,128)(2,1)S(1)}, bf16[128,256]{1,0:T(8,128)(2,1)}, u32[]{:S(2)}) copy-start(bf16[128,256]{1,0:T(8,128)(2,1)} %w_gates.3) | copy-start | bytes 196612
  103.2 12.1 %copy-start.6 = (f32[8,384]{1,0:T(8,128)S(1)}, f32[8,384]{1,0:T(8,128)}, u32[]{:S(2)}) copy-start(f32[8,384]{1,0:T(8,128)} %copy-done.5) | copy-start | bytes 36868

commit v6 on v5

--- a/solution.py
+++ b/solution.py
@@ -20,43 +20,45 @@
     return lax.dot_general(a, b, ((contract[:1], contract[1:]), ((), ())), preferred_element_type=F32)
 
 
-def swap_groups(x):
-    sub = lax.broadcasted_iota(jnp.int32, x.shape, 1)
-    lane = lax.broadcasted_iota(jnp.int32, x.shape, 2)
-    for step in (4, 2, 1):
-        up = pltpu.roll(pltpu.roll(x, LOW - step, 1), step, 2)
-        down = pltpu.roll(pltpu.roll(x, step, 1), 128 - step, 2)
-        sub_bit, lane_bit = (sub & step) != 0, (lane & step) != 0
-        x = jnp.where(sub_bit == lane_bit, x, jnp.where(lane_bit, up, down))
-    return x
-
-
-def to_matrix(rows, first, per, out):
-    for i_hi in range(3):
-        part = rows[pl.ds(first + i_hi, 128, stride=per), :].reshape(16, LOW, 128)
-        part = swap_groups(part)
-        for z in range(4):
-            for c_hi in range(4):
-                row = 24 * z + LOW * i_hi
-                out[row : row + LOW, 128 * c_hi : 128 * (c_hi + 1)] = part[4 * z + c_hi]
+def swap_quads(quad):
+    lane = lax.broadcasted_iota(jnp.int32, (LOW, 128), 1)
+    quad = list(quad)
+    for step in (2, 1):
+        low = (lane & (32 * step)) == 0
+        for a in range(4):
+            if a & step == 0:
+                one, two = quad[a], quad[a + step]
+                quad[a] = jnp.where(low, one, pltpu.roll(two, 32 * step, 1))
+                quad[a + step] = jnp.where(low, pltpu.roll(one, 128 - 32 * step, 1), two)
+    return quad
+
+
+def to_matrix(rows, first, per):
+    bands = {}
+    for i_hi in range(3):
+        turned = rows[pl.ds(first + i_hi, 128, stride=per), :].T
+        for j_hi in range(3):
+            parts = [turned[LOW * (4 * j_hi + j_lo) : LOW * (4 * j_hi + j_lo + 1)] for j_lo in range(4)]
+            for z, part in enumerate(swap_quads(parts)):
+                bands[z, i_hi, j_hi] = part
+    return jnp.concatenate(
+        [
+            jnp.concatenate([bands[z, i_hi, j_hi] for j_hi in range(3)], axis=1)
+            for z in range(4)
+            for i_hi in range(3)
+        ],
+        axis=0,
+    )
 
 
 def to_rows(matrix, rows, first, per):
     for i_hi in range(3):
         parts = []
-        for z in range(4):
-            row = 24 * z + LOW * i_hi
-            parts += [matrix[row : row + LOW, 128 * c : 128 * (c + 1)] for c in range(4)]
-        rows[pl.ds(first + i_hi, 128, stride=per), :] = swap_groups(jnp.stack(parts)).reshape(128, 128)
-
-
-def spread():
-    lane = lax.broadcasted_iota(jnp.int32, (1, 512), 1)
-    slot = lane % 128 // LOW
-    token = (lane // 128 * LOW + lane % LOW) * 12 + slot
-    token = jnp.where(slot < 12, token, -1)
-    hit = lax.broadcasted_iota(jnp.int32, (384, 512), 0) == token
-    return jnp.where(hit, 1.0, 0.0).astype(BF16)
+        for j_hi in range(3):
+            bands = [24 * z + LOW * i_hi for z in range(4)]
+            parts += swap_quads([matrix[band : band + LOW, 128 * j_hi : 128 * (j_hi + 1)] for band in bands])
+        parts += [jnp.zeros(((SLOTS - 12) * LOW, 128), F32)]
+        rows[pl.ds(first + i_hi, 128, stride=per), :] = jnp.concatenate(parts, axis=0).T
 
 
 def live_mask(counts):
@@ -143,20 +145,25 @@
     gain_t[...] = column(in_gain[...], 128)
 
 
-def split_kernel(both, left, right, rows, matrix):
+def split_kernel(both, left, right, rows, natural):
     rows[...] = both[...].astype(F32)
-    one_hot = spread()
-    to_matrix(rows, 0, 6, matrix)
-    left[...] = dot(matrix[...].astype(BF16), one_hot, (1, 1)).astype(BF16)
-    to_matrix(rows, 3, 6, matrix)
-    packed = dot(matrix[...].astype(BF16), one_hot, (1, 1)).astype(BF16)
+    matrix = to_matrix(rows, 3, 6)
+    packed = []
+    for t in range(3):
+        natural[t] = third(matrix, t)
+        packed += [jnp.concatenate([natural[t, pl.ds(slot, LOW, stride=12), :] for slot in range(12)], axis=0)]
+    packed = jnp.concatenate(packed, axis=1).astype(BF16)
     for part in range(4):
         right[part] = packed
-
-
-def inner_kernel(left, right, inner, rows):
-    product = dot(left[...], right[...].reshape(384, 384), (1, 1)).astype(BF16)
-    to_rows(dot(product, spread(), (1, 0)), rows, 0, 4)
+    left[...] = to_matrix(rows, 0, 6).astype(BF16)
+
+
+def inner_kernel(left, right, inner, right_all, rows):
+    parts = [right[part].astype(F32) for part in range(4)]
+    ordered = [parts[part][LOW * slot : LOW * (slot + 1)] for slot in range(12) for part in range(4)]
+    ordered = jnp.concatenate(ordered, axis=0).astype(BF16)
+    right_all[...] = ordered
+    to_rows(dot(left[...], ordered, (1, 1)), rows, 0, 4)
     rows[pl.ds(3, 128, stride=4), :] = jnp.zeros((128, 128), F32)
     inner[...] = rows[...].astype(BF16)
 
@@ -185,20 +192,24 @@
     d_normed[...] = dot(w_out_gate[...], d_gate_out, (1, 0))
 
 
-def grad_kernel(d_inner, left, right, d_left, d_right, rows, matrix):
+def grad_kernel(d_inner, left, right_all, d_left, d_right, rows):
     rows[...] = d_inner[...].astype(F32)
-    to_matrix(rows, 0, 4, matrix)
-    packed = dot(matrix[...].astype(BF16), spread(), (1, 1)).astype(BF16)
-    d_left[...] = dot(packed, right[...].reshape(384, 384), (1, 0)).astype(BF16)
-    d_right[...] = dot(packed, left[...], (0, 0)).astype(BF16).reshape(4, 96, 384)
-
-
-def merge_kernel(d_left, d_right, d_both, rows):
-    one_hot = spread()
-    to_rows(dot(d_left[...], one_hot, (1, 0)), rows, 0, 6)
+    packed = to_matrix(rows, 0, 4).astype(BF16)
+    sums = dot(packed, left[...], (0, 0))
+    for part in range(4):
+        bands = [32 * slot + LOW * part for slot in range(12)]
+        d_right[part] = jnp.concatenate([sums[band : band + LOW] for band in bands], axis=0).astype(BF16)
+    d_left[...] = dot(packed, right_all[...], (1, 0))
+
+
+def merge_kernel(d_left, d_right, d_both, rows, natural):
+    to_rows(d_left[...], rows, 0, 6)
     parts = [d_right[part].astype(F32) for part in range(4)]
-    total = ((parts[0] + parts[1]) + (parts[2] + parts[3])).astype(BF16)
-    to_rows(dot(total, one_hot, (1, 0)), rows, 3, 6)
+    total = (parts[0] + parts[1]) + (parts[2] + parts[3])
+    for t in range(3):
+        for slot in range(12):
+            natural[t, pl.ds(slot, LOW, stride=12), :] = third(total, t)[LOW * slot : LOW * (slot + 1)]
+    to_rows(jnp.concatenate([natural[t] for t in range(3)], axis=1), rows, 3, 6)
     d_both[...] = rows[...].astype(BF16)
 
 
@@ -280,9 +291,9 @@
         [chain_counts, normed, cotangent, values, gate, hat, inv, w_out_gate, w_out, in_gain, out_gain],
         scalars=1,
     )
-    left, right = call(split_kernel, [((96, 384), BF16), ((4, 96, 384), BF16)], [both], [two, (96, 512)])
+    left, right = call(split_kernel, [((96, 384), BF16), ((4, 96, 384), BF16)], [both], [two, (3, 96, 128)])
     right = lax.all_to_all(right, "x", 0, 0)
-    (inner,) = call(inner_kernel, [(one, BF16)], [left, right], [one])
+    inner, right = call(inner_kernel, [(one, BF16), ((384, 384), BF16)], [left, right], [one])
     inner = exchange(inner)
     d_inner, inner_hat = call(norm_kernel, [(one, BF16), (tall, F32)], [inner, scaled], [one])
     d_inner = exchange(d_inner)
@@ -294,10 +305,10 @@
         last=1,
     )
     d_left, d_right = call(
-        grad_kernel, [((96, 384), BF16), ((4, 96, 384), BF16)], [d_inner, left, right], [one, (96, 512)]
+        grad_kernel, [((96, 384), F32), ((4, 96, 384), BF16)], [d_inner, left, right], [one]
     )
     d_right = lax.all_to_all(d_right, "x", 0, 0)
-    (d_both,) = call(merge_kernel, [(two, BF16)], [d_left, d_right], [two])
+    (d_both,) = call(merge_kernel, [(two, BF16)], [d_left, d_right], [two, (3, 96, 128)])
     d_both = exchange(d_both)
     (grad,) = call(
         back_kernel,

time: 117 us -> 115 us (0.983)
  Pallas kernels: 9.6 us -> 8.25 us
    pallas_call x8, Pallas kernels: 8.1 us -> 6.75 us  [call(): pl.pallas_call(kernel, out_shape=shapes, in_specs=[smem] * scalars + [vme...]
where the time goes in v6:
time: 115 us
  blocking collectives  68.6 us (60%)
  waiting for transfers between devices  22.2 us (19%)
  starting transfers between devices  13.3 us (12%)
  Pallas kernels  8.25 us (7%)
  local copies, waits for them, and re-layouts  1.91 us (2%)
    all_to_all x2, blocking collectives, exchange(): lax.all_to_all(rows.reshape(128, -1, 2, 128), GROUP, 0, 0)  49.4 us
    all_to_all x2, waiting for transfers between devices, exchange(): lax.all_to_all(rows.reshape(128, -1, 2, 128), GROUP, 0, 0)  22.2 us
    all_to_all x2, starting transfers between devices, exchange(): lax.all_to_all(rows.reshape(128, -1, 2, 128), GROUP, 0, 0)  13.3 us
    all_to_all x1, blocking collectives, shards(): right = lax.all_to_all(right, 'x', 0, 0)  10.2 us
    all_to_all x1, blocking collectives, shards(): d_right = lax.all_to_all(d_right, 'x', 0, 0)  9 us
    pallas_call x8, Pallas kernels, call(): pl.pallas_call(kernel, out_shape=shapes, in_specs=[smem] * scalars + [vme...  6.75 us
  transfers between devices with their start and end apart: 2, of which 2 were waited for; matrix products, arithmetic and copies ran while one was open for 0% of the time, Pallas kernels for 2%

profile of v6, /device:TPU:1, one launch (start us, length us, event | category | flops | bytes accessed | tf_op | source)
XLA Modules:
  0.0 115.0 jit_solution(12300769473948491683)
XLA Ops:
  0.6 1.5 %shard_map.122 = (bf16[768,128]{1,0:T(8,128)(2,1)S(1)}, f32[256,384]{1,0:T(8,128)S(1)}, f32[256,384]{1,0:T(8,128)S(1)}, f32[384,128]{1,0:T(8,128)S(1)}, f32[384,...) custom-call(s32[4]{0:T(128)} %counts.3, bf16[12,24,128]{2,1,0:T(8,128)(2,1)} %bitcast.23, f32[1,128]{1,0:T(1,128)} %bitcast.21, ...), custom_call_target="tpu_custom_call" | custom-call | tf_op jit(solution)/shard_map/pallas_call | solution.py:252
  2.1 31.8 %all_to_all.30 = bf16[128,3,2,128]{3,2,1,0:T(2,128)(2,1)S(1)} all-to-all(bf16[128,3,2,128]{3,2,1,0:T(2,128)(2,1)S(1)} %bitcast.18), channel_id=1, replica_groups=mesh['x'=4,'z_lo'=4,'y'=8,'z_hi'=2,'core'=2] {'z_lo','y','z_hi','core'}, dimensions={0} | all-to-all | bytes 393216 | tf_op jit(solution)/shard_map/all_to_all | solution.py:263
  34.0 0.4 shard_map.123
  34.4 10.2 %all_to_all.31.right = bf16[4,96,384]{2,1,0:T(8,128)(2,1)S(1)} all-to-all(bf16[4,96,384]{2,1,0:T(8,128)(2,1)S(1)} %get-tuple-element.28), channel_id=1, replica_groups=mesh['x'=4,'z_lo'=4,'y'=8,'z_hi'=2,'core'=2] {'x'}, dimensions={0} | all-to-all | bytes 589824 | tf_op jit(solution)/shard_map/all_to_all | solution.py:295
  44.6 1.2 %shard_map.124 = (bf16[512,128]{1,0:T(8,128)(2,1)}, bf16[384,384]{1,0:T(8,128)(2,1)S(1)}) custom-call(bf16[96,384]{1,0:T(8,128)(2,1)S(1)} %get-tuple-element.27.left, bf16[4,96,384]{2,1,0:T(8,128)(2,1)S(1)} %all_to_all.31.right), custom_call_target="tpu_custom_call" | custom-call | bytes 368640 | tf_op jit(solution)/shard_map/pallas_call | solution.py:237
  45.8 0.0 copy-start.2
  45.8 0.0 copy-start.3
  45.8 0.0 copy-start.4
  45.8 6.8 %all-to-all-start.2 = ((bf16[128,2,2,128]{3,2,1,0:T(2,128)(2,1)}), bf16[128,2,2,128]{3,2,1,0:T(2,128)(2,1)S(1)}, u32[]{:S(2)}, u32[]{:S(2)}) async-start(bf16[128,2,2,128]{3,2,1,0:T(2,128)(2,1)} %bitcast.5), calls=%async_computation.2 | async-start | bytes 262144 | tf_op jit(solution)/shard_map/all_to_all | solution.py:263
  52.6 0.0 copy-start.9
  52.6 0.0 copy-start.10
  52.6 0.0 copy-start.11
  52.6 0.0 copy-done.2
  52.7 0.0 copy-done.3
  52.7 0.0 copy-done.4
  52.7 0.6 copy-done.9
  53.3 0.0 copy-done.10
  53.3 0.0 copy-done.11
  53.3 1.0 shard_map.125
  54.3 0.0 copy-start.7
  54.3 0.6 copy-done.7
  54.9 0.0 copy-start.5
  54.9 10.1 %all-to-all-done.2 = bf16[128,2,2,128]{3,2,1,0:T(2,128)(2,1)S(1)} async-done(((bf16[128,2,2,128]{3,2,1,0:T(2,128)(2,1)}), bf16[128,2,2,128]{3,2,1,0:T(2,128)(2,1)S(1)}, u32[]{:S(2)}, u32[]{:S(2)}) %all-to-all-start.2) | async-done | bytes 131104 | tf_op jit(solution)/shard_map/all_to_all | solution.py:263
  65.0 0.2 shard_map.126
  65.2 0.0 copy-done.5
  65.2 17.5 %all_to_all.32 = bf16[128,2,2,128]{3,2,1,0:T(2,128)(2,1)S(1)} all-to-all(bf16[128,2,2,128]{3,2,1,0:T(2,128)(2,1)S(1)} %bitcast.19), channel_id=1, replica_groups=mesh['x'=4,'z_lo'=4,'y'=8,'z_hi'=2,'core'=2] {'z_lo','y','z_hi','core'}, dimensions={0} | all-to-all | bytes 262144 | tf_op jit(solution)/shard_map/all_to_all | solution.py:263
  82.7 0.6 shard_map.128
  83.3 9.0 %all_to_all.33.d_right = bf16[4,96,384]{2,1,0:T(8,128)(2,1)S(1)} all-to-all(bf16[4,96,384]{2,1,0:T(8,128)(2,1)S(1)} %get-tuple-element.43), channel_id=1, replica_groups=mesh['x'=4,'z_lo'=4,'y'=8,'z_hi'=2,'core'=2] {'x'}, dimensions={0} | all-to-all | bytes 589824 | tf_op jit(solution)/shard_map/all_to_all | solution.py:310
  92.3 1.5 %shard_map.129 = bf16[768,128]{1,0:T(8,128)(2,1)} custom-call(f32[96,384]{1,0:T(8,128)S(1)} %get-tuple-element.42.d_left, bf16[4,96,384]{2,1,0:T(8,128)(2,1)S(1)} %all_to_all.33.d_right), custom_call_target="tpu_custom_call" | custom-call | bytes 442368 | tf_op jit(solution)/shard_map/pallas_call | solution.py:237
  93.8 6.5 %all-to-all-start.5 = ((bf16[128,3,2,128]{3,2,1,0:T(2,128)(2,1)}), bf16[128,3,2,128]{3,2,1,0:T(2,128)(2,1)S(1)}, u32[]{:S(2)}, u32[]{:S(2)}) async-start(bf16[128,3,2,128]{3,2,1,0:T(2,128)(2,1)} %bitcast.11), calls=%async_computation.5 | async-start | bytes 393216 | tf_op jit(solution)/shard_map/all_to_all | solution.py:263
  100.3 0.0 copy-start.12
  100.3 0.0 copy-start.13
  100.3 0.6 copy-done.12
  100.9 0.0 copy-done.13
  100.9 0.0 copy-start
  100.9 0.0 copy-start.1
  100.9 0.0 copy-start.6
  100.9 1.0 shard_map.127
  101.9 0.0 copy-start.8
  101.9 12.1 %all-to-all-done.5 = bf16[128,3,2,128]{3,2,1,0:T(2,128)(2,1)S(1)} async-done(((bf16[128,3,2,128]{3,2,1,0:T(2,128)(2,1)}), bf16[128,3,2,128]{3,2,1,0:T(2,128)(2,1)S(1)}, u32[]{:S(2)}, u32[]{:S(2)}) %all-to-all-start.5) | async-done | bytes 196640 | tf_op jit(solution)/shard_map/all_to_all | solution.py:263
  114.0 0.0 copy-done
  114.0 0.0 copy-done.1
  114.0 0.0 copy-done.6
  114.0 0.0 copy-done.8
  114.0 1.0 shard_map.130
Async XLA Ops:
  45.8 6.9 %copy-start.2 = (bf16[128,128]{1,0:T(8,128)(2,1)S(1)}, bf16[128,128]{1,0:T(8,128)(2,1)}, u32[]{:S(2)}) copy-start(bf16[128,128]{1,0:T(8,128)(2,1)} %w_out_gate.3) | copy-start | bytes 98308
  45.8 6.9 %copy-start.3 = (bf16[128,128]{1,0:T(8,128)(2,1)S(1)}, bf16[128,128]{1,0:T(8,128)(2,1)}, u32[]{:S(2)}) copy-start(bf16[128,128]{1,0:T(8,128)(2,1)} %w_out.3) | copy-start | bytes 98308
  45.8 6.9 %copy-start.4 = (bf16[24,12,128]{2,0,1:T(8,128)(2,1)S(1)}, bf16[24,12,128]{2,0,1:T(8,128)(2,1)}, u32[]{:S(2)}) copy-start(bf16[24,12,128]{2,0,1:T(8,128)(2,1)} %param.12) | copy-start | bytes 221188
  45.8 19.2 %all-to-all-start.2 = ((bf16[128,2,2,128]{3,2,1,0:T(2,128)(2,1)}), bf16[128,2,2,128]{3,2,1,0:T(2,128)(2,1)S(1)}, u32[]{:S(2)}, u32[]{:S(2)}) async-start(bf16[128,2,2,128]{3,2,1,0:T(2,128)(2,1)} %bitcast.5), calls=%async_computation.2 | async-start | bytes 262144 | tf_op jit(solution)/shard_map/all_to_all | solution.py:263
  52.6 0.7 copy-start.9
  52.6 0.7 copy-start.10
  52.6 0.7 copy-start.11
  54.3 0.6 copy-start.7
  54.9 10.3 %copy-start.5 = (f32[128,128]{1,0:T(8,128)}, f32[128,128]{1,0:T(8,128)S(1)}, u32[]{:S(2)}) copy-start(f32[128,128]{1,0:T(8,128)S(1)} %get-tuple-element.49.gain_t) | copy-start | bytes 196612
  93.8 20.2 %all-to-all-start.5 = ((bf16[128,3,2,128]{3,2,1,0:T(2,128)(2,1)}), bf16[128,3,2,128]{3,2,1,0:T(2,128)(2,1)S(1)}, u32[]{:S(2)}, u32[]{:S(2)}) async-start(bf16[128,3,2,128]{3,2,1,0:T(2,128)(2,1)} %bitcast.11), calls=%async_computation.5 | async-start | bytes 393216 | tf_op jit(solution)/shard_map/all_to_all | solution.py:263
  100.3 0.7 copy-start.12
  100.3 0.7 copy-start.13
  100.9 13.1 %copy-start = (bf16[128,256]{1,0:T(8,128)(2,1)S(1)}, bf16[128,256]{1,0:T(8,128)(2,1)}, u32[]{:S(2)}) copy-start(bf16[128,256]{1,0:T(8,128)(2,1)} %w_values.3) | copy-start | bytes 196612
  100.9 13.1 %copy-start.1 = (bf16[128,256]{1,0:T(8,128)(2,1)S(1)}, bf16[128,256]{1,0:T(8,128)(2,1)}, u32[]{:S(2)}) copy-start(bf16[128,256]{1,0:T(8,128)(2,1)} %w_gates.3) | copy-start | bytes 196612
  100.9 13.1 %copy-start.6 = (f32[128,128]{1,0:T(8,128)S(1)}, f32[128,128]{1,0:T(8,128)}, u32[]{:S(2)}) copy-start(f32[128,128]{1,0:T(8,128)} %copy-done.5) | copy-start | bytes 196612
  101.9 12.1 %copy-start.8 = (f32[8,384]{1,0:T(8,128)S(1)}, f32[8,384]{1,0:T(8,128)}, u32[]{:S(2)}) copy-start(f32[8,384]{1,0:T(8,128)} %copy-done.7) | copy-start | bytes 36868

commit v7 on v6

--- a/solution.py
+++ b/solution.py
@@ -71,9 +71,9 @@
     return live.astype(F32)
 
 
-def column(vector, width):
-    square = jnp.broadcast_to(vector.reshape(1, 128), (128, 128)).T
-    return jnp.concatenate([square] * (width // 128), axis=1)
+def columns(*vectors):
+    spare = jnp.zeros((128 - len(vectors), 128), F32)
+    return jnp.concatenate([*vectors, spare], axis=0).T
 
 
 def load_tile(tile):
@@ -96,53 +96,41 @@
     return value[:, 128 * i_hi : 128 * (i_hi + 1)]
 
 
-def front_kernel(
-    counts, pair, gain, bias, w_values, w_gates, both, values, gate, hat, inv, normed,
-    rows, counts_s, pair_s, gain_s, bias_s, w_values_s, w_gates_s, sems,
-):
-    ends = ((pair, pair_s), (gain, gain_s), (bias, bias_s), (w_values, w_values_s), (w_gates, w_gates_s), (counts, counts_s))
-    copies = [pltpu.make_async_copy(src, dst, sems.at[n]) for n, (src, dst) in enumerate(ends)]
+def front_kernel(*refs):
+    ends, (both, scaled, out_sig, upstream, to_values, to_gates, hat, inv, cols) = refs[:11], refs[11:20]
+    rows, held, sems = refs[20], refs[21:32], refs[32]
+    copies = [pltpu.make_async_copy(src, dst, sems.at[n]) for n, (src, dst) in enumerate(zip(ends, held))]
     for copy in copies:
         copy.start()
+    pair, cotangent, in_gain, in_bias, out_gain, out_bias, w_values, w_gates, w_out_gate, w_out, counts = held
     copies[0].wait()
-    x = load_tile(pair_s)
-    centre = x - jnp.mean(x, axis=1, keepdims=True)
-    inv_std = lax.rsqrt(jnp.mean(centre * centre, axis=1, keepdims=True) + EPS)
+    x = load_tile(pair).T
+    centre = x - jnp.mean(x, axis=0, keepdims=True)
+    inv_std = lax.rsqrt(jnp.mean(centre * centre, axis=0, keepdims=True) + EPS)
     pair_hat = centre * inv_std
+    hat[...] = pair_hat
+    inv[...] = jnp.broadcast_to(inv_std, (8, 384))
     for copy in copies[1:]:
         copy.wait()
-    normed_b = (pair_hat * gain_s[...] + bias_s[...]).astype(BF16)
-    hat[...] = pair_hat
-    inv[...] = jnp.broadcast_to(inv_std, (384, 128))
-    normed[...] = normed_b
-    vals = dot(w_values_s[...], normed_b, (0, 1))
-    sig = jax.nn.sigmoid(dot(w_gates_s[...], normed_b, (0, 1)))
-    values[...] = vals
-    gate[...] = sig
-    out = sig * vals * live_mask(counts_s)
+    vectors = columns(in_gain[...], in_bias[...], out_gain[...], out_bias[...])
+    cols[...] = vectors
+    normed_b = (pair_hat * vectors[:, 0:1] + vectors[:, 1:2]).astype(BF16)
+    vals = dot(w_values[...], normed_b, (0, 0))
+    sig = jax.nn.sigmoid(dot(w_gates[...], normed_b, (0, 0)))
+    live = live_mask(counts)
+    sig_live = sig * live
+    out = sig_live * vals
     for i_hi in range(3):
         rows[pl.ds(i_hi, 128, stride=6), :] = third(out[:128], i_hi)
         rows[pl.ds(3 + i_hi, 128, stride=6), :] = third(out[128:], i_hi)
     both[...] = rows[...].astype(BF16)
-
-
-def gate_kernel(
-    counts, normed, cotangent, values, gate, hat, inv, w_out_gate, w_out, in_gain, out_gain,
-    out_sig, upstream, scaled, to_values, to_gates, hat_t, inv_t, gain_t,
-):
-    sig = jax.nn.sigmoid(dot(w_out_gate[...], normed[...], (0, 1)))
+    to_values[...] = sig_live
+    to_gates[...] = out * (1.0 - sig)
+    sig = jax.nn.sigmoid(dot(w_out_gate[...], normed_b, (0, 0)))
     up = load_tile(cotangent).T
-    d_proj = (up * sig).astype(BF16)
     out_sig[...] = sig
     upstream[...] = up
-    scaled[...] = dot(w_out[...], d_proj, (1, 0)) * column(out_gain[...], 384)
-    live = live_mask(counts)
-    sig = gate[...]
-    to_values[...] = sig * live
-    to_gates[...] = values[...] * sig * (1.0 - sig) * live
-    hat_t[...] = hat[...].T
-    inv_t[...] = inv[...].T[:8]
-    gain_t[...] = column(in_gain[...], 128)
+    scaled[...] = dot(w_out[...], (up * sig).astype(BF16), (1, 0)) * vectors[:, 2:3]
 
 
 def split_kernel(both, left, right, rows, natural):
@@ -183,15 +171,6 @@
     d_inner[...] = rows[...].astype(BF16)
 
 
-def update_kernel(inner_hat, out_sig, upstream, out_gain, out_bias, w_out, w_out_gate, update, d_normed, tile):
-    inner_n = inner_hat[...] * column(out_gain[...], 384) + column(out_bias[...], 384)
-    proj = dot(w_out[...], inner_n.astype(BF16), (0, 0))
-    sig = out_sig[...]
-    store_tile((sig * proj).T, tile, update)
-    d_gate_out = (upstream[...] * proj * sig * (1.0 - sig)).astype(BF16)
-    d_normed[...] = dot(w_out_gate[...], d_gate_out, (1, 0))
-
-
 def grad_kernel(d_inner, left, right_all, d_left, d_right, rows):
     rows[...] = d_inner[...].astype(F32)
     packed = to_matrix(rows, 0, 4).astype(BF16)
@@ -213,7 +192,17 @@
     d_both[...] = rows[...].astype(BF16)
 
 
-def back_kernel(d_both, to_values, to_gates, d_out, hat_t, inv_t, gain_t, w_values, w_gates, grad, rows, tile):
+def back_kernel(
+    d_both, to_values, to_gates, hat, inv, cols, inner_hat, out_sig, upstream,
+    w_values, w_gates, w_out_gate, w_out, update, grad, rows, tile,
+):
+    vectors = cols[...]
+    inner_n = inner_hat[...] * vectors[:, 2:3] + vectors[:, 3:4]
+    proj = dot(w_out[...], inner_n.astype(BF16), (0, 0))
+    sig = out_sig[...]
+    gated = sig * proj
+    store_tile(gated.T, tile, update)
+    d_gate_out = (upstream[...] * gated * (1.0 - sig)).astype(BF16)
     rows[...] = d_both[...].astype(F32)
     parts = [
         jnp.concatenate([rows[pl.ds(3 * side + i_hi, 128, stride=6), :] for i_hi in range(3)], axis=1)
@@ -222,39 +211,38 @@
     incoming = jnp.concatenate(parts, axis=0)
     d_values = (incoming * to_values[...]).astype(BF16)
     d_gates = (incoming * to_gates[...]).astype(BF16)
-    d_normed = d_out[...] + dot(w_values[...], d_values, (1, 0)) + dot(w_gates[...], d_gates, (1, 0))
-    scaled = d_normed * jnp.concatenate([gain_t[...]] * 3, axis=1)
-    pair_hat = hat_t[...]
-    first_mean = jnp.mean(scaled, axis=0, keepdims=True)
-    second_mean = jnp.mean(scaled * pair_hat, axis=0, keepdims=True)
-    store_tile((inv_t[:1] * (scaled - first_mean - pair_hat * second_mean)).T, tile, grad)
-
-
-def call(kernel, outs, args, scratch=(), scalars=0, flops=0, last=0):
-    vmem, smem = pl.BlockSpec(memory_space=pltpu.VMEM), pl.BlockSpec(memory_space=pltpu.SMEM)
-    size = sum(a.size * a.dtype.itemsize for a in args)
-    shapes = [jax.ShapeDtypeStruct(*out) if n < last else pltpu.VMEM(*out) for n, out in enumerate(outs)]
+    d_normed = dot(w_out_gate[...], d_gate_out, (1, 0))
+    d_normed += dot(w_values[...], d_values, (1, 0)) + dot(w_gates[...], d_gates, (1, 0))
+    up = d_normed * vectors[:, 0:1]
+    pair_hat = hat[...]
+    first_mean = jnp.mean(up, axis=0, keepdims=True)
+    second_mean = jnp.mean(up * pair_hat, axis=0, keepdims=True)
+    store_tile((inv[:1] * (up - first_mean - pair_hat * second_mean)).T, tile, grad)
+
+
+def call(kernel, outs, args, scratch=(), last=False):
+    vmem = pl.BlockSpec(memory_space=pltpu.VMEM)
+    space = jax.ShapeDtypeStruct if last else pltpu.VMEM
     return pl.pallas_call(
         kernel,
-        out_shape=shapes,
-        in_specs=[smem] * scalars + [vmem] * (len(args) - scalars),
+        out_shape=[space(*out) for out in outs],
+        in_specs=[vmem] * len(args),
         out_specs=[vmem] * len(outs),
         scratch_shapes=[pltpu.VMEM(shape, F32) for shape in scratch],
         compiler_params=pltpu.CompilerParams(vmem_limit_bytes=24 * 1024 * 1024),
-        cost_estimate=pl.CostEstimate(flops=flops, bytes_accessed=size, transcendentals=0),
     )(*args)
 
 
 def call_front(outs, args, rows):
     args = [pltpu.with_memory_space_constraint(arg, pltpu.HBM) for arg in args]
-    spaces = [pltpu.SMEM] + [pltpu.VMEM] * 5
+    spaces = [pltpu.VMEM] * (len(args) - 1) + [pltpu.SMEM]
     held = [space(arg.shape, arg.dtype) for space, arg in zip(spaces, args)]
     return pl.pallas_call(
         front_kernel,
         out_shape=[pltpu.VMEM(*out) for out in outs],
-        in_specs=[pl.BlockSpec(memory_space=pltpu.HBM)] * 6,
+        in_specs=[pl.BlockSpec(memory_space=pltpu.HBM)] * len(args),
         out_specs=[pl.BlockSpec(memory_space=pltpu.VMEM)] * len(outs),
-        scratch_shapes=[pltpu.VMEM(rows, F32)] + held + [pltpu.SemaphoreType.DMA((6,))],
+        scratch_shapes=[pltpu.VMEM(rows, F32)] + held + [pltpu.SemaphoreType.DMA((len(args),))],
         compiler_params=pltpu.CompilerParams(vmem_limit_bytes=24 * 1024 * 1024),
     )(*args)
 
@@ -277,45 +265,41 @@
     w_out,
 ):
     pair, cotangent = pair.transpose(1, 0, 2), cotangent.transpose(1, 0, 2)
-    wide, tall, tokens, tile = (256, 384), (128, 384), (384, 128), (12, 24, 128)
+    wide, tall, tile = (256, 384), (128, 384), (12, 24, 128)
     one, two = (512, 128), (768, 128)
-    both, values, gate, hat, inv, normed = call_front(
-        [(two, BF16), (wide, F32), (wide, F32), (tokens, F32), (tokens, F32), (tokens, BF16)],
-        [chain_counts, pair, in_gain.reshape(1, 128), in_bias.reshape(1, 128), w_values, w_gates],
+    vectors = [vector.reshape(1, 128) for vector in (in_gain, in_bias, out_gain, out_bias)]
+    both, scaled, out_sig, upstream, to_values, to_gates, hat, inv, cols = call_front(
+        [(two, BF16)]
+        + [(tall, F32)] * 3
+        + [(wide, F32)] * 2
+        + [(tall, F32), ((8, 384), F32), ((128, 128), F32)],
+        [pair, cotangent, *vectors, w_values, w_gates, w_out_gate, w_out, chain_counts],
         two,
     )
     both = exchange(both)
-    out_sig, upstream, scaled, to_values, to_gates, hat_t, inv_t, gain_t = call(
-        gate_kernel,
-        [(tall, F32)] * 3 + [(wide, F32)] * 2 + [(tall, F32), ((8, 384), F32), ((128, 128), F32)],
-        [chain_counts, normed, cotangent, values, gate, hat, inv, w_out_gate, w_out, in_gain, out_gain],
-        scalars=1,
-    )
-    left, right = call(split_kernel, [((96, 384), BF16), ((4, 96, 384), BF16)], [both], [two, (3, 96, 128)])
+    left, right = call(
+        split_kernel, [((96, 384), BF16), ((4, 96, 384), BF16)], [both], [two, (3, 96, 128)]
+    )
     right = lax.all_to_all(right, "x", 0, 0)
     inner, right = call(inner_kernel, [(one, BF16), ((384, 384), BF16)], [left, right], [one])
     inner = exchange(inner)
     d_inner, inner_hat = call(norm_kernel, [(one, BF16), (tall, F32)], [inner, scaled], [one])
     d_inner = exchange(d_inner)
-    update, d_out = call(
-        update_kernel,
-        [(tile, BF16), (tall, F32)],
-        [inner_hat, out_sig, upstream, out_gain, out_bias, w_out, w_out_gate],
-        [tile],
-        last=1,
-    )
     d_left, d_right = call(
         grad_kernel, [((96, 384), F32), ((4, 96, 384), BF16)], [d_inner, left, right], [one]
     )
     d_right = lax.all_to_all(d_right, "x", 0, 0)
     (d_both,) = call(merge_kernel, [(two, BF16)], [d_left, d_right], [two, (3, 96, 128)])
     d_both = exchange(d_both)
-    (grad,) = call(
+    update, grad = call(
         back_kernel,
-        [(tile, BF16)],
-        [d_both, to_values, to_gates, d_out, hat_t, inv_t, gain_t, w_values, w_gates],
+        [(tile, BF16)] * 2,
+        [
+            d_both, to_values, to_gates, hat, inv, cols, inner_hat, out_sig, upstream,
+            w_values, w_gates, w_out_gate, w_out,
+        ],
         [two, tile],
-        last=1,
+        last=True,
     )
     return (update.transpose(1, 0, 2), grad.transpose(1, 0, 2))
 

time: 115 us -> 114 us (level)
  blocking collectives: 68.6 us -> 107 us
  waiting for transfers between devices: 22.2 us -> 0 us
  starting transfers between devices: 13.3 us -> 0 us
  Pallas kernels: 8.25 us -> 5.53 us
  local copies, waits for them, and re-layouts: 1.91 us -> 0.03 us
    all_to_all x2 -> x4, blocking collectives: 49.4 us -> 87.9 us  [exchange(): lax.all_to_all(rows.reshape(128, -1, 2, 128), GROUP, 0, 0)]
    all_to_all x2 -> x0, waiting for transfers between devices: 22.2 us -> none  [exchange(): lax.all_to_all(rows.reshape(128, -1, 2, 128), GROUP, 0, 0)]
    all_to_all x2 -> x0, starting transfers between devices: 13.3 us -> none  [exchange(): lax.all_to_all(rows.reshape(128, -1, 2, 128), GROUP, 0, 0)]
    pallas_call x8 -> x6, Pallas kernels: 6.75 us -> 3.63 us  [call(): pl.pallas_call(kernel, out_shape=[space(*out) for out in outs], in_specs=...]
    unnamed x28 -> x8, local copies, waits for them, and re-layouts: 1.91 us -> 0.03 us
  transfers between devices with their start and end apart: 2 -> 0, of which waited for: 2 -> 0; matrix products, arithmetic and copies ran while one was open for 0% -> 0% of each run, Pallas kernels for 2% -> 0%
where the time goes in v7:
time: 114 us; the launch traced here: 113 us
  blocking collectives  107 us (94%)
  Pallas kernels  5.53 us (5%)
    all_to_all x4, blocking collectives, exchange(): lax.all_to_all(rows.reshape(128, -1, 2, 128), GROUP, 0, 0)  87.9 us
    all_to_all x1, blocking collectives, shards(): right = lax.all_to_all(right, 'x', 0, 0)  10.2 us
    all_to_all x1, blocking collectives, shards(): d_right = lax.all_to_all(d_right, 'x', 0, 0)  9 us
    pallas_call x6, Pallas kernels, call(): pl.pallas_call(kernel, out_shape=[space(*out) for out in outs], in_specs=...  3.63 us

profile of v7, /device:TPU:1, one launch (start us, length us, event | category | flops | bytes accessed | tf_op | source)
XLA Modules:
  0.0 113.4 jit_solution(11451921821100321102)
XLA Ops:
  0.6 1.9 %shard_map.122 = (bf16[768,128]{1,0:T(8,128)(2,1)S(1)}, f32[128,384]{1,0:T(8,128)S(1)}, f32[128,384]{1,0:T(8,128)S(1)}, f32[128,384]{1,0:T(8,128)S(1)}, f32[256,...) custom-call(bf16[12,24,128]{2,1,0:T(8,128)(2,1)} %bitcast.24, ...), custom_call_target="tpu_custom_call" | custom-call | tf_op jit(solution)/shard_map/pallas_call | solution.py:240
  2.5 31.8 %all_to_all.30 = bf16[128,3,2,128]{3,2,1,0:T(2,128)(2,1)S(1)} all-to-all(bf16[128,3,2,128]{3,2,1,0:T(2,128)(2,1)S(1)} %bitcast.21), channel_id=1, replica_groups=mesh['x'=4,'z_lo'=4,'y'=8,'z_hi'=2,'core'=2] {'z_lo','y','z_hi','core'}, dimensions={0} | all-to-all | bytes 393216 | tf_op jit(solution)/shard_map/all_to_all | solution.py:251
  34.4 0.4 shard_map.123
  34.8 10.2 %all_to_all.31.right = bf16[4,96,384]{2,1,0:T(8,128)(2,1)S(1)} all-to-all(bf16[4,96,384]{2,1,0:T(8,128)(2,1)S(1)} %get-tuple-element.23), channel_id=1, replica_groups=mesh['x'=4,'z_lo'=4,'y'=8,'z_hi'=2,'core'=2] {'x'}, dimensions={0} | all-to-all | bytes 589824 | tf_op jit(solution)/shard_map/all_to_all | solution.py:283
  45.0 0.5 shard_map.124
  45.5 18.7 %all_to_all.32 = bf16[128,2,2,128]{3,2,1,0:T(2,128)(2,1)S(1)} all-to-all(bf16[128,2,2,128]{3,2,1,0:T(2,128)(2,1)S(1)} %bitcast.23), channel_id=1, replica_groups=mesh['x'=4,'z_lo'=4,'y'=8,'z_hi'=2,'core'=2] {'z_lo','y','z_hi','core'}, dimensions={0} | all-to-all | bytes 262144 | tf_op jit(solution)/shard_map/all_to_all | solution.py:251
  64.2 0.2 shard_map.125
  64.4 17.5 %all_to_all.33 = bf16[128,2,2,128]{3,2,1,0:T(2,128)(2,1)S(1)} all-to-all(bf16[128,2,2,128]{3,2,1,0:T(2,128)(2,1)S(1)} %bitcast.22), channel_id=1, replica_groups=mesh['x'=4,'z_lo'=4,'y'=8,'z_hi'=2,'core'=2] {'z_lo','y','z_hi','core'}, dimensions={0} | all-to-all | bytes 262144 | tf_op jit(solution)/shard_map/all_to_all | solution.py:251
  81.9 0.6 shard_map.126
  82.5 9.0 %all_to_all.34.d_right = bf16[4,96,384]{2,1,0:T(8,128)(2,1)S(1)} all-to-all(bf16[4,96,384]{2,1,0:T(8,128)(2,1)S(1)} %get-tuple-element.29), channel_id=1, replica_groups=mesh['x'=4,'z_lo'=4,'y'=8,'z_hi'=2,'core'=2] {'x'}, dimensions={0} | all-to-all | bytes 589824 | tf_op jit(solution)/shard_map/all_to_all | solution.py:291
  91.5 0.8 shard_map.127
  92.3 0.0 copy-start
  92.3 0.0 copy-start.1
  92.3 0.0 copy-start.2
  92.3 0.0 copy-start.3
  92.3 19.9 %all_to_all.35 = bf16[128,3,2,128]{3,2,1,0:T(2,128)(2,1)S(1)} all-to-all(bf16[128,3,2,128]{3,2,1,0:T(2,128)(2,1)S(1)} %bitcast.17), channel_id=1, replica_groups=mesh['x'=4,'z_lo'=4,'y'=8,'z_hi'=2,'core'=2] {'z_lo','y','z_hi','core'}, dimensions={0} | all-to-all | bytes 393216 | tf_op jit(solution)/shard_map/all_to_all | solution.py:251
  112.2 0.0 copy-done
  112.2 0.0 copy-done.1
  112.2 0.0 copy-done.2
  112.2 0.0 copy-done.3
  112.2 1.2 %shard_map.128 = (bf16[12,24,128]{2,1,0:T(8,128)(2,1)}, bf16[12,24,128]{2,1,0:T(8,128)(2,1)}) custom-call(bf16[768,128]{1,0:T(8,128)(2,1)S(1)} %bitcast.18, f32[256,384]{1,0:T(8,128)S(1)} %get-tuple-element.30.to_values, f32[256,384]{1,0:T(8,128)S(1)} %get-tuple-element.31.to_gates, f32[128,384]{1,0:T(8,128)S(1)} %get-tuple-element.32.hat, ...), custom_call_target="tpu_custom_call" | custom-call | tf_op jit(solution)/shard_map/pallas_call | solution.py:226
Async XLA Ops:
  92.3 19.9 %copy-start = (bf16[128,256]{1,0:T(8,128)(2,1)S(1)}, bf16[128,256]{1,0:T(8,128)(2,1)}, u32[]{:S(2)}) copy-start(bf16[128,256]{1,0:T(8,128)(2,1)} %w_values.1) | copy-start | bytes 196612
  92.3 19.9 %copy-start.1 = (bf16[128,256]{1,0:T(8,128)(2,1)S(1)}, bf16[128,256]{1,0:T(8,128)(2,1)}, u32[]{:S(2)}) copy-start(bf16[128,256]{1,0:T(8,128)(2,1)} %w_gates.1) | copy-start | bytes 196612
  92.3 19.9 %copy-start.2 = (bf16[128,128]{1,0:T(8,128)(2,1)S(1)}, bf16[128,128]{1,0:T(8,128)(2,1)}, u32[]{:S(2)}) copy-start(bf16[128,128]{1,0:T(8,128)(2,1)} %w_out_gate.1) | copy-start | bytes 98308
  92.3 19.9 %copy-start.3 = (bf16[128,128]{1,0:T(8,128)(2,1)S(1)}, bf16[128,128]{1,0:T(8,128)(2,1)}, u32[]{:S(2)}) copy-start(bf16[128,128]{1,0:T(8,128)(2,1)} %w_out.1) | copy-start | bytes 98308

commit v8 on v7

--- a/solution.py
+++ b/solution.py
@@ -103,42 +103,43 @@
     for copy in copies:
         copy.start()
     pair, cotangent, in_gain, in_bias, out_gain, out_bias, w_values, w_gates, w_out_gate, w_out, counts = held
-    copies[0].wait()
-    x = load_tile(pair).T
-    centre = x - jnp.mean(x, axis=0, keepdims=True)
-    inv_std = lax.rsqrt(jnp.mean(centre * centre, axis=0, keepdims=True) + EPS)
-    pair_hat = centre * inv_std
-    hat[...] = pair_hat
-    inv[...] = jnp.broadcast_to(inv_std, (8, 384))
-    for copy in copies[1:]:
+    for copy in copies:
         copy.wait()
     vectors = columns(in_gain[...], in_bias[...], out_gain[...], out_bias[...])
     cols[...] = vectors
-    normed_b = (pair_hat * vectors[:, 0:1] + vectors[:, 1:2]).astype(BF16)
-    vals = dot(w_values[...], normed_b, (0, 0))
-    sig = jax.nn.sigmoid(dot(w_gates[...], normed_b, (0, 0)))
-    live = live_mask(counts)
-    sig_live = sig * live
-    out = sig_live * vals
-    for i_hi in range(3):
-        rows[pl.ds(i_hi, 128, stride=6), :] = third(out[:128], i_hi)
-        rows[pl.ds(3 + i_hi, 128, stride=6), :] = third(out[128:], i_hi)
-    both[...] = rows[...].astype(BF16)
-    to_values[...] = sig_live
-    to_gates[...] = out * (1.0 - sig)
-    sig = jax.nn.sigmoid(dot(w_out_gate[...], normed_b, (0, 0)))
-    up = load_tile(cotangent).T
-    out_sig[...] = sig
-    upstream[...] = up
-    scaled[...] = dot(w_out[...], (up * sig).astype(BF16), (1, 0)) * vectors[:, 2:3]
+    live_all = live_mask(counts)
+    tile_x, tile_up = load_tile(pair), load_tile(cotangent)
+    for i_hi in range(3):
+        lanes = slice(128 * i_hi, 128 * (i_hi + 1))
+        x = tile_x[lanes].T
+        centre = x - jnp.mean(x, axis=0, keepdims=True)
+        inv_std = lax.rsqrt(jnp.mean(centre * centre, axis=0, keepdims=True) + EPS)
+        pair_hat = centre * inv_std
+        hat[:, lanes] = pair_hat
+        inv[:, lanes] = jnp.broadcast_to(inv_std, (8, 128))
+        normed_b = (pair_hat * vectors[:, 0:1] + vectors[:, 1:2]).astype(BF16)
+        vals = dot(w_values[...], normed_b, (0, 0))
+        sig = jax.nn.sigmoid(dot(w_gates[...], normed_b, (0, 0)))
+        sig_live = sig * third(live_all, i_hi)
+        out = sig_live * vals
+        rows[pl.ds(i_hi, 128, stride=6), :] = out[:128]
+        rows[pl.ds(3 + i_hi, 128, stride=6), :] = out[128:]
+        to_values[:, lanes] = sig_live
+        to_gates[:, lanes] = out * (1.0 - sig)
+        sig = jax.nn.sigmoid(dot(w_out_gate[...], normed_b, (0, 0)))
+        up = tile_up[lanes].T
+        out_sig[:, lanes] = sig
+        upstream[:, lanes] = up.astype(BF16)
+        scaled[:, lanes] = dot(w_out[...], (up * sig).astype(BF16), (1, 0)) * vectors[:, 2:3]
+    both[...] = rows[:768].astype(BF16)
 
 
 def split_kernel(both, left, right, rows, natural):
-    rows[...] = both[...].astype(F32)
+    rows[:768] = both[...].astype(F32)
     matrix = to_matrix(rows, 3, 6)
     packed = []
     for t in range(3):
-        natural[t] = third(matrix, t)
+        natural[t, :96] = third(matrix, t)
         packed += [jnp.concatenate([natural[t, pl.ds(slot, LOW, stride=12), :] for slot in range(12)], axis=0)]
     packed = jnp.concatenate(packed, axis=1).astype(BF16)
     for part in range(4):
@@ -153,11 +154,11 @@
     right_all[...] = ordered
     to_rows(dot(left[...], ordered, (1, 1)), rows, 0, 4)
     rows[pl.ds(3, 128, stride=4), :] = jnp.zeros((128, 128), F32)
-    inner[...] = rows[...].astype(BF16)
+    inner[...] = rows[:512].astype(BF16)
 
 
 def norm_kernel(inner, scaled, d_inner, inner_hat, rows):
-    rows[...] = inner[...].astype(F32)
+    rows[:512] = inner[...].astype(F32)
     for i_hi in range(3):
         x = rows[pl.ds(i_hi, 128, stride=4), :]
         centre = x - jnp.mean(x, axis=0, keepdims=True)
@@ -168,11 +169,11 @@
         second_mean = jnp.mean(up * hat, axis=0, keepdims=True)
         rows[pl.ds(i_hi, 128, stride=4), :] = inv_std * (up - first_mean - hat * second_mean)
         inner_hat[:, 128 * i_hi : 128 * (i_hi + 1)] = hat
-    d_inner[...] = rows[...].astype(BF16)
+    d_inner[...] = rows[:512].astype(BF16)
 
 
 def grad_kernel(d_inner, left, right_all, d_left, d_right, rows):
-    rows[...] = d_inner[...].astype(F32)
+    rows[:512] = d_inner[...].astype(F32)
     packed = to_matrix(rows, 0, 4).astype(BF16)
     sums = dot(packed, left[...], (0, 0))
     for part in range(4):
@@ -188,8 +189,8 @@
     for t in range(3):
         for slot in range(12):
             natural[t, pl.ds(slot, LOW, stride=12), :] = third(total, t)[LOW * slot : LOW * (slot + 1)]
-    to_rows(jnp.concatenate([natural[t] for t in range(3)], axis=1), rows, 3, 6)
-    d_both[...] = rows[...].astype(BF16)
+    to_rows(jnp.concatenate([natural[t, :96] for t in range(3)], axis=1), rows, 3, 6)
+    d_both[...] = rows[:768].astype(BF16)
 
 
 def back_kernel(
@@ -202,8 +203,8 @@
     sig = out_sig[...]
     gated = sig * proj
     store_tile(gated.T, tile, update)
-    d_gate_out = (upstream[...] * gated * (1.0 - sig)).astype(BF16)
-    rows[...] = d_both[...].astype(F32)
+    d_gate_out = (upstream[...].astype(F32) * gated * (1.0 - sig)).astype(BF16)
+    rows[:768] = d_both[...].astype(F32)
     parts = [
         jnp.concatenate([rows[pl.ds(3 * side + i_hi, 128, stride=6), :] for i_hi in range(3)], axis=1)
         for side in range(2)
@@ -267,29 +268,31 @@
     pair, cotangent = pair.transpose(1, 0, 2), cotangent.transpose(1, 0, 2)
     wide, tall, tile = (256, 384), (128, 384), (12, 24, 128)
     one, two = (512, 128), (768, 128)
+    one_rows, two_rows, natural = (520, 128), (776, 128), (3, 112, 128)
     vectors = [vector.reshape(1, 128) for vector in (in_gain, in_bias, out_gain, out_bias)]
     both, scaled, out_sig, upstream, to_values, to_gates, hat, inv, cols = call_front(
         [(two, BF16)]
-        + [(tall, F32)] * 3
+        + [(tall, F32)] * 2
+        + [(tall, BF16)]
         + [(wide, F32)] * 2
         + [(tall, F32), ((8, 384), F32), ((128, 128), F32)],
         [pair, cotangent, *vectors, w_values, w_gates, w_out_gate, w_out, chain_counts],
-        two,
+        two_rows,
     )
     both = exchange(both)
     left, right = call(
-        split_kernel, [((96, 384), BF16), ((4, 96, 384), BF16)], [both], [two, (3, 96, 128)]
+        split_kernel, [((96, 384), BF16), ((4, 96, 384), BF16)], [both], [two_rows, natural]
     )
     right = lax.all_to_all(right, "x", 0, 0)
-    inner, right = call(inner_kernel, [(one, BF16), ((384, 384), BF16)], [left, right], [one])
+    inner, right = call(inner_kernel, [(one, BF16), ((384, 384), BF16)], [left, right], [one_rows])
     inner = exchange(inner)
-    d_inner, inner_hat = call(norm_kernel, [(one, BF16), (tall, F32)], [inner, scaled], [one])
+    d_inner, inner_hat = call(norm_kernel, [(one, BF16), (tall, F32)], [inner, scaled], [one_rows])
     d_inner = exchange(d_inner)
     d_left, d_right = call(
-        grad_kernel, [((96, 384), F32), ((4, 96, 384), BF16)], [d_inner, left, right], [one]
+        grad_kernel, [((96, 384), F32), ((4, 96, 384), BF16)], [d_inner, left, right], [one_rows]
     )
     d_right = lax.all_to_all(d_right, "x", 0, 0)
-    (d_both,) = call(merge_kernel, [(two, BF16)], [d_left, d_right], [two, (3, 96, 128)])
+    (d_both,) = call(merge_kernel, [(two, BF16)], [d_left, d_right], [two_rows, natural])
     d_both = exchange(d_both)
     update, grad = call(
         back_kernel,
@@ -298,7 +301,7 @@
             d_both, to_values, to_gates, hat, inv, cols, inner_hat, out_sig, upstream,
             w_values, w_gates, w_out_gate, w_out,
         ],
-        [two, tile],
+        [two_rows, tile],
         last=True,
     )
     return (update.transpose(1, 0, 2), grad.transpose(1, 0, 2))

time: 114 us -> 114 us (level)
  no operation moved by 1% of the time
where the time goes in v8:
time: 114 us; the launch traced here: 113 us
  blocking collectives  107 us (94%)
  Pallas kernels  5.42 us (5%)
    all_to_all x4, blocking collectives, exchange(): lax.all_to_all(rows.reshape(128, -1, 2, 128), GROUP, 0, 0)  87.9 us
    all_to_all x1, blocking collectives, shards(): right = lax.all_to_all(right, 'x', 0, 0)  10.2 us
    all_to_all x1, blocking collectives, shards(): d_right = lax.all_to_all(d_right, 'x', 0, 0)  9 us
    pallas_call x6, Pallas kernels, call(): pl.pallas_call(kernel, out_shape=[space(*out) for out in outs], in_specs=...  3.63 us

profile of v8, /device:TPU:1, one launch (start us, length us, event | category | flops | bytes accessed | tf_op | source)
XLA Modules:
  0.0 113.3 jit_solution(14111051679424898106)
XLA Ops:
  0.6 1.8 %shard_map.122 = (bf16[768,128]{1,0:T(8,128)(2,1)S(1)}, f32[128,384]{1,0:T(8,128)S(1)}, f32[128,384]{1,0:T(8,128)S(1)}, bf16[128,384]{1,0:T(8,128)(2,1)S(1)}, f3...) custom-call(bf16[12,24,128]{2,1,0:T(8,128)(2,1)} %bitcast.24, ...), custom_call_target="tpu_custom_call" | custom-call | tf_op jit(solution)/shard_map/pallas_call | solution.py:241
  2.4 31.8 %all_to_all.30 = bf16[128,3,2,128]{3,2,1,0:T(2,128)(2,1)S(1)} all-to-all(bf16[128,3,2,128]{3,2,1,0:T(2,128)(2,1)S(1)} %bitcast.21), channel_id=1, replica_groups=mesh['x'=4,'z_lo'=4,'y'=8,'z_hi'=2,'core'=2] {'z_lo','y','z_hi','core'}, dimensions={0} | all-to-all | bytes 393216 | tf_op jit(solution)/shard_map/all_to_all | solution.py:252
  34.3 0.4 shard_map.123
  34.7 10.2 %all_to_all.31.right = bf16[4,96,384]{2,1,0:T(8,128)(2,1)S(1)} all-to-all(bf16[4,96,384]{2,1,0:T(8,128)(2,1)S(1)} %get-tuple-element.23), channel_id=1, replica_groups=mesh['x'=4,'z_lo'=4,'y'=8,'z_hi'=2,'core'=2] {'x'}, dimensions={0} | all-to-all | bytes 589824 | tf_op jit(solution)/shard_map/all_to_all | solution.py:286
  44.9 0.5 shard_map.124
  45.4 18.7 %all_to_all.32 = bf16[128,2,2,128]{3,2,1,0:T(2,128)(2,1)S(1)} all-to-all(bf16[128,2,2,128]{3,2,1,0:T(2,128)(2,1)S(1)} %bitcast.23), channel_id=1, replica_groups=mesh['x'=4,'z_lo'=4,'y'=8,'z_hi'=2,'core'=2] {'z_lo','y','z_hi','core'}, dimensions={0} | all-to-all | bytes 262144 | tf_op jit(solution)/shard_map/all_to_all | solution.py:252
  64.1 0.2 shard_map.125
  64.3 17.5 %all_to_all.33 = bf16[128,2,2,128]{3,2,1,0:T(2,128)(2,1)S(1)} all-to-all(bf16[128,2,2,128]{3,2,1,0:T(2,128)(2,1)S(1)} %bitcast.22), channel_id=1, replica_groups=mesh['x'=4,'z_lo'=4,'y'=8,'z_hi'=2,'core'=2] {'z_lo','y','z_hi','core'}, dimensions={0} | all-to-all | bytes 262144 | tf_op jit(solution)/shard_map/all_to_all | solution.py:252
  81.8 0.6 shard_map.126
  82.4 9.0 %all_to_all.34.d_right = bf16[4,96,384]{2,1,0:T(8,128)(2,1)S(1)} all-to-all(bf16[4,96,384]{2,1,0:T(8,128)(2,1)S(1)} %get-tuple-element.29), channel_id=1, replica_groups=mesh['x'=4,'z_lo'=4,'y'=8,'z_hi'=2,'core'=2] {'x'}, dimensions={0} | all-to-all | bytes 589824 | tf_op jit(solution)/shard_map/all_to_all | solution.py:294
  91.4 0.8 shard_map.127
  92.2 0.0 copy-start
  92.2 0.0 copy-start.1
  92.2 0.0 copy-start.2
  92.2 0.0 copy-start.3
  92.2 19.9 %all_to_all.35 = bf16[128,3,2,128]{3,2,1,0:T(2,128)(2,1)S(1)} all-to-all(bf16[128,3,2,128]{3,2,1,0:T(2,128)(2,1)S(1)} %bitcast.18), channel_id=1, replica_groups=mesh['x'=4,'z_lo'=4,'y'=8,'z_hi'=2,'core'=2] {'z_lo','y','z_hi','core'}, dimensions={0} | all-to-all | bytes 393216 | tf_op jit(solution)/shard_map/all_to_all | solution.py:252
  112.1 0.0 copy-done
  112.1 0.0 copy-done.1
  112.1 0.0 copy-done.2
  112.1 0.0 copy-done.3
  112.1 1.2 %shard_map.128 = (bf16[12,24,128]{2,1,0:T(8,128)(2,1)}, bf16[12,24,128]{2,1,0:T(8,128)(2,1)}) custom-call(bf16[768,128]{1,0:T(8,128)(2,1)S(1)} %bitcast.16, f32[256,384]{1,0:T(8,128)S(1)} %get-tuple-element.30.to_values, f32[256,384]{1,0:T(8,128)S(1)} %get-tuple-element.31.to_gates, f32[128,384]{1,0:T(8,128)S(1)} %get-tuple-element.32.hat, ...), custom_call_target="tpu_custom_call" | custom-call | tf_op jit(solution)/shard_map/pallas_call | solution.py:227
Async XLA Ops:
  92.2 19.9 %copy-start = (bf16[128,256]{1,0:T(8,128)(2,1)S(1)}, bf16[128,256]{1,0:T(8,128)(2,1)}, u32[]{:S(2)}) copy-start(bf16[128,256]{1,0:T(8,128)(2,1)} %w_values.1) | copy-start | bytes 196612
  92.2 19.9 %copy-start.1 = (bf16[128,256]{1,0:T(8,128)(2,1)S(1)}, bf16[128,256]{1,0:T(8,128)(2,1)}, u32[]{:S(2)}) copy-start(bf16[128,256]{1,0:T(8,128)(2,1)} %w_gates.1) | copy-start | bytes 196612
  92.2 19.9 %copy-start.2 = (bf16[128,128]{1,0:T(8,128)(2,1)S(1)}, bf16[128,128]{1,0:T(8,128)(2,1)}, u32[]{:S(2)}) copy-start(bf16[128,128]{1,0:T(8,128)(2,1)} %w_out_gate.1) | copy-start | bytes 98308
  92.2 19.9 %copy-start.3 = (bf16[128,128]{1,0:T(8,128)(2,1)S(1)}, bf16[128,128]{1,0:T(8,128)(2,1)}, u32[]{:S(2)}) copy-start(bf16[128,128]{1,0:T(8,128)(2,1)} %w_out.1) | copy-start | bytes 98308

commit v9 on v8

--- a/solution.py
+++ b/solution.py
@@ -21,16 +21,7 @@
 
 
 def swap_quads(quad):
-    lane = lax.broadcasted_iota(jnp.int32, (LOW, 128), 1)
-    quad = list(quad)
-    for step in (2, 1):
-        low = (lane & (32 * step)) == 0
-        for a in range(4):
-            if a & step == 0:
-                one, two = quad[a], quad[a + step]
-                quad[a] = jnp.where(low, one, pltpu.roll(two, 32 * step, 1))
-                quad[a + step] = jnp.where(low, pltpu.roll(one, 128 - 32 * step, 1), two)
-    return quad
+    return [jnp.concatenate([part[:, 32 * b : 32 * (b + 1)] for part in quad], axis=1) for b in range(4)]
 
 
 def to_matrix(rows, first, per):
@@ -52,11 +43,17 @@
 
 
 def to_rows(matrix, rows, first, per):
-    for i_hi in range(3):
-        parts = []
-        for j_hi in range(3):
-            bands = [24 * z + LOW * i_hi for z in range(4)]
-            parts += swap_quads([matrix[band : band + LOW, 128 * j_hi : 128 * (j_hi + 1)] for band in bands])
+    pieces = [(i_hi, j_hi) for i_hi in range(3) for j_hi in range(3)]
+    quad = []
+    for z in range(4):
+        bands = [
+            matrix[24 * z + LOW * i_hi : 24 * z + LOW * (i_hi + 1), 128 * j_hi : 128 * (j_hi + 1)]
+            for i_hi, j_hi in pieces
+        ]
+        quad += [jnp.concatenate(bands, axis=0)]
+    quad = swap_quads(quad)
+    for i_hi in range(3):
+        parts = [part[LOW * n : LOW * (n + 1)] for n in range(3 * i_hi, 3 * i_hi + 3) for part in quad]
         parts += [jnp.zeros(((SLOTS - 12) * LOW, 128), F32)]
         rows[pl.ds(first + i_hi, 128, stride=per), :] = jnp.concatenate(parts, axis=0).T
 

time: 114 us -> 113 us (level)
  no operation moved by 1% of the time
where the time goes in v9:
time: 113 us
  blocking collectives  107 us (95%)
  Pallas kernels  4.93 us (4%)
    all_to_all x4, blocking collectives, exchange(): lax.all_to_all(rows.reshape(128, -1, 2, 128), GROUP, 0, 0)  87.9 us
    all_to_all x1, blocking collectives, shards(): right = lax.all_to_all(right, 'x', 0, 0)  10.2 us
    all_to_all x1, blocking collectives, shards(): d_right = lax.all_to_all(d_right, 'x', 0, 0)  9 us
    pallas_call x6, Pallas kernels, call(): pl.pallas_call(kernel, out_shape=[space(*out) for out in outs], in_specs=...  3.14 us

profile of v9, /device:TPU:1, one launch (start us, length us, event | category | flops | bytes accessed | tf_op | source)
XLA Modules:
  0.0 112.8 jit_solution(10395264024363213383)
XLA Ops:
  0.6 1.8 %shard_map.122 = (bf16[768,128]{1,0:T(8,128)(2,1)S(1)}, f32[128,384]{1,0:T(8,128)S(1)}, f32[128,384]{1,0:T(8,128)S(1)}, bf16[128,384]{1,0:T(8,128)(2,1)S(1)}, f3...) custom-call(bf16[12,24,128]{2,1,0:T(8,128)(2,1)} %bitcast.24, ...), custom_call_target="tpu_custom_call" | custom-call | tf_op jit(solution)/shard_map/pallas_call | solution.py:238
  2.4 31.8 %all_to_all.30 = bf16[128,3,2,128]{3,2,1,0:T(2,128)(2,1)S(1)} all-to-all(bf16[128,3,2,128]{3,2,1,0:T(2,128)(2,1)S(1)} %bitcast.21), channel_id=1, replica_groups=mesh['x'=4,'z_lo'=4,'y'=8,'z_hi'=2,'core'=2] {'z_lo','y','z_hi','core'}, dimensions={0} | all-to-all | bytes 393216 | tf_op jit(solution)/shard_map/all_to_all | solution.py:249
  34.3 0.3 shard_map.123
  34.6 10.2 %all_to_all.31.right = bf16[4,96,384]{2,1,0:T(8,128)(2,1)S(1)} all-to-all(bf16[4,96,384]{2,1,0:T(8,128)(2,1)S(1)} %get-tuple-element.23), channel_id=1, replica_groups=mesh['x'=4,'z_lo'=4,'y'=8,'z_hi'=2,'core'=2] {'x'}, dimensions={0} | all-to-all | bytes 589824 | tf_op jit(solution)/shard_map/all_to_all | solution.py:283
  44.8 0.5 shard_map.124
  45.3 18.7 %all_to_all.32 = bf16[128,2,2,128]{3,2,1,0:T(2,128)(2,1)S(1)} all-to-all(bf16[128,2,2,128]{3,2,1,0:T(2,128)(2,1)S(1)} %bitcast.23), channel_id=1, replica_groups=mesh['x'=4,'z_lo'=4,'y'=8,'z_hi'=2,'core'=2] {'z_lo','y','z_hi','core'}, dimensions={0} | all-to-all | bytes 262144 | tf_op jit(solution)/shard_map/all_to_all | solution.py:249
  64.0 0.2 shard_map.125
  64.2 17.5 %all_to_all.33 = bf16[128,2,2,128]{3,2,1,0:T(2,128)(2,1)S(1)} all-to-all(bf16[128,2,2,128]{3,2,1,0:T(2,128)(2,1)S(1)} %bitcast.22), channel_id=1, replica_groups=mesh['x'=4,'z_lo'=4,'y'=8,'z_hi'=2,'core'=2] {'z_lo','y','z_hi','core'}, dimensions={0} | all-to-all | bytes 262144 | tf_op jit(solution)/shard_map/all_to_all | solution.py:249
  81.7 0.5 shard_map.126
  82.2 9.0 %all_to_all.34.d_right = bf16[4,96,384]{2,1,0:T(8,128)(2,1)S(1)} all-to-all(bf16[4,96,384]{2,1,0:T(8,128)(2,1)S(1)} %get-tuple-element.29), channel_id=1, replica_groups=mesh['x'=4,'z_lo'=4,'y'=8,'z_hi'=2,'core'=2] {'x'}, dimensions={0} | all-to-all | bytes 589824 | tf_op jit(solution)/shard_map/all_to_all | solution.py:291
  91.2 0.4 shard_map.127
  91.7 0.0 copy-start
  91.7 0.0 copy-start.1
  91.7 0.0 copy-start.2
  91.7 0.0 copy-start.3
  91.7 19.9 %all_to_all.35 = bf16[128,3,2,128]{3,2,1,0:T(2,128)(2,1)S(1)} all-to-all(bf16[128,3,2,128]{3,2,1,0:T(2,128)(2,1)S(1)} %bitcast.18), channel_id=1, replica_groups=mesh['x'=4,'z_lo'=4,'y'=8,'z_hi'=2,'core'=2] {'z_lo','y','z_hi','core'}, dimensions={0} | all-to-all | bytes 393216 | tf_op jit(solution)/shard_map/all_to_all | solution.py:249
  111.6 0.0 copy-done
  111.6 0.0 copy-done.1
  111.6 0.0 copy-done.2
  111.6 0.0 copy-done.3
  111.6 1.2 %shard_map.128 = (bf16[12,24,128]{2,1,0:T(8,128)(2,1)}, bf16[12,24,128]{2,1,0:T(8,128)(2,1)}) custom-call(bf16[768,128]{1,0:T(8,128)(2,1)S(1)} %bitcast.16, f32[256,384]{1,0:T(8,128)S(1)} %get-tuple-element.30.to_values, f32[256,384]{1,0:T(8,128)S(1)} %get-tuple-element.31.to_gates, f32[128,384]{1,0:T(8,128)S(1)} %get-tuple-element.32.hat, ...), custom_call_target="tpu_custom_call" | custom-call | tf_op jit(solution)/shard_map/pallas_call | solution.py:224
Async XLA Ops:
  91.7 19.9 %copy-start = (bf16[128,256]{1,0:T(8,128)(2,1)S(1)}, bf16[128,256]{1,0:T(8,128)(2,1)}, u32[]{:S(2)}) copy-start(bf16[128,256]{1,0:T(8,128)(2,1)} %w_values.1) | copy-start | bytes 196612
  91.7 19.9 %copy-start.1 = (bf16[128,256]{1,0:T(8,128)(2,1)S(1)}, bf16[128,256]{1,0:T(8,128)(2,1)}, u32[]{:S(2)}) copy-start(bf16[128,256]{1,0:T(8,128)(2,1)} %w_gates.1) | copy-start | bytes 196612
  91.7 19.9 %copy-start.2 = (bf16[128,128]{1,0:T(8,128)(2,1)S(1)}, bf16[128,128]{1,0:T(8,128)(2,1)}, u32[]{:S(2)}) copy-start(bf16[128,128]{1,0:T(8,128)(2,1)} %w_out_gate.1) | copy-start | bytes 98308
  91.7 19.9 %copy-start.3 = (bf16[128,128]{1,0:T(8,128)(2,1)S(1)}, bf16[128,128]{1,0:T(8,128)(2,1)}, u32[]{:S(2)}) copy-start(bf16[128,128]{1,0:T(8,128)(2,1)} %w_out.1) | copy-start | bytes 98308

commit v10 on v9

--- a/solution.py
+++ b/solution.py
@@ -94,18 +94,18 @@
 
 
 def front_kernel(*refs):
-    ends, (both, scaled, out_sig, upstream, to_values, to_gates, hat, inv, cols) = refs[:11], refs[11:20]
-    rows, held, sems = refs[20], refs[21:32], refs[32]
+    ends, (both, normed, to_values, to_gates, hat, inv, cols) = refs[:8], refs[8:15]
+    rows, held, sems = refs[15], refs[16:24], refs[24]
     copies = [pltpu.make_async_copy(src, dst, sems.at[n]) for n, (src, dst) in enumerate(zip(ends, held))]
     for copy in copies:
         copy.start()
-    pair, cotangent, in_gain, in_bias, out_gain, out_bias, w_values, w_gates, w_out_gate, w_out, counts = held
+    pair, in_gain, in_bias, out_gain, out_bias, w_values, w_gates, counts = held
     for copy in copies:
         copy.wait()
     vectors = columns(in_gain[...], in_bias[...], out_gain[...], out_bias[...])
     cols[...] = vectors
     live_all = live_mask(counts)
-    tile_x, tile_up = load_tile(pair), load_tile(cotangent)
+    tile_x = load_tile(pair)
     for i_hi in range(3):
         lanes = slice(128 * i_hi, 128 * (i_hi + 1))
         x = tile_x[lanes].T
@@ -115,6 +115,7 @@
         hat[:, lanes] = pair_hat
         inv[:, lanes] = jnp.broadcast_to(inv_std, (8, 128))
         normed_b = (pair_hat * vectors[:, 0:1] + vectors[:, 1:2]).astype(BF16)
+        normed[:, lanes] = normed_b
         vals = dot(w_values[...], normed_b, (0, 0))
         sig = jax.nn.sigmoid(dot(w_gates[...], normed_b, (0, 0)))
         sig_live = sig * third(live_all, i_hi)
@@ -123,15 +124,17 @@
         rows[pl.ds(3 + i_hi, 128, stride=6), :] = out[128:]
         to_values[:, lanes] = sig_live
         to_gates[:, lanes] = out * (1.0 - sig)
-        sig = jax.nn.sigmoid(dot(w_out_gate[...], normed_b, (0, 0)))
-        up = tile_up[lanes].T
-        out_sig[:, lanes] = sig
-        upstream[:, lanes] = up.astype(BF16)
-        scaled[:, lanes] = dot(w_out[...], (up * sig).astype(BF16), (1, 0)) * vectors[:, 2:3]
     both[...] = rows[:768].astype(BF16)
 
 
-def split_kernel(both, left, right, rows, natural):
+def split_kernel(
+    both, normed, cotangent, w_out_gate, w_out, cols, left, right, scaled, out_sig, upstream, rows, natural
+):
+    sig = jax.nn.sigmoid(dot(w_out_gate[...], normed[...], (0, 0)))
+    up = load_tile(cotangent).T
+    out_sig[...] = sig
+    upstream[...] = up.astype(BF16)
+    scaled[...] = dot(w_out[...], (up * sig).astype(BF16), (1, 0)) * cols[:, 2:3]
     rows[:768] = both[...].astype(F32)
     matrix = to_matrix(rows, 3, 6)
     packed = []
@@ -267,18 +270,19 @@
     one, two = (512, 128), (768, 128)
     one_rows, two_rows, natural = (520, 128), (776, 128), (3, 112, 128)
     vectors = [vector.reshape(1, 128) for vector in (in_gain, in_bias, out_gain, out_bias)]
-    both, scaled, out_sig, upstream, to_values, to_gates, hat, inv, cols = call_front(
-        [(two, BF16)]
-        + [(tall, F32)] * 2
-        + [(tall, BF16)]
+    both, normed, to_values, to_gates, hat, inv, cols = call_front(
+        [(two, BF16), (tall, BF16)]
         + [(wide, F32)] * 2
         + [(tall, F32), ((8, 384), F32), ((128, 128), F32)],
-        [pair, cotangent, *vectors, w_values, w_gates, w_out_gate, w_out, chain_counts],
+        [pair, *vectors, w_values, w_gates, chain_counts],
         two_rows,
     )
     both = exchange(both)
-    left, right = call(
-        split_kernel, [((96, 384), BF16), ((4, 96, 384), BF16)], [both], [two_rows, natural]
+    left, right, scaled, out_sig, upstream = call(
+        split_kernel,
+        [((96, 384), BF16), ((4, 96, 384), BF16), (tall, F32), (tall, F32), (tall, BF16)],
+        [both, normed, cotangent, w_out_gate, w_out, cols],
+        [two_rows, natural],
     )
     right = lax.all_to_all(right, "x", 0, 0)
     inner, right = call(inner_kernel, [(one, BF16), ((384, 384), BF16)], [left, right], [one_rows])

time: 113 us -> 113 us (level)
  no operation moved by 1% of the time
where the time goes in v10:
time: 113 us
  blocking collectives  107 us (95%)
  Pallas kernels  4.81 us (4%)
    all_to_all x4, blocking collectives, exchange(): lax.all_to_all(rows.reshape(128, -1, 2, 128), GROUP, 0, 0)  88 us
    all_to_all x1, blocking collectives, shards(): right = lax.all_to_all(right, 'x', 0, 0)  10.2 us
    all_to_all x1, blocking collectives, shards(): d_right = lax.all_to_all(d_right, 'x', 0, 0)  9 us
    pallas_call x6, Pallas kernels, call(): pl.pallas_call(kernel, out_shape=[space(*out) for out in outs], in_specs=...  3.23 us

profile of v10, /device:TPU:1, one launch (start us, length us, event | category | flops | bytes accessed | tf_op | source)
XLA Modules:
  0.0 112.8 jit_solution(6836008353575122702)
XLA Ops:
  0.6 1.6 %shard_map.122 = (bf16[768,128]{1,0:T(8,128)(2,1)S(1)}, bf16[128,384]{1,0:T(8,128)(2,1)S(1)}, f32[256,384]{1,0:T(8,128)S(1)}, f32[256,384]{1,0:T(8,128)S(1)}, f3...) custom-call(bf16[12,24,128]{2,1,0:T(8,128)(2,1)} %bitcast.25, f32[1,128]{1,0:T(1,128)} %bitcast.26, ...), custom_call_target="tpu_custom_call" | custom-call | tf_op jit(solution)/shard_map/pallas_call | solution.py:241
  2.2 0.0 copy-start.2
  2.2 0.0 copy-start.3
  2.2 0.0 copy-start.4
  2.3 32.0 %all_to_all.30 = bf16[128,3,2,128]{3,2,1,0:T(2,128)(2,1)S(1)} all-to-all(bf16[128,3,2,128]{3,2,1,0:T(2,128)(2,1)S(1)} %bitcast.21), channel_id=1, replica_groups=mesh['x'=4,'z_lo'=4,'y'=8,'z_hi'=2,'core'=2] {'z_lo','y','z_hi','core'}, dimensions={0} | all-to-all | bytes 393216 | tf_op jit(solution)/shard_map/all_to_all | solution.py:252
  34.2 0.0 copy-done.2
  34.2 0.0 copy-done.3
  34.2 0.0 copy-done.4
  34.2 0.4 shard_map.123
  34.6 10.2 %all_to_all.31.right = bf16[4,96,384]{2,1,0:T(8,128)(2,1)S(1)} all-to-all(bf16[4,96,384]{2,1,0:T(8,128)(2,1)S(1)} %get-tuple-element.26), channel_id=1, replica_groups=mesh['x'=4,'z_lo'=4,'y'=8,'z_hi'=2,'core'=2] {'x'}, dimensions={0} | all-to-all | bytes 589824 | tf_op jit(solution)/shard_map/all_to_all | solution.py:287
  44.9 0.5 shard_map.124
  45.4 18.7 %all_to_all.32 = bf16[128,2,2,128]{3,2,1,0:T(2,128)(2,1)S(1)} all-to-all(bf16[128,2,2,128]{3,2,1,0:T(2,128)(2,1)S(1)} %bitcast.23), channel_id=1, replica_groups=mesh['x'=4,'z_lo'=4,'y'=8,'z_hi'=2,'core'=2] {'z_lo','y','z_hi','core'}, dimensions={0} | all-to-all | bytes 262144 | tf_op jit(solution)/shard_map/all_to_all | solution.py:252
  64.0 0.2 shard_map.125
  64.2 17.5 %all_to_all.33 = bf16[128,2,2,128]{3,2,1,0:T(2,128)(2,1)S(1)} all-to-all(bf16[128,2,2,128]{3,2,1,0:T(2,128)(2,1)S(1)} %bitcast.22), channel_id=1, replica_groups=mesh['x'=4,'z_lo'=4,'y'=8,'z_hi'=2,'core'=2] {'z_lo','y','z_hi','core'}, dimensions={0} | all-to-all | bytes 262144 | tf_op jit(solution)/shard_map/all_to_all | solution.py:252
  81.8 0.5 shard_map.126
  82.3 9.0 %all_to_all.34.d_right = bf16[4,96,384]{2,1,0:T(8,128)(2,1)S(1)} all-to-all(bf16[4,96,384]{2,1,0:T(8,128)(2,1)S(1)} %get-tuple-element.32), channel_id=1, replica_groups=mesh['x'=4,'z_lo'=4,'y'=8,'z_hi'=2,'core'=2] {'x'}, dimensions={0} | all-to-all | bytes 589824 | tf_op jit(solution)/shard_map/all_to_all | solution.py:295
  91.3 0.4 shard_map.127
  91.7 0.0 copy-start
  91.7 0.0 copy-start.1
  91.8 19.9 %all_to_all.35 = bf16[128,3,2,128]{3,2,1,0:T(2,128)(2,1)S(1)} all-to-all(bf16[128,3,2,128]{3,2,1,0:T(2,128)(2,1)S(1)} %bitcast.18), channel_id=1, replica_groups=mesh['x'=4,'z_lo'=4,'y'=8,'z_hi'=2,'core'=2] {'z_lo','y','z_hi','core'}, dimensions={0} | all-to-all | bytes 393216 | tf_op jit(solution)/shard_map/all_to_all | solution.py:252
  111.6 0.0 copy-done
  111.6 0.0 copy-done.1
  111.6 1.2 %shard_map.128 = (bf16[12,24,128]{2,1,0:T(8,128)(2,1)}, bf16[12,24,128]{2,1,0:T(8,128)(2,1)}) custom-call(bf16[768,128]{1,0:T(8,128)(2,1)S(1)} %bitcast.16, f32[256,384]{1,0:T(8,128)S(1)} %get-tuple-element.33.to_values, f32[256,384]{1,0:T(8,128)S(1)} %get-tuple-element.34.to_gates, f32[128,384]{1,0:T(8,128)S(1)} %get-tuple-element.35.hat, ...), custom_call_target="tpu_custom_call" | custom-call | tf_op jit(solution)/shard_map/pallas_call | solution.py:227
Async XLA Ops:
  2.2 32.0 %copy-start.2 = (bf16[128,128]{1,0:T(8,128)(2,1)S(1)}, bf16[128,128]{1,0:T(8,128)(2,1)}, u32[]{:S(2)}) copy-start(bf16[128,128]{1,0:T(8,128)(2,1)} %w_out_gate.3) | copy-start | bytes 98308
  2.2 32.0 %copy-start.3 = (bf16[128,128]{1,0:T(8,128)(2,1)S(1)}, bf16[128,128]{1,0:T(8,128)(2,1)}, u32[]{:S(2)}) copy-start(bf16[128,128]{1,0:T(8,128)(2,1)} %w_out.3) | copy-start | bytes 98308
  2.2 32.0 %copy-start.4 = (bf16[24,12,128]{2,0,1:T(8,128)(2,1)S(1)}, bf16[24,12,128]{2,0,1:T(8,128)(2,1)}, u32[]{:S(2)}) copy-start(bf16[24,12,128]{2,0,1:T(8,128)(2,1)} %param.12) | copy-start | bytes 221188
  91.7 19.9 %copy-start = (bf16[128,256]{1,0:T(8,128)(2,1)S(1)}, bf16[128,256]{1,0:T(8,128)(2,1)}, u32[]{:S(2)}) copy-start(bf16[128,256]{1,0:T(8,128)(2,1)} %w_values.1) | copy-start | bytes 196612
  91.7 19.9 %copy-start.1 = (bf16[128,256]{1,0:T(8,128)(2,1)S(1)}, bf16[128,256]{1,0:T(8,128)(2,1)}, u32[]{:S(2)}) copy-start(bf16[128,256]{1,0:T(8,128)(2,1)} %w_gates.1) | copy-start | bytes 196612

commit v11 on v10

--- a/solution.py
+++ b/solution.py
@@ -182,7 +182,16 @@
     d_left[...] = dot(packed, right_all[...], (1, 0))
 
 
-def merge_kernel(d_left, d_right, d_both, rows, natural):
+def merge_kernel(
+    d_left, d_right, inner_hat, out_sig, upstream, cols, w_out, w_out_gate, d_both, gated, d_out, rows, natural
+):
+    inner_n = inner_hat[...] * cols[:, 2:3] + cols[:, 3:4]
+    proj = dot(w_out[...], inner_n.astype(BF16), (0, 0))
+    sig = out_sig[...]
+    product = sig * proj
+    gated[...] = product
+    d_gate_out = (upstream[...].astype(F32) * product * (1.0 - sig)).astype(BF16)
+    d_out[...] = dot(w_out_gate[...], d_gate_out, (1, 0))
     to_rows(d_left[...], rows, 0, 6)
     parts = [d_right[part].astype(F32) for part in range(4)]
     total = (parts[0] + parts[1]) + (parts[2] + parts[3])
@@ -194,16 +203,9 @@
 
 
 def back_kernel(
-    d_both, to_values, to_gates, hat, inv, cols, inner_hat, out_sig, upstream,
-    w_values, w_gates, w_out_gate, w_out, update, grad, rows, tile,
+    d_both, to_values, to_gates, hat, inv, cols, gated, d_out, w_values, w_gates, update, grad, rows, tile
 ):
-    vectors = cols[...]
-    inner_n = inner_hat[...] * vectors[:, 2:3] + vectors[:, 3:4]
-    proj = dot(w_out[...], inner_n.astype(BF16), (0, 0))
-    sig = out_sig[...]
-    gated = sig * proj
-    store_tile(gated.T, tile, update)
-    d_gate_out = (upstream[...].astype(F32) * gated * (1.0 - sig)).astype(BF16)
+    store_tile(gated[...].T, tile, update)
     rows[:768] = d_both[...].astype(F32)
     parts = [
         jnp.concatenate([rows[pl.ds(3 * side + i_hi, 128, stride=6), :] for i_hi in range(3)], axis=1)
@@ -212,9 +214,8 @@
     incoming = jnp.concatenate(parts, axis=0)
     d_values = (incoming * to_values[...]).astype(BF16)
     d_gates = (incoming * to_gates[...]).astype(BF16)
-    d_normed = dot(w_out_gate[...], d_gate_out, (1, 0))
-    d_normed += dot(w_values[...], d_values, (1, 0)) + dot(w_gates[...], d_gates, (1, 0))
-    up = d_normed * vectors[:, 0:1]
+    d_normed = d_out[...] + dot(w_values[...], d_values, (1, 0)) + dot(w_gates[...], d_gates, (1, 0))
+    up = d_normed * cols[:, 0:1]
     pair_hat = hat[...]
     first_mean = jnp.mean(up, axis=0, keepdims=True)
     second_mean = jnp.mean(up * pair_hat, axis=0, keepdims=True)
@@ -293,15 +294,17 @@
         grad_kernel, [((96, 384), F32), ((4, 96, 384), BF16)], [d_inner, left, right], [one_rows]
     )
     d_right = lax.all_to_all(d_right, "x", 0, 0)
-    (d_both,) = call(merge_kernel, [(two, BF16)], [d_left, d_right], [two_rows, natural])
+    d_both, gated, d_out = call(
+        merge_kernel,
+        [(two, BF16), (tall, F32), (tall, F32)],
+        [d_left, d_right, inner_hat, out_sig, upstream, cols, w_out, w_out_gate],
+        [two_rows, natural],
+    )
     d_both = exchange(d_both)
     update, grad = call(
         back_kernel,
         [(tile, BF16)] * 2,
-        [
-            d_both, to_values, to_gates, hat, inv, cols, inner_hat, out_sig, upstream,
-            w_values, w_gates, w_out_gate, w_out,
-        ],
+        [d_both, to_values, to_gates, hat, inv, cols, gated, d_out, w_values, w_gates],
         [two_rows, tile],
         last=True,
     )

time: 113 us -> 113 us (level)
  no operation moved by 1% of the time
where the time goes in v11:
time: 113 us
  blocking collectives  107 us (95%)
  Pallas kernels  4.73 us (4%)
    all_to_all x4, blocking collectives, exchange(): lax.all_to_all(rows.reshape(128, -1, 2, 128), GROUP, 0, 0)  88 us
    all_to_all x1, blocking collectives, shards(): right = lax.all_to_all(right, 'x', 0, 0)  10.2 us
    all_to_all x1, blocking collectives, shards(): d_right = lax.all_to_all(d_right, 'x', 0, 0)  9 us
    pallas_call x6, Pallas kernels, call(): pl.pallas_call(kernel, out_shape=[space(*out) for out in outs], in_specs=...  3.15 us

profile of v11, /device:TPU:1, one launch (start us, length us, event | category | flops | bytes accessed | tf_op | source)
XLA Modules:
  0.0 112.7 jit_solution(16573737589248679630)
XLA Ops:
  0.6 1.6 %shard_map.122 = (bf16[768,128]{1,0:T(8,128)(2,1)S(1)}, bf16[128,384]{1,0:T(8,128)(2,1)S(1)}, f32[256,384]{1,0:T(8,128)S(1)}, f32[256,384]{1,0:T(8,128)S(1)}, f3...) custom-call(bf16[12,24,128]{2,1,0:T(8,128)(2,1)} %bitcast.25, f32[1,128]{1,0:T(1,128)} %bitcast.26, ...), custom_call_target="tpu_custom_call" | custom-call | tf_op jit(solution)/shard_map/pallas_call | solution.py:242
  2.2 0.0 copy-start.2
  2.2 0.0 copy-start.3
  2.2 0.0 copy-start.4
  2.3 32.0 %all_to_all.30 = bf16[128,3,2,128]{3,2,1,0:T(2,128)(2,1)S(1)} all-to-all(bf16[128,3,2,128]{3,2,1,0:T(2,128)(2,1)S(1)} %bitcast.21), channel_id=1, replica_groups=mesh['x'=4,'z_lo'=4,'y'=8,'z_hi'=2,'core'=2] {'z_lo','y','z_hi','core'}, dimensions={0} | all-to-all | bytes 393216 | tf_op jit(solution)/shard_map/all_to_all | solution.py:253
  34.2 0.0 copy-done.2
  34.2 0.0 copy-done.3
  34.2 0.0 copy-done.4
  34.2 0.4 shard_map.123
  34.6 10.2 %all_to_all.31.right = bf16[4,96,384]{2,1,0:T(8,128)(2,1)S(1)} all-to-all(bf16[4,96,384]{2,1,0:T(8,128)(2,1)S(1)} %get-tuple-element.29), channel_id=1, replica_groups=mesh['x'=4,'z_lo'=4,'y'=8,'z_hi'=2,'core'=2] {'x'}, dimensions={0} | all-to-all | bytes 589824 | tf_op jit(solution)/shard_map/all_to_all | solution.py:288
  44.9 0.5 shard_map.124
  45.4 18.7 %all_to_all.32 = bf16[128,2,2,128]{3,2,1,0:T(2,128)(2,1)S(1)} all-to-all(bf16[128,2,2,128]{3,2,1,0:T(2,128)(2,1)S(1)} %bitcast.23), channel_id=1, replica_groups=mesh['x'=4,'z_lo'=4,'y'=8,'z_hi'=2,'core'=2] {'z_lo','y','z_hi','core'}, dimensions={0} | all-to-all | bytes 262144 | tf_op jit(solution)/shard_map/all_to_all | solution.py:253
  64.0 0.2 shard_map.125
  64.2 17.5 %all_to_all.33 = bf16[128,2,2,128]{3,2,1,0:T(2,128)(2,1)S(1)} all-to-all(bf16[128,2,2,128]{3,2,1,0:T(2,128)(2,1)S(1)} %bitcast.22), channel_id=1, replica_groups=mesh['x'=4,'z_lo'=4,'y'=8,'z_hi'=2,'core'=2] {'z_lo','y','z_hi','core'}, dimensions={0} | all-to-all | bytes 262144 | tf_op jit(solution)/shard_map/all_to_all | solution.py:253
  81.7 0.5 shard_map.126
  82.3 9.0 %all_to_all.34.d_right = bf16[4,96,384]{2,1,0:T(8,128)(2,1)S(1)} all-to-all(bf16[4,96,384]{2,1,0:T(8,128)(2,1)S(1)} %get-tuple-element.35), channel_id=1, replica_groups=mesh['x'=4,'z_lo'=4,'y'=8,'z_hi'=2,'core'=2] {'x'}, dimensions={0} | all-to-all | bytes 589824 | tf_op jit(solution)/shard_map/all_to_all | solution.py:296
  91.3 0.6 shard_map.127
  91.8 0.0 copy-start
  91.8 0.0 copy-start.1
  91.9 19.9 %all_to_all.35 = bf16[128,3,2,128]{3,2,1,0:T(2,128)(2,1)S(1)} all-to-all(bf16[128,3,2,128]{3,2,1,0:T(2,128)(2,1)S(1)} %bitcast.20), channel_id=1, replica_groups=mesh['x'=4,'z_lo'=4,'y'=8,'z_hi'=2,'core'=2] {'z_lo','y','z_hi','core'}, dimensions={0} | all-to-all | bytes 393216 | tf_op jit(solution)/shard_map/all_to_all | solution.py:253
  111.7 0.0 copy-done
  111.7 0.0 copy-done.1
  111.7 1.0 shard_map.128
Async XLA Ops:
  2.2 32.0 %copy-start.2 = (bf16[128,128]{1,0:T(8,128)(2,1)S(1)}, bf16[128,128]{1,0:T(8,128)(2,1)}, u32[]{:S(2)}) copy-start(bf16[128,128]{1,0:T(8,128)(2,1)} %w_out_gate.3) | copy-start | bytes 98308
  2.2 32.0 %copy-start.3 = (bf16[128,128]{1,0:T(8,128)(2,1)S(1)}, bf16[128,128]{1,0:T(8,128)(2,1)}, u32[]{:S(2)}) copy-start(bf16[128,128]{1,0:T(8,128)(2,1)} %w_out.3) | copy-start | bytes 98308
  2.2 32.0 %copy-start.4 = (bf16[24,12,128]{2,0,1:T(8,128)(2,1)S(1)}, bf16[24,12,128]{2,0,1:T(8,128)(2,1)}, u32[]{:S(2)}) copy-start(bf16[24,12,128]{2,0,1:T(8,128)(2,1)} %param.12) | copy-start | bytes 221188
  91.8 19.9 %copy-start = (bf16[128,256]{1,0:T(8,128)(2,1)S(1)}, bf16[128,256]{1,0:T(8,128)(2,1)}, u32[]{:S(2)}) copy-start(bf16[128,256]{1,0:T(8,128)(2,1)} %w_values.1) | copy-start | bytes 196612
  91.8 19.9 %copy-start.1 = (bf16[128,256]{1,0:T(8,128)(2,1)S(1)}, bf16[128,256]{1,0:T(8,128)(2,1)}, u32[]{:S(2)}) copy-start(bf16[128,256]{1,0:T(8,128)(2,1)} %w_gates.1) | copy-start | bytes 196612

commit v12 on v11

--- a/solution.py
+++ b/solution.py
@@ -152,8 +152,8 @@
     ordered = [parts[part][LOW * slot : LOW * (slot + 1)] for slot in range(12) for part in range(4)]
     ordered = jnp.concatenate(ordered, axis=0).astype(BF16)
     right_all[...] = ordered
+    rows[:512] = jnp.zeros((512, 128), F32)
     to_rows(dot(left[...], ordered, (1, 1)), rows, 0, 4)
-    rows[pl.ds(3, 128, stride=4), :] = jnp.zeros((128, 128), F32)
     inner[...] = rows[:512].astype(BF16)
 
 

time: 113 us -> 113 us (level)
  no operation moved by 1% of the time
where the time goes in v12:
time: 113 us
  blocking collectives  107 us (95%)
  Pallas kernels  4.73 us (4%)
    all_to_all x4, blocking collectives, exchange(): lax.all_to_all(rows.reshape(128, -1, 2, 128), GROUP, 0, 0)  88 us
    all_to_all x1, blocking collectives, shards(): right = lax.all_to_all(right, 'x', 0, 0)  10.2 us
    all_to_all x1, blocking collectives, shards(): d_right = lax.all_to_all(d_right, 'x', 0, 0)  9 us
    pallas_call x6, Pallas kernels, call(): pl.pallas_call(kernel, out_shape=[space(*out) for out in outs], in_specs=...  3.15 us

profile of v12, /device:TPU:1, one launch (start us, length us, event | category | flops | bytes accessed | tf_op | source)
XLA Modules:
  0.0 112.7 jit_solution(900779480247690644)
XLA Ops:
  0.6 1.6 %shard_map.122 = (bf16[768,128]{1,0:T(8,128)(2,1)S(1)}, bf16[128,384]{1,0:T(8,128)(2,1)S(1)}, f32[256,384]{1,0:T(8,128)S(1)}, f32[256,384]{1,0:T(8,128)S(1)}, f3...) custom-call(bf16[12,24,128]{2,1,0:T(8,128)(2,1)} %bitcast.25, f32[1,128]{1,0:T(1,128)} %bitcast.26, ...), custom_call_target="tpu_custom_call" | custom-call | tf_op jit(solution)/shard_map/pallas_call | solution.py:242
  2.2 0.0 copy-start.2
  2.2 0.0 copy-start.3
  2.2 0.0 copy-start.4
  2.3 32.0 %all_to_all.30 = bf16[128,3,2,128]{3,2,1,0:T(2,128)(2,1)S(1)} all-to-all(bf16[128,3,2,128]{3,2,1,0:T(2,128)(2,1)S(1)} %bitcast.21), channel_id=1, replica_groups=mesh['x'=4,'z_lo'=4,'y'=8,'z_hi'=2,'core'=2] {'z_lo','y','z_hi','core'}, dimensions={0} | all-to-all | bytes 393216 | tf_op jit(solution)/shard_map/all_to_all | solution.py:253
  34.2 0.0 copy-done.2
  34.2 0.0 copy-done.3
  34.2 0.0 copy-done.4
  34.2 0.4 shard_map.123
  34.6 10.2 %all_to_all.31.right = bf16[4,96,384]{2,1,0:T(8,128)(2,1)S(1)} all-to-all(bf16[4,96,384]{2,1,0:T(8,128)(2,1)S(1)} %get-tuple-element.29), channel_id=1, replica_groups=mesh['x'=4,'z_lo'=4,'y'=8,'z_hi'=2,'core'=2] {'x'}, dimensions={0} | all-to-all | bytes 589824 | tf_op jit(solution)/shard_map/all_to_all | solution.py:288
  44.9 0.5 shard_map.124
  45.4 18.7 %all_to_all.32 = bf16[128,2,2,128]{3,2,1,0:T(2,128)(2,1)S(1)} all-to-all(bf16[128,2,2,128]{3,2,1,0:T(2,128)(2,1)S(1)} %bitcast.23), channel_id=1, replica_groups=mesh['x'=4,'z_lo'=4,'y'=8,'z_hi'=2,'core'=2] {'z_lo','y','z_hi','core'}, dimensions={0} | all-to-all | bytes 262144 | tf_op jit(solution)/shard_map/all_to_all | solution.py:253
  64.0 0.2 shard_map.125
  64.2 17.5 %all_to_all.33 = bf16[128,2,2,128]{3,2,1,0:T(2,128)(2,1)S(1)} all-to-all(bf16[128,2,2,128]{3,2,1,0:T(2,128)(2,1)S(1)} %bitcast.22), channel_id=1, replica_groups=mesh['x'=4,'z_lo'=4,'y'=8,'z_hi'=2,'core'=2] {'z_lo','y','z_hi','core'}, dimensions={0} | all-to-all | bytes 262144 | tf_op jit(solution)/shard_map/all_to_all | solution.py:253
  81.7 0.5 shard_map.126
  82.3 9.0 %all_to_all.34.d_right = bf16[4,96,384]{2,1,0:T(8,128)(2,1)S(1)} all-to-all(bf16[4,96,384]{2,1,0:T(8,128)(2,1)S(1)} %get-tuple-element.35), channel_id=1, replica_groups=mesh['x'=4,'z_lo'=4,'y'=8,'z_hi'=2,'core'=2] {'x'}, dimensions={0} | all-to-all | bytes 589824 | tf_op jit(solution)/shard_map/all_to_all | solution.py:296
  91.3 0.6 shard_map.127
  91.8 0.0 copy-start
  91.8 0.0 copy-start.1
  91.9 19.9 %all_to_all.35 = bf16[128,3,2,128]{3,2,1,0:T(2,128)(2,1)S(1)} all-to-all(bf16[128,3,2,128]{3,2,1,0:T(2,128)(2,1)S(1)} %bitcast.20), channel_id=1, replica_groups=mesh['x'=4,'z_lo'=4,'y'=8,'z_hi'=2,'core'=2] {'z_lo','y','z_hi','core'}, dimensions={0} | all-to-all | bytes 393216 | tf_op jit(solution)/shard_map/all_to_all | solution.py:253
  111.7 0.0 copy-done
  111.7 0.0 copy-done.1
  111.7 1.0 shard_map.128
Async XLA Ops:
  2.2 32.0 %copy-start.2 = (bf16[128,128]{1,0:T(8,128)(2,1)S(1)}, bf16[128,128]{1,0:T(8,128)(2,1)}, u32[]{:S(2)}) copy-start(bf16[128,128]{1,0:T(8,128)(2,1)} %w_out_gate.3) | copy-start | bytes 98308
  2.2 32.0 %copy-start.3 = (bf16[128,128]{1,0:T(8,128)(2,1)S(1)}, bf16[128,128]{1,0:T(8,128)(2,1)}, u32[]{:S(2)}) copy-start(bf16[128,128]{1,0:T(8,128)(2,1)} %w_out.3) | copy-start | bytes 98308
  2.2 32.0 %copy-start.4 = (bf16[24,12,128]{2,0,1:T(8,128)(2,1)S(1)}, bf16[24,12,128]{2,0,1:T(8,128)(2,1)}, u32[]{:S(2)}) copy-start(bf16[24,12,128]{2,0,1:T(8,128)(2,1)} %param.12) | copy-start | bytes 221188
  91.8 19.9 %copy-start = (bf16[128,256]{1,0:T(8,128)(2,1)S(1)}, bf16[128,256]{1,0:T(8,128)(2,1)}, u32[]{:S(2)}) copy-start(bf16[128,256]{1,0:T(8,128)(2,1)} %w_values.1) | copy-start | bytes 196612
  91.8 19.9 %copy-start.1 = (bf16[128,256]{1,0:T(8,128)(2,1)S(1)}, bf16[128,256]{1,0:T(8,128)(2,1)}, u32[]{:S(2)}) copy-start(bf16[128,256]{1,0:T(8,128)(2,1)} %w_gates.1) | copy-start | bytes 196612
